TPU v7x, 256 devices: a whole 4x4x8 slice. The times are simulated.
256 devices in a mesh: tile: 64 (over z, y, core), chan: 4 (over x).
Axes of the slice: x: 4, y: 4, z: 8, core: 2. Of those that a mesh axis runs over, the one named last changes fastest.
Arguments:
- features: bfloat16 [128, 262144], P('chan', 'tile'), may hold values from -6 to 6
- conv1_weight: bfloat16 [9, 128, 128], P(None, 'chan'), may hold values from -0.1875 to 0.1875
- down_weight: bfloat16 [4, 128, 128], P(None, 'chan'), may hold values from -0.25 to 0.25
- conv2_weight: bfloat16 [9, 128, 128], P(None, 'chan'), may hold values from -0.1875 to 0.1875
- up_weight: bfloat16 [128, 128], P('chan'), may hold values from -0.5 to 0.5
- out_grad: bfloat16 [128, 262144], P('chan', 'tile'), may hold values from -6 to 6
- adjacency: int32 [64, 8, 2], replicated, may hold values from -1 to 63, as said below
Outputs:
- output: bfloat16 [128, 262144], P('chan', 'tile')
- grad_conv1: float32 [9, 128, 128], P(None, 'chan')
- grad_down: float32 [4, 128, 128], P(None, 'chan')
- grad_conv2: float32 [9, 128, 128], P(None, 'chan')
- grad_up: float32 [128, 128], P('chan')
Inputs may be any that keep to these rules, and one draw needn't show every extreme that they name: adjacency[t, k, 0] is the tile beside side k of tile t (sides north, east, south, west, then corners north-east, south-east, south-west, north-west); it is -1 only at corners, where no single tile meets; adjacency[t, k, 1] is the number of counterclockwise quarter turns, 0 to 3, of that neighbour as seen from tile t.
All inputs are finite; a program needn't handle non-finite values.
Results may differ from a plain program's by a relative error of at most 0.0073.
Values may be sent and summed in bfloat16 or wider, within the bound.
A program may use at most 128 MiB of HBM per device.

v0:
```python
from functools import partial

import jax
import jax.numpy as jnp
from jax import lax
from jax.sharding import PartitionSpec as P

SIDE = 64


side_turns = (0, 1, 2, 3, 0, 2, 2, 0)


def as_sent(array):
    return jax.tree.map(lambda a: a.astype(jnp.bfloat16) if a.dtype == jnp.float32 else a, array)


def turned(values, quarter):
    return jnp.rot90(values, quarter, axes=(1, 2))


def build_rims(center, width):
    side_len = center.shape[1]
    return jnp.stack(
        [
            center[:, side_len - width :, :],
            turned(center[:, :, :width], 1),
            turned(center[:, :width, :], 2),
            turned(center[:, :, side_len - width :], 3),
        ]
    )


def pad_block(center, picked, width):
    side_len = center.shape[1]
    north_rows = picked[0]
    east_cols = turned(picked[1], -1)
    south_rows = turned(picked[2], -2)
    west_cols = turned(picked[3], -3)
    north_east = picked[4][:, :, :width]
    south_east = turned(picked[5], -2)[:, :, :width]
    south_west = turned(picked[6], -2)[:, :, side_len - width :]
    north_west = picked[7][:, :, side_len - width :]
    top_band = jnp.concatenate([north_west, north_rows, north_east], axis=2)
    middle = jnp.concatenate([west_cols, center, east_cols], axis=2)
    low_band = jnp.concatenate([south_west, south_rows, south_east], axis=2)
    return jnp.concatenate([top_band, middle, low_band], axis=1)


def choose_rims(partners, rim_slots, current, incoming, first_row):
    row_count = incoming.shape[0]
    inside = (partners >= 0) & (partners < row_count)
    clipped = jnp.clip(partners, 0, row_count - 1)
    selected = incoming[clipped, rim_slots]
    return jnp.where(inside[:, None, None, None], selected, current)


def neighbour_pad(center, table_row, width):
    partners = table_row[:, 0]
    rim_slots = (table_row[:, 1] + jnp.array(side_turns, jnp.int32)) % 4
    rim_rows = build_rims(center, width)
    empty = jnp.zeros((8,) + rim_rows.shape[1:], center.dtype)
    chooser = partial(choose_rims, partners, rim_slots)
    picked = chooser(
        empty, lax.all_gather(as_sent(rim_rows[None]), "tile", axis=0, tiled=True), jnp.int32(0)
    )
    return (pad_block(center, picked, width), partners, rim_slots)


def fine_gather(values):
    return lax.all_gather(as_sent(values), "chan", axis=0, tiled=True).astype(values.dtype)


def coarse_gather(values):
    return lax.all_gather(as_sent(values), "chan", axis=0, tiled=True).astype(values.dtype)


def spread_back(term_fn, row_total):
    return lax.psum_scatter(
        term_fn(jnp.int32(0), row_total * lax.axis_size("chan")),
        "chan",
        scatter_dimension=0,
        tiled=True,
    )


def tile_sums(grads):
    return lax.psum(grads, "tile")


def conv_taps(weights, padded, dilation, rows, cols):
    summed = jnp.zeros((weights.shape[1], rows * cols), jnp.float32)
    for row_tap in range(3):
        for col_tap in range(3):
            window = padded[
                :,
                row_tap * dilation : row_tap * dilation + rows,
                col_tap * dilation : col_tap * dilation + cols,
            ].reshape(padded.shape[0], rows * cols)
            summed = summed + jnp.dot(
                weights[3 * row_tap + col_tap], window, preferred_element_type=jnp.float32
            )
    return summed


def conv_grads(cotangent, padded, dilation, rows, cols):
    result = []
    for row_tap in range(3):
        for col_tap in range(3):
            window = padded[
                :,
                row_tap * dilation : row_tap * dilation + rows,
                col_tap * dilation : col_tap * dilation + cols,
            ].reshape(padded.shape[0], rows * cols)
            result.append(
                lax.dot_general(
                    cotangent, window, (((1,), (1,)), ((), ())), preferred_element_type=jnp.float32
                )
            )
    return jnp.stack(result)


def conv_back_terms(weight_cols, cotangent, dilation, rows, cols):
    summed = jnp.zeros(
        (weight_cols.shape[2], rows + 2 * dilation, cols + 2 * dilation), jnp.float32
    )
    for row_tap in range(3):
        for col_tap in range(3):
            term = lax.dot_general(
                weight_cols[3 * row_tap + col_tap],
                cotangent,
                (((0,), (0,)), ((), ())),
                preferred_element_type=jnp.float32,
            ).reshape(weight_cols.shape[2], rows, cols)
            summed = summed + jnp.pad(
                term,
                (
                    (0, 0),
                    (row_tap * dilation, 2 * dilation - row_tap * dilation),
                    (col_tap * dilation, 2 * dilation - col_tap * dilation),
                ),
            )
    return summed


def quarter_parts(values, rows, cols):
    blocks = values.reshape(values.shape[0], rows, 2, cols, 2)
    return [
        blocks[:, :, row_tap, :, col_tap].reshape(values.shape[0], rows * cols)
        for row_tap in range(2)
        for col_tap in range(2)
    ]


def down_conv(weights, values, rows, cols):
    parts_list = quarter_parts(values, rows, cols)
    summed = jnp.dot(weights[0], parts_list[0], preferred_element_type=jnp.float32)
    for quarter in range(1, 4):
        summed = summed + jnp.dot(
            weights[quarter], parts_list[quarter], preferred_element_type=jnp.float32
        )
    return summed


def down_grads(cotangent, values, rows, cols):
    parts_list = quarter_parts(values, rows, cols)
    return jnp.stack(
        [
            lax.dot_general(
                cotangent, piece_part, (((1,), (1,)), ((), ())), preferred_element_type=jnp.float32
            )
            for piece_part in parts_list
        ]
    )


def down_back(weight_cols, cotangent, rows, cols):
    stacked = jnp.stack(
        [
            lax.dot_general(
                weight_cols[quarter],
                cotangent,
                (((0,), (0,)), ((), ())),
                preferred_element_type=jnp.float32,
            )
            for quarter in range(4)
        ]
    )
    chans = weight_cols.shape[2]
    return (
        stacked.reshape(2, 2, chans, rows, cols)
        .transpose(2, 3, 0, 4, 1)
        .reshape(chans, 4 * rows * cols)
    )


def up_copy(values, rows, cols):
    chans = values.shape[0]
    grown = jnp.broadcast_to(values.reshape(chans, rows, 1, cols, 1), (chans, rows, 2, cols, 2))
    return grown.reshape(chans, 4 * rows * cols)


def pool_cells(cotangent, rows, cols):
    chans = cotangent.shape[0]
    return (
        cotangent.astype(jnp.float32)
        .reshape(chans, rows, 2, cols, 2)
        .sum(axis=(2, 4))
        .reshape(chans, rows * cols)
    )


def gelu_back(preact, cotangent):
    return jax.vjp(jax.nn.gelu, preact)[1](cotangent)[0]


def pad_transpose(cotangent, chans, half_len):
    zero_center = jnp.zeros((chans, half_len, half_len), jnp.float32)
    zero_picked = jnp.zeros((8, chans, 1, half_len), jnp.float32)

    def padding(center, picked):
        return pad_block(center, picked, 1)

    _, pullback = jax.vjp(padding, zero_center, zero_picked)
    return pullback(cotangent)


def rims_transpose(returned, chans, half_len):
    zero_center = jnp.zeros((chans, half_len, half_len), jnp.float32)

    def rimming(center):
        return build_rims(center, 1)

    _, pullback = jax.vjp(rimming, zero_center)
    return pullback(returned)[0]


def coarse_cotangent(coarse_back, partners, rim_slots, chan_count, half_len, tile_count):
    grad_center, grad_picked = pad_transpose(coarse_back, chan_count, half_len)
    has_partner = (partners >= 0).astype(jnp.float32)
    buffer = (
        jnp.zeros((tile_count, 4, chan_count, 1, half_len), jnp.float32)
        .at[jnp.clip(partners, 0, tile_count - 1), rim_slots]
        .add(grad_picked * has_partner[:, None, None, None])
    )
    returned = lax.psum_scatter(buffer, "tile", scatter_dimension=0, tiled=True)[0]
    return grad_center + rims_transpose(returned, chan_count, half_len)


def channel_pass(
    fine_pad,
    partners,
    rim_slots,
    table_row,
    conv1_weight,
    down_weight,
    conv2_weight,
    up_weight,
    out_grad,
    side_len,
    tile_count,
):
    chan_count = fine_pad.shape[0]
    half_len = side_len // 2
    fine_all = fine_gather(fine_pad)
    pre_one = conv_taps(conv1_weight, fine_all, 2, side_len, side_len)
    act_one = jax.nn.gelu(pre_one).astype(jnp.bfloat16)
    act_one_all = fine_gather(act_one)
    pre_two = down_conv(down_weight, act_one_all, half_len, half_len)
    act_two = jax.nn.gelu(pre_two).astype(jnp.bfloat16)
    coarse_pad, _, _ = neighbour_pad(act_two.reshape(chan_count, half_len, half_len), table_row, 1)
    coarse_all = coarse_gather(coarse_pad)
    pre_three = conv_taps(conv2_weight, coarse_all, 1, half_len, half_len)
    coarse = jax.nn.gelu(pre_three).astype(jnp.bfloat16)
    coarse_full = coarse_gather(coarse)
    lifted = jnp.dot(up_weight, coarse_full, preferred_element_type=jnp.float32)
    output = (act_one.astype(jnp.float32) + up_copy(lifted, half_len, half_len)).astype(
        jnp.bfloat16
    )
    pooled = pool_cells(out_grad, half_len, half_len).astype(jnp.bfloat16)
    grad_up = lax.dot_general(
        pooled, coarse_full, (((1,), (1,)), ((), ())), preferred_element_type=jnp.float32
    )

    def up_terms(row_start, row_count):
        weight_cols = lax.dynamic_slice_in_dim(up_weight, row_start, row_count, 1)
        return lax.dot_general(
            weight_cols, pooled, (((0,), (0,)), ((), ())), preferred_element_type=jnp.float32
        )

    back_up = spread_back(up_terms, chan_count)
    grad_three = gelu_back(pre_three, back_up).astype(jnp.bfloat16)
    grad_conv2 = conv_grads(grad_three, coarse_all, 1, half_len, half_len)

    def coarse_terms(row_start, row_count):
        weight_cols = lax.dynamic_slice_in_dim(conv2_weight, row_start, row_count, 2)
        return conv_back_terms(weight_cols, grad_three, 1, half_len, half_len)

    coarse_back = spread_back(coarse_terms, chan_count)
    grad_act_two = coarse_cotangent(
        coarse_back, partners, rim_slots, chan_count, half_len, tile_count
    )
    grad_act_two = grad_act_two.reshape(chan_count, half_len * half_len)
    grad_two = gelu_back(pre_two, grad_act_two).astype(jnp.bfloat16)
    grad_down = down_grads(grad_two, act_one_all, half_len, half_len)

    def fine_terms(row_start, row_count):
        weight_cols = lax.dynamic_slice_in_dim(down_weight, row_start, row_count, 2)
        return down_back(weight_cols, grad_two, half_len, half_len)

    spread = spread_back(fine_terms, chan_count)
    grad_act_one = out_grad.astype(jnp.float32) + spread
    grad_one = gelu_back(pre_one, grad_act_one).astype(jnp.bfloat16)
    grad_conv1 = conv_grads(grad_one, fine_all, 2, side_len, side_len)
    return (output, (grad_conv1, grad_down, grad_conv2, grad_up))


def per_device(features, conv1_weight, down_weight, conv2_weight, up_weight, out_grad, adjacency):
    chan_count = features.shape[0]
    side_len = SIDE
    tile_count = lax.axis_size("tile")
    grad_scale = (tile_count * side_len * side_len) ** (-0.5)
    table_row = adjacency[lax.axis_index("tile")]
    center = features.reshape(chan_count, side_len, side_len)
    fine_pad, partners, rim_slots = neighbour_pad(center, table_row, 2)
    output, grads = channel_pass(
        fine_pad,
        partners,
        rim_slots,
        table_row,
        conv1_weight,
        down_weight,
        conv2_weight,
        up_weight,
        out_grad,
        side_len,
        tile_count,
    )
    summed_grads = tile_sums(grads)
    return (
        output,
        summed_grads[0] * grad_scale,
        summed_grads[1] * grad_scale,
        summed_grads[2] * grad_scale,
        summed_grads[3] * grad_scale,
    )


def solution(mesh):
    placed = (
        P("chan", "tile"),
        P(None, "chan", None),
        P(None, "chan", None),
        P(None, "chan", None),
        P("chan", None),
        P("chan", "tile"),
        P(),
    )
    return jax.shard_map(
        per_device,
        mesh=mesh,
        in_specs=placed,
        out_specs=(
            P("chan", "tile"),
            P(None, "chan", None),
            P(None, "chan", None),
            P(None, "chan", None),
            P("chan", None),
        ),
        check_vma=False,
    )
```

profile of v0, /device:TPU:1, one launch (start us, length us, event | category | flops | bytes accessed | tf_op | source)
XLA Modules:
  0.0 1133.7 jit_solution(10649288548129305712)
XLA Ops:
  12.0 82.6 %all-gather.10.cloned.1.call-done = bf16[256,32,2,64]{3,1,2,0:T(8,128)(2,1)} async-done(((bf16[4,32,2,64]{3,1,2,0:T(8,128)(2,1)}), bf16[256,32,2,64]{3,1,2,0:T(8,128)(2,1)}) %all-gather.10.cloned.1.call-update) | async-done | bytes 2097168 | tf_op jit(solution)/shard_map/all_gather | solution.py:65
  100.6 31.4 %all-gather.6.cloned.1.call-done = bf16[128,68,68]{2,0,1:T(8,128)(2,1)} async-done(((bf16[32,68,68]{2,0,1:T(8,128)(2,1)}), bf16[128,68,68]{2,0,1:T(8,128)(2,1)}) %all-gather.6.cloned.1.call-update) | async-done | bytes 1183760 | tf_op jit(solution)/shard_map/all_gather | solution.py:71
  132.0 16.8 %fusion.130 = (bf16[128,64,64]{2,0,1:T(8,128)(2,1)}, bf16[128,64,64]{2,0,1:T(8,128)(2,1)}, bf16[128,64,64]{2,0,1:T(8,128)(2,1)S(1)}, bf16[128,64,64]{2,0,1:T(8,1...) fusion(bf16[128,68,68]{2,0,1:T(8,128)(2,1)} %all-gather.6.clone, ...), kind=kLoop, calls=%fused_computation.243 | loop fusion | bytes 18874368 | tf_op jit(solution)/shard_map/slice | solution.py:95
  180.1 3.3 reduce_sum.9
  184.6 19.4 %all-gather.8.cloned.1.call-done = bf16[128,4096]{1,0:T(8,128)(2,1)} async-done(((bf16[32,4096]{1,0:T(8,128)(2,1)}), bf16[128,4096]{1,0:T(8,128)(2,1)}) %all-gather.8.cloned.1.call-update) | async-done | bytes 1048592 | tf_op jit(solution)/shard_map/all_gather | solution.py:71
  206.3 4.1 fusion.132
  223.9 58.0 %all-gather.1 = bf16[256,32,1,32]{3,1,2,0:T(8,128)(2,1)} all-gather(bf16[4,32,1,32]{3,1,2,0:T(8,128)(2,1)S(1)} %pad_maximum_fusion.4), channel_id=3, replica_groups=mesh['tile'=64,'chan'=4] {'tile'}, dimensions={0}, use_global_device_ids=true | all-gather | bytes 532480 | tf_op jit(solution)/shard_map/all_gather | solution.py:65
  295.7 13.6 %all_gather.22 = bf16[128,34,34]{2,0,1:T(8,128)(2,1)S(1)} all-gather(bf16[32,34,34]{2,0,1:T(8,128)(2,1)S(1)} %maximum_maximum_fusion.1), channel_id=1, replica_groups=mesh['tile'=64,'chan'=4] {'chan'}, dimensions={0}, use_global_device_ids=true | all-gather | bytes 369920 | tf_op jit(solution)/shard_map/all_gather | solution.py:75
  309.3 4.5 fusion.131
  355.9 3.0 copy.285
  358.8 3.0 copy.286
  361.9 3.0 copy.287
  367.9 3.1 copy.289
  376.8 3.0 copy.292
  379.8 3.0 copy.293
  382.8 9.3 pad_add_fusion
  392.4 32.1 %reduce-scatter.6.cloned.1.call-done = f32[32,34,34]{2,0,1:T(8,128)} async-done(((f32[128,34,34]{2,0,1:T(8,128)}), f32[32,34,34]{2,0,1:T(8,128)}) %reduce-scatter.6.cloned.1.call-update) | async-done | bytes 147984 | tf_op jit(solution)/shard_map/reduce_scatter | solution.py:79
  439.7 193.0 %all-reduce.30.cloned.1.call-done = f32[64,4,32,1,32]{4,2,3,1,0:T(8,128)} async-done(((f32[64,4,32,1,32]{4,2,3,1,0:T(8,128)}), f32[64,4,32,1,32]{4,2,3,1,0:T(8,128)}) %all-reduce.30.cloned.1.call-update) | async-done | bytes 1048592
  645.0 3.3 copy.299
  652.1 9.7 all_gather.23
  663.6 3.5 broadcast_in_dim.84
  667.1 3.0 copy.282
  671.9 246.8 %psum.31 = f32[32,128]{1,0:T(8,128)} all-reduce(f32[32,128]{1,0:T(8,128)} %fusion.138), channel_id=1, replica_groups=mesh['tile'=64,'chan'=4] {'tile'}, use_global_device_ids=true, to_apply=%region_9.10 | all-reduce | flops 4096 | bytes 32768 | tf_op jit(solution)/shard_map/psum | solution.py:88
  941.3 180.5 %all-reduce.32.cloned.1.call-done = (f32[9,32,128]{2,1,0:T(8,128)}, f32[4,32,128]{2,1,0:T(8,128)}, f32[9,32,128]{2,1,0:T(8,128)}) async-done(((f32[9,32,128]{2,1,0:T(8,128)}, f32[4,32,128]{2,1,0:T(8,128)}, f32[9,32,128]{2,1,0:T(8,128)}), (f32[9,32,128]{2,1,0:T(8,128)}, f32[4,32,128]{2,1,0:T(8,128)}, f32[9,32,128]{2,1,0:T(8,128)})) %all-reduce.32.cloned.1.call-update) | async-done | bytes 360464 | tf_op jit(solution)/shard_map/psum | solution.py:88
  (271 shorter events, 185.5 us)
Async XLA Ops:
  7.2 176.3 %copy-start = (bf16[32,128]{1,0:T(8,128)(2,1)S(1)}, bf16[32,128]{1,0:T(8,128)(2,1)}, u32[]{:S(2)}) copy-start(bf16[32,128]{1,0:T(8,128)(2,1)} %param.13) | copy-start | bytes 24580
  7.2 87.5 %all-gather.10.cloned.1.call-start = ((), (), s32[]{:S(2)}) async-start(), calls=%async_computation.8 | async-start | bytes 4259840 | tf_op jit(solution)/shard_map/all_gather | solution.py:65
  11.2 120.8 %all-gather.6.cloned.1.call-start = ((), (), s32[]{:S(2)}) async-start(), calls=%async_computation.3 | async-start | bytes 2785280 | tf_op jit(solution)/shard_map/all_gather | solution.py:71
  12.0 85.4 %copy-start.37 = (pred[8]{0:T(512)(128)(4,1)}, pred[8]{0:T(512)(128)(4,1)S(1)}, u32[]{:S(2)}) copy-start(pred[8]{0:T(512)(128)(4,1)S(1)} %get-tuple-element.71) | copy-start | bytes 28
  100.6 103.4 %all-gather.8.cloned.1.call-start = ((), (), s32[]{:S(2)}) async-start(), calls=%async_computation.4 | async-start | bytes 1310720 | tf_op jit(solution)/shard_map/all_gather | solution.py:71
  178.1 164.8 %reduce-scatter.4.cloned.1.call-start = ((), (), s32[]{:S(2)}) async-start(), calls=%async_computation.5 | async-start | bytes 655360 | tf_op jit(solution)/shard_map/reduce_scatter | solution.py:79
  183.4 27.0 %copy-start.10 = (bf16[32,32,32]{0,2,1:T(8,128)(2,1)}, bf16[32,32,32]{0,2,1:T(8,128)(2,1)S(1)}, u32[]{:S(2)}) copy-start(bf16[32,32,32]{0,2,1:T(8,128)(2,1)S(1)} %reduce_sum.9) | copy-start | bytes 196612
  184.6 239.9 %reduce-scatter.6.cloned.1.call-start = ((), (), s32[]{:S(2)}) async-start(), calls=%async_computation.6 | async-start | bytes 2785280 | tf_op jit(solution)/shard_map/reduce_scatter | solution.py:79
  215.4 78.9 %copy-start.27 = (bf16[32,32,32]{2,0,1:T(8,128)(2,1)S(1)}, bf16[32,32,32]{2,0,1:T(8,128)(2,1)}, u32[]{:S(2)}) copy-start(bf16[32,32,32]{2,0,1:T(8,128)(2,1)} %copy.265) | copy-start | bytes 196612
  322.1 9.6 copy-start.20
  335.5 7.4 copy-start.21
  392.1 40.8 %copy-start.38 = (f32[8]{0:T(128)S(1)}, f32[8]{0:T(128)}, u32[]{:S(2)}) copy-start(f32[8]{0:T(128)} %get-tuple-element.70) | copy-start | bytes 100
  392.1 240.6 %all-reduce.30.cloned.1.call-start = ((), (), s32[]{:S(2)}) async-start(), calls=%async_computation.9 | async-start | bytes 8388608
  438.5 495.2 %reduce-scatter.8.cloned.1.call-start = ((), (), s32[]{:S(2)}) async-start(), calls=%async_computation.7 | async-start | bytes 2621440 | tf_op jit(solution)/shard_map/reduce_scatter | solution.py:79
  651.3 470.5 %all-reduce.32.cloned.1.call-start = ((), (), s32[]{:S(2)}) async-start(), calls=%async_computation.10 | async-start | bytes 720896 | tf_op jit(solution)/shard_map/psum | solution.py:88
  671.9 260.5 %copy-start.13 = (bf16[128,32,1,32,1]{0,3,4,2,1:T(8,128)(2,1)S(1)}, bf16[128,32,1,32,1]{0,3,4,2,1:T(8,128)(2,1)}, u32[]{:S(2)}) copy-start(bf16[128,32,1,32,1]{0,3,4,2,1:T(8,128)(2,1)} %copy-done.12) | copy-start | bytes 786436
  918.7 10.6 copy-start.23
  918.7 11.4 %copy-start.22 = (bf16[128,32,32]{0,2,1:T(8,128)(2,1)S(1)}, bf16[128,32,32]{0,2,1:T(8,128)(2,1)}, u32[]{:S(2)}) copy-start(bf16[128,32,32]{0,2,1:T(8,128)(2,1)} %copy-done.21) | copy-start | bytes 786436
  918.7 12.2 %copy-start.28 = (bf16[128,32,32]{0,2,1:T(8,128)(2,1)S(1)}, bf16[128,32,32]{0,2,1:T(8,128)(2,1)}, u32[]{:S(2)}) copy-start(bf16[128,32,32]{0,2,1:T(8,128)(2,1)} %copy.326) | copy-start | bytes 786436
  918.7 13.0 %copy-start.25 = (bf16[32,4096]{1,0:T(8,128)(2,1)S(1)}, bf16[32,4096]{1,0:T(8,128)(2,1)}, u32[]{:S(2)}) copy-start(bf16[32,4096]{1,0:T(8,128)(2,1)} %get-tuple-element.72) | copy-start | bytes 786436
  918.7 13.0 %copy-start.26 = (f32[32,4096]{1,0:T(8,128)S(1)}, f32[32,4096]{1,0:T(8,128)}, u32[]{:S(2)}) copy-start(f32[32,4096]{1,0:T(8,128)} %copy.282) | copy-start | bytes 1572868
  920.5 12.0 %copy-start.15 = (bf16[128,32,1,32,1]{0,3,4,2,1:T(8,128)(2,1)S(1)}, bf16[128,32,1,32,1]{0,3,4,2,1:T(8,128)(2,1)}, u32[]{:S(2)}) copy-start(bf16[128,32,1,32,1]{0,3,4,2,1:T(8,128)(2,1)} %copy-done.14) | copy-start | bytes 786436
  922.3 10.4 copy-start.17
  924.1 8.8 copy-start.19
  (25 other events, 55.3 us)
Sparse Core Ops, SparseCore 0:
  11.4 83.2 all-gather.9
  100.7 31.2 all-gather.5
  178.3 25.6 all-gather.7
  206.4 23.5 reduce-scatter.3
  392.2 32.2 reduce-scatter.5
  438.6 194.0 all-reduce.29
  651.4 33.0 reduce-scatter.7
  940.8 180.9 all-reduce.31
where the time goes:
time: 1150 us; the launch traced here: 1130 us
  waiting for transfers between devices  539 us (47%)
  blocking collectives  328 us (29%)
  local copies, waits for them, and re-layouts  162 us (14%)
  matrix products  56.4 us (5%)
  other arithmetic  31.7 us (3%)
  between operations  15.4 us (1%)
    psum x1, blocking collectives, tile_sums(): return lax.psum(grads, 'tile')  247 us
    unnamed x9, waiting for transfers between devices  193 us
    psum x1, waiting for transfers between devices, tile_sums(): return lax.psum(grads, 'tile')  181 us
    all_gather x1, waiting for transfers between devices, neighbour_pad(): lax.all_gather(as_sent(rim_rows[None]), 'tile', axis=0, tiled=True)  82.6 us
    all_gather x1, blocking collectives, neighbour_pad(): lax.all_gather(as_sent(rim_rows[None]), 'tile', axis=0, tiled=True)  58 us
    all_gather x2, waiting for transfers between devices, fine_gather(): lax.all_gather(as_sent(values), 'chan', axis=0, tiled=True)  50.8 us
    unnamed x108, local copies, waits for them, and re-layouts  50.1 us
    reduce_scatter x3, waiting for transfers between devices, spread_back(): lax.psum_scatter(term_fn(jnp.int32(0), row_total * lax.axis_size('chan'))...  32.1 us
  transfers between devices with their start and end apart: 8, of which 6 were waited for; matrix products, arithmetic and copies ran while one was open for 9% of the time, Pallas kernels for 0%

commit v1 on v0

v1 whole, which is shorter than its diff:
```python
import functools

import jax
import jax.numpy as jnp
import numpy as np
from jax import lax
from jax.experimental import pallas as pl
from jax.experimental.pallas import tpu as pltpu
from jax.sharding import PartitionSpec as P

BF = jnp.bfloat16
F32 = jnp.float32
MESH = pl.DeviceIdType.MESH
TURNS = (0, 1, 2, 3, 0, 2, 2, 0)
VM = pl.BlockSpec(memory_space=pltpu.VMEM)
SM = pl.BlockSpec(memory_space=pltpu.SMEM)
ANY = pl.BlockSpec(memory_space=pl.ANY)
LIMIT = 56 * 1024 * 1024


def fine_perm():
    out = np.zeros((3, 128, 128), np.float32)
    for b in range(3):
        for rr in range(2):
            for par in range(2):
                for k in range(32):
                    col = 2 * (k - 1 + b) + par
                    if 0 <= col < 64:
                        out[b, rr * 64 + par * 32 + k, rr * 64 + col] = 1
    return out


def corner_maps():
    out = np.zeros((4, 128, 128), np.float32)
    for i in range(2):
        for j in range(2):
            out[0, i * 64 + j, 2 * i + j] = 1
            out[1, (1 - i) * 64 + 63 - j, 4 + 2 * i + j] = 1
            out[2, (1 - i) * 64 + 1 - j, 8 + 2 * i + j] = 1
            out[3, i * 64 + 62 + j, 12 + 2 * i + j] = 1
    return out


def fine_rim_maps():
    sel = np.zeros((4, 128, 640), np.float32)
    for q in range(4):
        for r in range(20):
            ir = 16 * q - 2 + r
            for par in range(2):
                if 0 <= ir < 64:
                    west = 384 + par * 64 + 63 - ir
                    east = 128 + (1 - par) * 64 + ir
                elif ir < 0:
                    west = 512 + 12 + 2 * (ir + 2) + par
                    east = 512 + 0 + 2 * (ir + 2) + par
                else:
                    west = 512 + 8 + 2 * (ir - 64) + par
                    east = 512 + 4 + 2 * (ir - 64) + par
                sel[q, r * 2 + par, west] = 1
                sel[q, 64 + r * 2 + par, east] = 1
    place = np.zeros((2, 1280, 128), np.float32)
    for r in range(20):
        for par in range(2):
            place[0, r * 64 + par * 32, r * 2 + par] = 1
            place[1, r * 64 + par * 32 + 31, 64 + r * 2 + par] = 1
    return sel, place


def coarse_rim_out():
    out = np.zeros((4, 256, 128), np.float32)
    for i in range(32):
        for s, (r, k) in enumerate(((31, i), (i, 0), (0, 31 - i), (31 - i, 31))):
            out[r // 8, (r % 8) * 32 + k, s * 32 + i] = 1
    return out


def coarse_rim_in():
    out = np.zeros((4, 960, 256), np.float32)
    for k in range(32):
        out[0, k, k] = 1
        out[3, 9 * 32 + k, 64 + 31 - k] = 1
    for q in range(4):
        for r in range(10):
            row = 8 * q - 1 + r
            if row < 0:
                west, east = 131, 128
            elif row >= 32:
                west, east = 130, 129
            else:
                west, east = 96 + 31 - row, 32 + row
            out[q, 320 + r * 32, west] = 1
            out[q, 640 + r * 32 + 31, east] = 1
    return out


def nt(a, b):
    return lax.dot_general(a, b, (((1,), (1,)), ((), ())), preferred_element_type=F32)


def tn(a, b):
    return lax.dot_general(a, b, (((0,), (0,)), ((), ())), preferred_element_type=F32)


def nn(a, b):
    return lax.dot_general(a, b, (((1,), (0,)), ((), ())), preferred_element_type=F32)


ROOT = 0.7978845608028654


def gelu(v):
    return 0.5 * v * (1.0 + jnp.tanh(ROOT * (v + 0.044715 * (v * v * v))))


def gelu_slope(v):
    t = jnp.tanh(ROOT * (v + 0.044715 * (v * v * v)))
    return 0.5 * (1.0 + t) + 0.5 * v * (1.0 - t * t) * (ROOT * (1.0 + 3 * 0.044715 * (v * v)))


def place_of():
    tile = lax.axis_index("tile")
    return tile, tile // 8, lax.rem(tile, 8), lax.axis_index("chan")


def x_peer(d):
    tile, _, _, x = place_of()
    return (tile, lax.rem(x + d, 4))


def z_peer(d):
    _, z, g, x = place_of()
    return (lax.rem(z + d, 8) * 8 + g, x)


def g_peer(d):
    _, z, g, x = place_of()
    return (z * 8 + lax.rem(g + d, 8), x)


def core_peer():
    tile, _, g, x = place_of()
    return (tile + 1 - 2 * lax.rem(g, 2), x)


def y_peer(d):
    _, z, g, x = place_of()
    return (z * 8 + lax.rem(g + 2 * d, 8), x)


def greet(peers):
    barrier = pltpu.get_barrier_semaphore()
    for peer in peers:
        pl.semaphore_signal(barrier, inc=1, device_id=peer, device_id_type=MESH)
    pl.semaphore_wait(barrier, len(peers))


def push(src, dst, ssem, rsem, peer):
    copy = pltpu.make_async_remote_copy(
        src_ref=src, dst_ref=dst, send_sem=ssem, recv_sem=rsem, device_id=peer, device_id_type=MESH
    )
    copy.start()
    return copy


def strips_kernel(table, feat, ograd, rims, w1, wd, w2, up, cmap,
                  f_out, g_out, w1_out, wd_out, w2_out, up_out, d_out,
                  held, slots, landed, lsem, xs, xr, zs, zr, gs, gr, ds, dr):
    tile, z, g, x = place_of()
    greet([x_peer(d) for d in (1, 2, 3)] + [z_peer(d) for d in range(1, 8)] + [g_peer(d) for d in range(1, 8)])
    mine = pl.ds(pl.multiple_of(x * 32, 32), 32)

    def pieces(j):
        start = pl.multiple_of(jnp.clip(j * 1024 - 128, 0, 2816), 128)
        lane = pl.multiple_of(j * 1024, 1024)
        return (
            (feat.at[:, pl.ds(start, 1280)], f_out.at[mine, :]),
            (w1, w1_out.at[:, mine, :]),
            (wd, wd_out.at[:, mine, :]),
            (ograd.at[:, pl.ds(lane, 1024)], g_out.at[mine, :]),
            (w2, w2_out.at[:, mine, :]),
            (up, up_out.at[mine, :]),
        )

    zc = [push(rims, held.at[pl.ds(z * 4, 4)], zs.at[d], zr.at[d], z_peer(d)) for d in range(1, 8)]
    own = pltpu.make_async_copy(rims, held.at[pl.ds(z * 4, 4)], lsem.at[6])
    own.start()
    xc, lc = [], []
    for n in range(6):
        for d in (1, 3, 2):
            src, dst = pieces(lax.rem(x + d, 4))[n]
            xc.append(push(src, dst, xs.at[n, d], xr.at[n, d], x_peer(d)))
        src, dst = pieces(x)[n]
        copy = pltpu.make_async_copy(src, dst, lsem.at[n])
        copy.start()
        lc.append(copy)
    own.wait()
    for c in zc:
        c.wait()
    gc = []
    for d in (1, 2, 3, 4, 5, 6, 7, 0):
        j = lax.rem(g + d, 8)
        corner = jnp.zeros((32, 128), F32)
        for k in range(8):
            v = table[j * 8 + k]
            block = held[jnp.maximum(v, 0)]
            block = jnp.where(v >= 0, block, jnp.zeros_like(block))
            if k < 4:
                slots[d, :, k * 128:(k + 1) * 128] = block
            else:
                corner = corner + nn(block, cmap[k - 4])
        slots[d, :, 512:640] = corner.astype(BF)
        if d:
            gc.append(push(slots.at[d], landed.at[d], gs.at[d], gr.at[d], g_peer(d)))
    for c in gc:
        c.wait()
    total = slots[0].astype(F32)
    for d in range(1, 8):
        total = total + landed[d].astype(F32)
    d_out[mine, :] = total.astype(BF)
    dc = [push(d_out.at[mine, :], d_out.at[mine, :], ds.at[d], dr.at[d], x_peer(d)) for d in (1, 3, 2)]
    for c in lc:
        c.wait()
    for c in xc:
        c.wait()
    for c in dc:
        c.wait()


def strips_call(table, feat, ograd, rims, w1, wd, w2, up, cmap):
    dma = pltpu.SemaphoreType.DMA
    return pl.pallas_call(
        strips_kernel,
        out_shape=(
            jax.ShapeDtypeStruct((128, 1280), BF),
            jax.ShapeDtypeStruct((128, 1024), BF),
            jax.ShapeDtypeStruct((9, 128, 128), BF),
            jax.ShapeDtypeStruct((4, 128, 128), BF),
            jax.ShapeDtypeStruct((9, 128, 128), BF),
            jax.ShapeDtypeStruct((128, 128), BF),
            jax.ShapeDtypeStruct((128, 640), BF),
        ),
        in_specs=[SM, ANY, ANY, VM, VM, VM, VM, VM, VM],
        out_specs=[VM] * 7,
        scratch_shapes=[
            pltpu.VMEM((32, 32, 128), BF),
            pltpu.VMEM((8, 32, 640), BF),
            pltpu.VMEM((8, 32, 640), BF),
            dma((7,)), dma((6, 4)), dma((6, 4)), dma((8,)), dma((8,)), dma((8,)), dma((8,)), dma((4,)), dma((4,)),
        ],
        compiler_params=pltpu.CompilerParams(collective_id=0, has_side_effects=True, vmem_limit_bytes=LIMIT),
    )(table, feat, ograd, rims, w1, wd, w2, up, cmap)


def taps_of(blocks, step, start, count):
    return jnp.concatenate(
        [blocks[b, pl.ds(a * step + start, count), :] for a in range(3) for b in range(3)], axis=1
    )


def side_by_side(weights, count):
    return jnp.concatenate([weights[t] for t in range(count)], axis=1)


def quarters(act):
    parts = act.reshape(8, 2, 2, 32, 128)
    return jnp.concatenate(
        [parts[:, a, b].reshape(256, 128) for a in range(2) for b in range(2)], axis=1
    )


def fine_kernel(f_ref, d_ref, w1, wd, perm, sel, place, rimout,
                cb, z1_ref, act1_ref, z2_ref, act2_ref, rq_ref):
    q = lax.axis_index("chan")
    shift = jnp.where(q == 0, -1, jnp.where(q == 3, 1, 0))
    perms = perm[...].reshape(384, 128)
    rim_rows = nt(sel[q], d_ref[...]).astype(BF)
    flip = (
        lax.broadcasted_iota(jnp.int32, (128, 128), 0) + lax.broadcasted_iota(jnp.int32, (128, 128), 1) == 127
    ).astype(F32).astype(BF)
    for n in range(10):
        at = jnp.clip(n + shift, 0, 9)
        block = f_ref[:, pl.ds(pl.multiple_of(at * 128, 128), 128)]
        if n == 0:
            block = jnp.where(q == 0, d_ref[:, 0:128], block)
        if n == 9:
            block = jnp.where(q == 3, nn(d_ref[:, 256:384], flip).astype(BF), block)
        turned = nt(perms, block)
        rows = pl.ds(n * 128, 128)
        cb[0, rows, :] = (turned[0:128] + nn(place[0, rows, :], rim_rows)).astype(BF)
        cb[1, rows, :] = turned[128:256].astype(BF)
        cb[2, rows, :] = (turned[256:384] + nn(place[1, rows, :], rim_rows)).astype(BF)
    w1c = side_by_side(w1, 9)
    for n in range(4):
        rows = pl.ds(n * 256, 256)
        pre = nt(taps_of(cb, 128, n * 256, 256), w1c)
        z1_ref[rows, :] = pre
        act1_ref[rows, :] = gelu(pre).astype(BF)
    pre = nt(quarters(act1_ref[...]), side_by_side(wd, 4))
    z2_ref[...] = pre
    act = gelu(pre).astype(BF)
    act2_ref[...] = act
    rq_ref[...] = tn(act, rimout[q]).astype(BF)


def fine_call(*args):
    return pl.pallas_call(
        fine_kernel,
        out_shape=(
            jax.ShapeDtypeStruct((3, 1280, 128), BF),
            jax.ShapeDtypeStruct((1024, 128), F32),
            jax.ShapeDtypeStruct((1024, 128), BF),
            jax.ShapeDtypeStruct((256, 128), F32),
            jax.ShapeDtypeStruct((256, 128), BF),
            jax.ShapeDtypeStruct((128, 128), BF),
        ),
        in_specs=[VM] * 8,
        out_specs=[VM] * 6,
        compiler_params=pltpu.CompilerParams(vmem_limit_bytes=LIMIT),
    )(*args)


def wanted(target, j):
    rows = lax.broadcasted_iota(jnp.int32, (1024, 256), 0)
    return jnp.where(rows == target[pl.ds(j, 1), :], 1.0, 0.0).astype(BF)


def coarse_rims_kernel(target, rq, act2, d_out, top, bottom,
                       xbuf, held, slots, landed, xs, xr, hs, hr, zs, zr, gs, gr, ds, dr):
    tile, z, g, x = place_of()
    greet([x_peer(d) for d in (1, 2, 3)] + [z_peer(d) for d in range(1, 8)] + [g_peer(d) for d in range(1, 8)])
    mine = pl.ds(pl.multiple_of(x * 32, 32), 32)
    xc = []
    for d in (1, 3, 2):
        theirs = pl.ds(pl.multiple_of(lax.rem(x + d, 4) * 32, 32), 32)
        xc.append(push(rq.at[theirs, :], xbuf.at[d], xs.at[d], xr.at[d], x_peer(d)))
    hc = [
        push(act2.at[pl.ds(224, 32), :], top, hs.at[0], hr.at[0], x_peer(1)),
        push(act2.at[pl.ds(0, 32), :], bottom, hs.at[1], hr.at[1], x_peer(3)),
    ]
    total = rq[mine, :].astype(F32)
    for c in xc:
        c.wait()
    for d in (1, 2, 3):
        total = total + xbuf[d].astype(F32)
    held[z] = total.astype(BF)
    zc = [push(held.at[z], held.at[z], zs.at[d], zr.at[d], z_peer(d)) for d in range(1, 8)]
    for c in zc:
        c.wait()
    every = jnp.concatenate([held[n] for n in range(8)], axis=1)
    gc = []
    for d in (1, 2, 3, 4, 5, 6, 7, 0):
        j = lax.rem(g + d, 8)
        slots[d] = nn(every, wanted(target, j)).astype(BF)
        if d:
            gc.append(push(slots.at[d], landed.at[d], gs.at[d], gr.at[d], g_peer(d)))
    for c in gc:
        c.wait()
    total = slots[0].astype(F32)
    for d in range(1, 8):
        total = total + landed[d].astype(F32)
    d_out[mine, :] = total.astype(BF)
    dc = [push(d_out.at[mine, :], d_out.at[mine, :], ds.at[d], dr.at[d], x_peer(d)) for d in (1, 3, 2)]
    for c in hc:
        c.wait()
    for c in dc:
        c.wait()


def coarse_rims_call(target, rq, act2):
    dma = pltpu.SemaphoreType.DMA
    return pl.pallas_call(
        coarse_rims_kernel,
        out_shape=(
            jax.ShapeDtypeStruct((128, 256), BF),
            jax.ShapeDtypeStruct((32, 128), BF),
            jax.ShapeDtypeStruct((32, 128), BF),
        ),
        in_specs=[VM] * 3,
        out_specs=[VM] * 3,
        scratch_shapes=[
            pltpu.VMEM((4, 32, 128), BF),
            pltpu.VMEM((8, 32, 128), BF),
            pltpu.VMEM((8, 32, 256), BF),
            pltpu.VMEM((8, 32, 256), BF),
            dma((4,)), dma((4,)), dma((2,)), dma((2,)), dma((8,)), dma((8,)), dma((8,)), dma((8,)), dma((4,)), dma((4,)),
        ],
        compiler_params=pltpu.CompilerParams(collective_id=1, has_side_effects=True, vmem_limit_bytes=LIMIT),
    )(target, rq, act2)


def coarse_kernel(act2, d_ref, top, bottom, w2, up, og, act1, perm, rimin,
                  out_ref, ogt, center, first, last, dq, grads):
    q = lax.axis_index("chan")
    sel = rimin[q]
    rim = nt(sel, d_ref[...])
    upper = jnp.where(q == 0, 0.0, top[...].astype(F32))
    lower = jnp.where(q == 3, 0.0, bottom[...].astype(F32))
    rows = jnp.concatenate([upper, act2[...].astype(F32), lower], axis=0) + rim[0:320]
    col = lax.rem(lax.broadcasted_iota(jnp.int32, (320, 128), 0), 32)
    west = jnp.where(col == 0, 0.0, pltpu.roll(rows, 1, 0)) + rim[320:640]
    east = jnp.where(col == 31, 0.0, pltpu.roll(rows, 319, 0)) + rim[640:960]
    blocks = [v.astype(BF) for v in (west, rows, east)]
    taps = jnp.concatenate([blocks[b][a * 32:a * 32 + 256] for a in range(3) for b in range(3)], axis=1)
    pre = nt(taps, side_by_side(w2, 9))
    coarse = gelu(pre).astype(BF)
    lifted = nt(coarse, up[...])
    flat = perm[1]
    for n in range(8):
        turned = nt(flat, og[:, n * 128:(n + 1) * 128])
        ogt[n * 128:(n + 1) * 128, :] = turned.astype(BF)
        row = lifted[n * 32:(n + 1) * 32]
        summed = act1[n * 128:(n + 1) * 128, :].astype(F32) + jnp.concatenate([row] * 4, axis=0)
        out_ref[:, n * 128:(n + 1) * 128] = tn(summed.astype(BF), flat).astype(BF)
    cells = ogt[...].astype(F32).reshape(8, 4, 32, 128)
    pooled = (cells[:, 0] + cells[:, 1] + cells[:, 2] + cells[:, 3]).reshape(256, 128).astype(BF)
    grads[:, 1152:1280] = tn(pooled, coarse)
    gz3 = (gelu_slope(pre) * nn(pooled, up[...])).astype(BF)
    grads[:, 0:1152] = tn(gz3, taps)
    none32, none64 = jnp.zeros((32, 128), F32), jnp.zeros((64, 128), F32)
    back = []
    for b in range(3):
        v0, v1, v2 = (nn(gz3, w2[3 * a + b]) for a in range(3))
        back.append(
            jnp.concatenate([v0, none64], axis=0)
            + jnp.concatenate([none32, v1, none32], axis=0)
            + jnp.concatenate([none64, v2], axis=0)
        )
    mid = (
        back[1]
        + jnp.where(col == 31, 0.0, pltpu.roll(back[0], 319, 0))
        + jnp.where(col == 0, 0.0, pltpu.roll(back[2], 1, 0))
    )
    center[...] = mid[32:288]
    first[...] = mid[0:32]
    last[...] = mid[288:320]
    cat = jnp.concatenate([mid.astype(BF), back[0].astype(BF), back[2].astype(BF)], axis=0)
    dq[...] = tn(cat, sel).astype(BF)


def coarse_call(*args):
    return pl.pallas_call(
        coarse_kernel,
        out_shape=(
            jax.ShapeDtypeStruct((128, 1024), BF),
            jax.ShapeDtypeStruct((1024, 128), BF),
            jax.ShapeDtypeStruct((256, 128), F32),
            jax.ShapeDtypeStruct((32, 128), F32),
            jax.ShapeDtypeStruct((32, 128), F32),
            jax.ShapeDtypeStruct((128, 256), BF),
            jax.ShapeDtypeStruct((128, 1280), F32),
        ),
        in_specs=[VM] * 10,
        out_specs=[VM] * 7,
        compiler_params=pltpu.CompilerParams(vmem_limit_bytes=LIMIT),
    )(*args)


def back_rims_kernel(target, dq, first, last, strip, t_out, top, bottom, out,
                     xbuf, held, slots, landed, osem, xs, xr, hs, hr, zs, zr, gs, gr, ds, dr, os, orr):
    tile, z, g, x = place_of()
    greet([x_peer(d) for d in (1, 2, 3)] + [z_peer(d) for d in range(1, 8)] + [g_peer(d) for d in range(1, 8)])
    mine = pl.ds(pl.multiple_of(x * 32, 32), 32)
    xc = []
    for d in (1, 3, 2):
        theirs = pl.ds(pl.multiple_of(lax.rem(x + d, 4) * 32, 32), 32)
        xc.append(push(dq.at[theirs, :], xbuf.at[d], xs.at[d], xr.at[d], x_peer(d)))
    hc = [
        push(last, top, hs.at[0], hr.at[0], x_peer(1)),
        push(first, bottom, hs.at[1], hr.at[1], x_peer(3)),
    ]
    lanes = pl.ds(pl.multiple_of(x * 1024, 1024), 1024)
    oc = []
    for d in (1, 3, 2):
        theirs = pl.ds(pl.multiple_of(lax.rem(x + d, 4) * 32, 32), 32)
        oc.append(push(strip.at[theirs, :], out.at[:, lanes], os.at[d], orr.at[d], x_peer(d)))
    own = pltpu.make_async_copy(strip.at[mine, :], out.at[:, lanes], osem)
    own.start()
    total = dq[mine, :].astype(F32)
    for c in xc:
        c.wait()
    for d in (1, 2, 3):
        total = total + xbuf[d].astype(F32)
    held[g] = total.astype(BF)
    gc = [push(held.at[g], held.at[g], gs.at[d], gr.at[d], g_peer(d)) for d in range(1, 8)]
    for c in gc:
        c.wait()
    total = nt(held[0], wanted(target, 0))
    for j in range(1, 8):
        total = total + nt(held[j], wanted(target, j))
    for n in range(8):
        slots[n] = total[:, n * 128:(n + 1) * 128]
    zc = [push(slots.at[lax.rem(z + d, 8)], landed.at[d], zs.at[d], zr.at[d], z_peer(d)) for d in range(1, 8)]
    for c in zc:
        c.wait()
    total = slots[z]
    for d in range(1, 8):
        total = total + landed[d]
    t_out[mine, :] = total
    dc = [push(t_out.at[mine, :], t_out.at[mine, :], ds.at[d], dr.at[d], x_peer(d)) for d in (1, 3, 2)]
    for c in hc:
        c.wait()
    for c in oc:
        c.wait()
    own.wait()
    for c in dc:
        c.wait()


def back_rims_call(target, dq, first, last, strip):
    dma = pltpu.SemaphoreType.DMA
    return pl.pallas_call(
        back_rims_kernel,
        out_shape=(
            jax.ShapeDtypeStruct((128, 128), F32),
            jax.ShapeDtypeStruct((32, 128), F32),
            jax.ShapeDtypeStruct((32, 128), F32),
            jax.ShapeDtypeStruct((32, 4096), BF),
        ),
        in_specs=[VM] * 5,
        out_specs=[VM] * 4,
        scratch_shapes=[
            pltpu.VMEM((4, 32, 256), BF),
            pltpu.VMEM((8, 32, 256), BF),
            pltpu.VMEM((8, 32, 128), F32),
            pltpu.VMEM((8, 32, 128), F32),
            dma, dma((4,)), dma((4,)), dma((2,)), dma((2,)), dma((8,)), dma((8,)), dma((8,)), dma((8,)),
            dma((4,)), dma((4,)), dma((4,)), dma((4,)),
        ],
        compiler_params=pltpu.CompilerParams(collective_id=2, has_side_effects=True, vmem_limit_bytes=LIMIT),
    )(target, dq, first, last, strip)


def fine_back_kernel(center, t_ref, top, bottom, z2, z1, act1, ogt, cb, wd, rimout, grads):
    q = lax.axis_index("chan")
    rim = t_ref[...]
    high = rim.astype(BF)
    low = (rim - high.astype(F32)).astype(BF)
    sel = rimout[q]
    upper = jnp.where(q == 0, 0.0, top[...])
    lower = jnp.where(q == 3, 0.0, bottom[...])
    middle = jnp.zeros((192, 128), F32)
    ga2 = center[...] + jnp.concatenate([upper, middle, lower], axis=0) + nt(sel, high) + nt(sel, low)
    gz2 = (gelu_slope(z2[...]) * ga2).astype(BF)
    grads[:, 1152:1664] = tn(gz2, quarters(act1[...]))
    fine = [nn(gz2, wd[t]).reshape(8, 1, 32, 128) for t in range(4)]
    spread = jnp.concatenate(fine, axis=1).reshape(1024, 128)
    gz1 = (gelu_slope(z1[...]) * (ogt[...].astype(F32) + spread)).astype(BF)
    for a in range(3):
        for b in range(3):
            t = 3 * a + b
            grads[:, t * 128:(t + 1) * 128] = tn(gz1, cb[b, a * 128:a * 128 + 1024, :])


def fine_back_call(*args):
    return pl.pallas_call(
        fine_back_kernel,
        out_shape=jax.ShapeDtypeStruct((128, 1664), F32),
        in_specs=[VM] * 11,
        out_specs=VM,
        compiler_params=pltpu.CompilerParams(vmem_limit_bytes=LIMIT),
    )(*args)


WIDE = 3072


def sums_kernel(fine, coarse, g1_out, gd_out, g2_out, gu_out,
                cout, cin, xout, xin, zout, zin, yin, full, final,
                cs, cr, xs, xr, zs, zr, ys, yr, as_, ar, fs, fr, scale):
    tile, z, g, x = place_of()
    y, core = g // 2, lax.rem(g, 2)
    greet(
        [core_peer()] + [x_peer(d) for d in (1, 2, 3)]
        + [z_peer(d) for d in range(1, 8)] + [y_peer(d) for d in (1, 2, 3)]
    )
    other = 1 - core
    cout[:, :, 0:1664] = fine[:, pl.ds(other, 1)].reshape(4, 16, 1664).astype(BF)
    cout[:, :, 1664:2944] = coarse[:, pl.ds(other, 1)].reshape(4, 16, 1280).astype(BF)
    cout[:, :, 2944:3072] = jnp.zeros((4, 16, 128), BF)
    cc = push(cout, cin, cs, cr, core_peer())
    cc.wait()
    xout[:, :, 0:1664] = (fine[:, pl.ds(core, 1)].reshape(4, 16, 1664) + cin[:, :, 0:1664].astype(F32)).astype(BF)
    xout[:, :, 1664:2944] = (coarse[:, pl.ds(core, 1)].reshape(4, 16, 1280) + cin[:, :, 1664:2944].astype(F32)).astype(BF)
    xout[:, :, 2944:3072] = jnp.zeros((4, 16, 128), BF)
    xc = [push(xout.at[lax.rem(x + d, 4)], xin.at[d], xs.at[d], xr.at[d], x_peer(d)) for d in (1, 3, 2)]
    for c in xc:
        c.wait()
    total = xout[x].astype(F32)
    for d in (1, 2, 3):
        total = total + xin[d].astype(F32)
    for n in range(8):
        zout[n] = total[:, n * 384:(n + 1) * 384].astype(BF)
    zc = [push(zout.at[lax.rem(z + d, 8)], zin.at[d], zs.at[d], zr.at[d], z_peer(d)) for d in range(1, 8)]
    for c in zc:
        c.wait()
    total = zout[z].astype(F32)
    for d in range(1, 8):
        total = total + zin[d].astype(F32)
    yin[y] = total
    yc = [push(yin.at[y], yin.at[y], ys.at[d], yr.at[d], y_peer(d)) for d in (1, 3, 2)]
    for c in yc:
        c.wait()
    full[z] = (((yin[0] + yin[1]) + (yin[2] + yin[3])) * scale).astype(BF)
    ac = [push(full.at[z], full.at[z], as_.at[d], ar.at[d], z_peer(d)) for d in range(1, 8)]
    for c in ac:
        c.wait()
    for n in range(8):
        final[pl.ds(core, 1), :, n * 384:(n + 1) * 384] = full[n].reshape(1, 16, 384)
    fc = push(final.at[core], final.at[core], fs, fr, core_peer())
    fc.wait()
    for c in range(2):
        rows = pl.ds(c * 16, 16)
        for t in range(23):
            block = final[c, :, t * 128:(t + 1) * 128].astype(F32)
            if t < 9:
                g1_out[t, rows, :] = block
            elif t < 13:
                gd_out[t - 9, rows, :] = block
            elif t < 22:
                g2_out[t - 13, rows, :] = block
            else:
                gu_out[rows, :] = block


def sums_call(fine, coarse, scale):
    dma = pltpu.SemaphoreType.DMA
    return pl.pallas_call(
        functools.partial(sums_kernel, scale=scale),
        out_shape=(
            jax.ShapeDtypeStruct((9, 32, 128), F32),
            jax.ShapeDtypeStruct((4, 32, 128), F32),
            jax.ShapeDtypeStruct((9, 32, 128), F32),
            jax.ShapeDtypeStruct((32, 128), F32),
        ),
        in_specs=[VM] * 2,
        out_specs=[VM] * 4,
        scratch_shapes=[
            pltpu.VMEM((4, 16, WIDE), BF),
            pltpu.VMEM((4, 16, WIDE), BF),
            pltpu.VMEM((4, 16, WIDE), BF),
            pltpu.VMEM((4, 16, WIDE), BF),
            pltpu.VMEM((8, 16, 384), BF),
            pltpu.VMEM((8, 16, 384), BF),
            pltpu.VMEM((4, 16, 384), F32),
            pltpu.VMEM((8, 16, 384), BF),
            pltpu.VMEM((2, 16, WIDE), BF),
            dma, dma, dma((4,)), dma((4,)), dma((8,)), dma((8,)), dma((4,)), dma((4,)), dma((8,)), dma((8,)), dma, dma,
        ],
        compiler_params=pltpu.CompilerParams(collective_id=3, has_side_effects=True, vmem_limit_bytes=LIMIT),
    )(fine, coarse)


def build_rims(center, width):
    side_len = center.shape[1]
    turned = functools.partial(jnp.rot90, axes=(1, 2))
    return jnp.stack(
        [
            center[:, side_len - width:, :],
            turned(center[:, :, :width], 1),
            turned(center[:, :width, :], 2),
            turned(center[:, :, side_len - width:], 3),
        ]
    )


def per_device(features, conv1_weight, down_weight, conv2_weight, up_weight, out_grad, adjacency):
    tile = lax.axis_index("tile")
    z, g = tile // 8, tile % 8
    rows = lax.dynamic_slice_in_dim(adjacency, z * 8, 8, 0)
    partner = rows[:, :, 0]
    slot = (rows[:, :, 1] + jnp.array(TURNS, jnp.int32)) % 4
    owned = (partner >= 0) & (partner % 8 == g)
    from_z = partner // 8
    table = jnp.where(owned, from_z * 4 + slot, -1).reshape(64)
    base = from_z * 128 + slot * 32
    sides = jnp.where(owned[:, :4, None], base[:, :4, None] + jnp.arange(32, dtype=jnp.int32), -1).reshape(8, 128)
    corners = jnp.where(owned[:, 4:], base[:, 4:] + jnp.array((0, 31, 0, 31), jnp.int32), -1)
    target = jnp.concatenate([sides, corners, jnp.full((8, 124), -1, jnp.int32)], axis=1)

    as_map = lambda m: jnp.asarray(m, BF)
    perm = as_map(fine_perm())
    fine_sel, fine_place = (as_map(m) for m in fine_rim_maps())
    rim_out, rim_in = as_map(coarse_rim_out()), as_map(coarse_rim_in())

    rims = build_rims(features.reshape(32, 64, 64), 2).reshape(4, 32, 128)
    strip, og, w1, wd, w2, up, picked = strips_call(
        table, features, out_grad, rims, conv1_weight, down_weight, conv2_weight, up_weight, as_map(corner_maps())
    )
    cb, z1, act1, z2, act2, rq = fine_call(strip, picked, w1, wd, perm, fine_sel, fine_place, rim_out)
    picked2, top, bottom = coarse_rims_call(target, rq, act2)
    out_strip, ogt, center, first, last, dq, grads_b = coarse_call(
        act2, picked2, top, bottom, w2, up, og, act1, perm, rim_in
    )
    back, top_back, bottom_back, output = back_rims_call(target, dq, first, last, out_strip)
    grads_a = fine_back_call(center, back, top_back, bottom_back, z2, z1, act1, ogt, cb, wd, rim_out)
    g1, gd, g2, gu = sums_call(
        grads_a.reshape(4, 2, 16, 1664), grads_b.reshape(4, 2, 16, 1280), 262144 ** -0.5
    )
    return output, g1, gd, g2, gu


def solution(mesh):
    weights = P(None, "chan", None)
    return jax.shard_map(
        per_device,
        mesh=mesh,
        in_specs=(P("chan", "tile"), weights, weights, weights, P("chan", None), P("chan", "tile"), P()),
        out_specs=(P("chan", "tile"), weights, weights, weights, P("chan", None)),
        check_vma=False,
    )
```

time: 1150 us -> 138 us (0.12); the launches traced: 1130 us -> 138 us
  waiting for transfers between devices: 539 us -> 0 us
  blocking collectives: 328 us -> 0 us
  local copies, waits for them, and re-layouts: 162 us -> 12.4 us
  Pallas kernels: 0 us -> 121 us
  matrix products: 56.4 us -> 0 us
  other arithmetic: 31.7 us -> 3.2 us
  between operations: 15.4 us -> 0.76 us
    psum x1 -> x0, blocking collectives: 247 us -> none  [tile_sums(): return lax.psum(grads, 'tile')]
    unnamed x9 -> x0, waiting for transfers between devices: 193 us -> none
    psum x1 -> x0, waiting for transfers between devices: 181 us -> none  [tile_sums(): return lax.psum(grads, 'tile')]
    all_gather x3 -> x0, waiting for transfers between devices: 133 us -> none  [the longest x1 82.6 us: neighbour_pad(): lax.all_gather(as_sent(rim_rows[None]), 'tile', axis=0, tiled=True)]
    pallas_call x0 -> x7, Pallas kernels: none -> 121 us  [the longest x1 31.5 us: sums_call(): pl.pallas_call(functools.partial(sums_kernel, scale=scale), out_shape=(ja...]
    all_gather x3 -> x0, blocking collectives: 81.2 us -> none  [the longest x1 58 us: neighbour_pad(): lax.all_gather(as_sent(rim_rows[None]), 'tile', axis=0, tiled=True)]
    dot_general x60 -> x0, matrix products: 56.4 us -> none  [the longest x18 19.7 us: conv_taps(): jnp.dot(weights[3 * row_tap + col_tap], window, preferred_element_type=jn...]
    unnamed x108 -> x10, local copies, waits for them, and re-layouts: 50.1 us -> 7.08 us
  transfers between devices with their start and end apart: 8 -> 0, of which waited for: 6 -> 0; matrix products, arithmetic and copies ran while one was open for 9% -> 0% of each run, Pallas kernels for 0% -> 0%
where the time goes in v1:
time: 138 us
  Pallas kernels  121 us (88%)
  local copies, waits for them, and re-layouts  12.4 us (9%)
  other arithmetic  3.2 us (2%)
    pallas_call x1, Pallas kernels, sums_call(): pl.pallas_call(functools.partial(sums_kernel, scale=scale), out_shape=(ja...  31.5 us
    pallas_call x1, Pallas kernels, strips_call(): pl.pallas_call(strips_kernel, out_shape=(jax.ShapeDtypeStruct((128, 1280)...  31 us
    pallas_call x1, Pallas kernels, back_rims_call(): pl.pallas_call(back_rims_kernel, out_shape=(jax.ShapeDtypeStruct((128, 12...  23 us
    pallas_call x1, Pallas kernels, coarse_rims_call(): pl.pallas_call(coarse_rims_kernel, out_shape=(jax.ShapeDtypeStruct((128,...  22.4 us
    unnamed x10, local copies, waits for them, and re-layouts  7.08 us
    pallas_call x1, Pallas kernels, coarse_call(): pl.pallas_call(coarse_kernel, out_shape=(jax.ShapeDtypeStruct((128, 1024)...  4.76 us
    pallas_call x1, Pallas kernels, fine_call(): pl.pallas_call(fine_kernel, out_shape=(jax.ShapeDtypeStruct((3, 1280, 128...  4.41 us
    pallas_call x1, Pallas kernels, fine_back_call(): pl.pallas_call(fine_back_kernel, out_shape=jax.ShapeDtypeStruct((128, 166...  4.14 us

profile of v1, /device:TPU:1, one launch (start us, length us, event | category | flops | bytes accessed | tf_op | source)
XLA Modules:
  0.0 137.5 jit_solution(5937690432981717585)
XLA Ops:
  0.8 0.7 add.77
  1.6 0.9 constant_dynamic-slice_fusion.1
  2.6 0.7 fusion.2
  3.4 0.5 and_select_fusion.2.table
  4.1 0.7 fusion.13
  5.0 0.6 add_add_fusion.target
  5.6 1.5 %reshape.40 = bf16[32,64,64]{2,1,0:T(8,128)(2,1)S(1)} reshape(bf16[32,4096]{1,0:T(8,128)(2,1)} %feat.1) | data formatting | bytes 524288 | tf_op jit(solution)/shard_map/reshape | solution.py:685
  7.5 0.2 fusion.12
  7.8 0.4 rev.17
  8.2 0.3 copy.21
  8.5 0.3 copy.26
  9.0 0.6 pad_maximum_fusion.rims
  9.7 31.0 %shard_map.182 = (bf16[128,1280]{1,0:T(8,128)(2,1)}, bf16[128,1024]{1,0:T(8,128)(2,1)}, bf16[9,128,128]{2,1,0:T(8,128)(2,1)}, bf16[4,128,128]{2,1,0:T(8,128)(2,1...) custom-call(s32[64]{0:T(128)} %and_select_fusion.2.table, ...), custom_call_target="tpu_custom_call" | custom-call | tf_op jit(solution)/shard_map/pallas_call | solution.py:231
  40.7 4.4 %shard_map.183 = (bf16[3,1280,128]{2,1,0:T(8,128)(2,1)}, f32[1024,128]{1,0:T(8,128)}, bf16[1024,128]{1,0:T(8,128)(2,1)}, f32[256,128]{1,0:T(8,128)}, bf16[256,128]{1,0:T(8,128)(2,1)}, /*index=5*/bf16[128,128]{1,0:T(8,128)(2,1)}) custom-call(bf16[128,1280]{1,0:T(8,128)(2,1)} %get-tuple-element.36.f_ref, bf16[128,640]{1,0:T(8,128)(2,1)} %get-tuple-element.37.d_ref, ...), custom_call_target="tpu_custom_call" | custom-call | tf_op jit(solution)/shard_map/pallas_call | solution.py:306
  45.1 22.4 %shard_map.184 = (bf16[128,256]{1,0:T(8,128)(2,1)}, bf16[32,128]{1,0:T(8,128)(2,1)}, bf16[32,128]{1,0:T(8,128)(2,1)}) custom-call(s32[8,256]{1,0:T(8,128)} %add_add_fusion.target, bf16[128,128]{1,0:T(8,128)(2,1)} %get-tuple-element.41.rq, bf16[256,128]{1,0:T(8,128)(2,1)} %get-tuple-element.40.act2), custom_call_target="tpu_custom_call" | custom-call | tf_op jit(solution)/shard_map/pallas_call | solution.py:371
  67.5 4.8 %shard_map.185 = (bf16[128,1024]{1,0:T(8,128)(2,1)}, bf16[1024,128]{1,0:T(8,128)(2,1)}, f32[256,128]{1,0:T(8,128)}, f32[32,128]{1,0:T(8,128)}, f32[32,128]{1,0:T...) custom-call(bf16[256,128]{1,0:T(8,128)(2,1)} %get-tuple-element.40.act2, ...), custom_call_target="tpu_custom_call" | custom-call | tf_op jit(solution)/shard_map/pallas_call | solution.py:441
  72.2 23.0 %shard_map.186 = (f32[128,128]{1,0:T(8,128)}, f32[32,128]{1,0:T(8,128)}, f32[32,128]{1,0:T(8,128)}, bf16[32,4096]{1,0:T(8,128)(2,1)}) custom-call(s32[8,256]{1,0:T(8,128)} %add_add_fusion.target, bf16[128,256]{1,0:T(8,128)(2,1)} %get-tuple-element.49.dq, f32[32,128]{1,0:T(8,128)} %get-tuple-element.50.first, f32[32,128]{1,0:T(8,128)} %get-tuple-element.51.last, ...), custom_call_target="tpu_custom_call" | custom-call | tf_op jit(solution)/shard_map/pallas_call | solution.py:511
  95.2 4.1 %shard_map.187 = f32[128,1664]{1,0:T(8,128)} custom-call(f32[256,128]{1,0:T(8,128)} %get-tuple-element.54.center, f32[128,128]{1,0:T(8,128)} %get-tuple-element.55.t_ref, f32[32,128]{1,0:T(8,128)} %get-tuple-element.56.top, f32[32,128]{1,0:T(8,128)} %get-tuple-element.57.bottom, f32[256,128]{1,0:T(8,128)} %get-tuple-element.58.z2, ...), custom_call_target="tpu_custom_call" | custom-call | tf_op jit(solution)/shard_map/pallas_call | solution.py:555
  99.3 31.5 %shard_map.188 = (f32[9,32,128]{2,1,0:T(8,128)}, f32[4,32,128]{2,1,0:T(8,128)}, f32[9,32,128]{2,1,0:T(8,128)}, f32[32,128]{1,0:T(8,128)}) custom-call(f32[4,2,16,1664]{3,2,1,0:T(8,128)} %bitcast.44, f32[4,2,16,1280]{3,2,1,0:T(8,128)} %bitcast.46), custom_call_target="tpu_custom_call" | custom-call | tf_op jit(solution)/shard_map/pallas_call | solution.py:627
  130.8 0.7 copy.32
  131.5 1.6 %copy.33 = f32[9,32,128]{2,1,0:T(8,128)} copy(f32[9,32,128]{2,1,0:T(8,128)} %get-tuple-element.81) | data formatting | bytes 294912
  133.1 1.5 %copy.34 = f32[4,32,128]{2,1,0:T(8,128)} copy(f32[4,32,128]{2,1,0:T(8,128)} %get-tuple-element.82) | data formatting | bytes 131072
  134.6 1.6 %copy.35 = f32[9,32,128]{2,1,0:T(8,128)} copy(f32[9,32,128]{2,1,0:T(8,128)} %get-tuple-element.83) | data formatting | bytes 294912
  136.2 1.3 copy.36
  (24 shorter events, 1.6 us)
Async XLA Ops:
  95.2 35.7 %copy-start = (bf16[32,4096]{1,0:T(8,128)(2,1)S(1)}, bf16[32,4096]{1,0:T(8,128)(2,1)}, u32[]{:S(2)}) copy-start(bf16[32,4096]{1,0:T(8,128)(2,1)} %get-tuple-element.80) | copy-start | bytes 786436

commit v2 on v1

v2 whole, which is shorter than its diff:
```python
import functools

import jax
import jax.numpy as jnp
import numpy as np
from jax import lax
from jax.experimental import pallas as pl
from jax.experimental.pallas import tpu as pltpu
from jax.sharding import PartitionSpec as P

BF = jnp.bfloat16
F32 = jnp.float32
MESH = pl.DeviceIdType.MESH
TURNS = (0, 1, 2, 3, 0, 2, 2, 0)
VM = pl.BlockSpec(memory_space=pltpu.VMEM)
SM = pl.BlockSpec(memory_space=pltpu.SMEM)
ANY = pl.BlockSpec(memory_space=pl.ANY)
LIMIT = 56 * 1024 * 1024


def fine_perm():
    out = np.zeros((3, 128, 128), np.float32)
    for b in range(3):
        for rr in range(2):
            for par in range(2):
                for k in range(32):
                    col = 2 * (k - 1 + b) + par
                    if 0 <= col < 64:
                        out[b, rr * 64 + par * 32 + k, rr * 64 + col] = 1
    return out


def corner_maps():
    out = np.zeros((4, 128, 128), np.float32)
    for i in range(2):
        for j in range(2):
            out[0, i * 64 + j, 2 * i + j] = 1
            out[1, (1 - i) * 64 + 63 - j, 4 + 2 * i + j] = 1
            out[2, (1 - i) * 64 + 1 - j, 8 + 2 * i + j] = 1
            out[3, i * 64 + 62 + j, 12 + 2 * i + j] = 1
    return out


def fine_rim_maps():
    sel = np.zeros((4, 128, 640), np.float32)
    for q in range(4):
        for r in range(20):
            ir = 16 * q - 2 + r
            for par in range(2):
                if 0 <= ir < 64:
                    west = 384 + par * 64 + 63 - ir
                    east = 128 + (1 - par) * 64 + ir
                elif ir < 0:
                    west = 512 + 12 + 2 * (ir + 2) + par
                    east = 512 + 0 + 2 * (ir + 2) + par
                else:
                    west = 512 + 8 + 2 * (ir - 64) + par
                    east = 512 + 4 + 2 * (ir - 64) + par
                sel[q, r * 2 + par, west] = 1
                sel[q, 64 + r * 2 + par, east] = 1
    place = np.zeros((2, 1280, 128), np.float32)
    for r in range(20):
        for par in range(2):
            place[0, r * 64 + par * 32, r * 2 + par] = 1
            place[1, r * 64 + par * 32 + 31, 64 + r * 2 + par] = 1
    return sel, place


def fine_rim_out():
    pick = np.zeros((1024, 128), np.float32)
    for r in range(16):
        for kind, col in enumerate((0, 1, 62, 63)):
            pick[r * 64 + col, kind * 16 + r] = 1
    put = np.zeros((4, 128, 256), np.float32)
    for s in range(4):
        for r16 in range(16):
            r = 16 * s + r16
            for kind, lane in enumerate((64 + r, r, 128 + 63 - r, 192 + 63 - r)):
                put[s, kind * 16 + r16, lane] = 1
    return pick, put


def coarse_rim_out():
    out = np.zeros((4, 256, 128), np.float32)
    for i in range(32):
        for s, (r, k) in enumerate(((31, i), (i, 0), (0, 31 - i), (31 - i, 31))):
            out[r // 8, (r % 8) * 32 + k, s * 32 + i] = 1
    return out


def coarse_rim_in():
    out = np.zeros((4, 960, 256), np.float32)
    for k in range(32):
        out[0, k, k] = 1
        out[3, 9 * 32 + k, 64 + 31 - k] = 1
    for q in range(4):
        for r in range(10):
            row = 8 * q - 1 + r
            if row < 0:
                west, east = 131, 128
            elif row >= 32:
                west, east = 130, 129
            else:
                west, east = 96 + 31 - row, 32 + row
            out[q, 320 + r * 32, west] = 1
            out[q, 640 + r * 32 + 31, east] = 1
    return out


def nt(a, b):
    return lax.dot_general(a, b, (((1,), (1,)), ((), ())), preferred_element_type=F32)


def tn(a, b):
    return lax.dot_general(a, b, (((0,), (0,)), ((), ())), preferred_element_type=F32)


def nn(a, b):
    return lax.dot_general(a, b, (((1,), (0,)), ((), ())), preferred_element_type=F32)


ROOT = 0.7978845608028654


def gelu(v):
    return 0.5 * v * (1.0 + jnp.tanh(ROOT * (v + 0.044715 * (v * v * v))))


def gelu_slope(v):
    t = jnp.tanh(ROOT * (v + 0.044715 * (v * v * v)))
    return 0.5 * (1.0 + t) + 0.5 * v * (1.0 - t * t) * (ROOT * (1.0 + 3 * 0.044715 * (v * v)))


def place_of():
    tile = lax.axis_index("tile")
    return tile, tile // 8, lax.rem(tile, 8), lax.axis_index("chan")


def x_peer(d):
    tile, _, _, x = place_of()
    return (tile, lax.rem(x + d, 4))


def z_peer(d):
    _, z, g, x = place_of()
    return (lax.rem(z + d, 8) * 8 + g, x)


def g_peer(d):
    _, z, g, x = place_of()
    return (z * 8 + lax.rem(g + d, 8), x)


def core_peer():
    tile, _, g, x = place_of()
    return (tile + 1 - 2 * lax.rem(g, 2), x)


def xy_peer(dx, dy):
    _, z, g, x = place_of()
    return (z * 8 + lax.rem(g + 2 * dy, 8), lax.rem(x + dx, 4))


def greet(peers):
    barrier = pltpu.get_barrier_semaphore()
    for peer in peers:
        pl.semaphore_signal(barrier, inc=1, device_id=peer, device_id_type=MESH)
    pl.semaphore_wait(barrier, len(peers))


def push(src, dst, ssem, rsem, peer):
    copy = pltpu.make_async_remote_copy(
        src_ref=src, dst_ref=dst, send_sem=ssem, recv_sem=rsem, device_id=peer, device_id_type=MESH
    )
    copy.start()
    return copy


AW, BW = 2048, 1536
XD = (1, 3, 2)
ZD = (4, 3, 5, 2, 6, 1, 7)
GD = (4, 3, 5, 2, 6, 1, 7)
XYD = [(dx, dy) for dx in range(4) for dy in range(4) if dx or dy]


def side_by_side(weights, count):
    return jnp.concatenate([weights[t] for t in range(count)], axis=1)


def quarters(act):
    parts = act.reshape(8, 2, 2, 32, 128)
    return jnp.concatenate(
        [parts[:, a, b].reshape(256, 128) for a in range(2) for b in range(2)], axis=1
    )


def flip_map():
    rows = lax.broadcasted_iota(jnp.int32, (128, 128), 0)
    cols = lax.broadcasted_iota(jnp.int32, (128, 128), 1)
    return jnp.where(rows + cols == 127, 1.0, 0.0).astype(BF)


def level_kernel(*refs):
    names = INPUTS + ("out", "final") + tuple(n for n, _ in SCRATCH)
    r = dict(zip(names, refs))
    tile, z, g, x = place_of()
    y, core = g // 2, lax.rem(g, 2)
    q = x
    adj = r["adj"]
    mine = pl.ds(pl.multiple_of(x * 32, 32), 32)

    def rows_of(n):
        return pl.ds(pl.multiple_of(n * 32, 32), 32)

    def local(n, src, dst):
        copy = pltpu.make_async_copy(src, dst, r["lsem"].at[n])
        copy.start()
        return copy

    own_feat = local(0, r["feat"], r["fv"])
    own = {
        "pick": local(1, r["pick"], r["v_pick"]),
        "put": local(2, r["put"], r["v_put"]),
        "perm": local(3, r["perm"], r["v_perm"]),
        "cmap": local(4, r["cmap"], r["v_cmap"]),
        "fsel": local(5, r["fsel"].at[q], r["v_fsel"]),
        "place": local(6, r["place"], r["v_place"]),
        "rout": local(7, r["rout"].at[q], r["v_rout"]),
        "rin": local(8, r["rin"].at[q], r["v_rin"]),
    }
    greet(
        [x_peer(d) for d in XD] + [z_peer(d) for d in ZD] + [g_peer(d) for d in GD]
        + [xy_peer(dx, dy) for dx, dy in XYD if dx and dy]
    )

    def piece(n, j):
        if n == 0:
            start = pl.multiple_of(jnp.clip(j * 1024 - 128, 0, 2816), 128)
            return r["feat"].at[:, pl.ds(start, 1280)], r["strip"].at[mine, :]
        if n == 3:
            return r["ograd"].at[:, pl.ds(pl.multiple_of(j * 1024, 1024), 1024)], r["og"].at[mine, :]
        if n == 5:
            return r["up"], r["v_up"].at[mine, :]
        name = {1: "w1", 2: "wd", 4: "w2"}[n]
        return r[name], r["v_" + name].at[:, mine, :]

    bulk = [[] for _ in range(6)]

    def send_bulk(n):
        for d in XD:
            src, dst = piece(n, lax.rem(x + d, 4))
            bulk[n].append(push(src, dst, r["bs"].at[n, d], r["br"].at[n, d], x_peer(d)))
        src, dst = piece(n, x)
        bulk[n].append(local(9 + n, src, dst))

    def take_bulk(n):
        for c in bulk[n]:
            c.wait()

    def spread(kind, dirs, peer, src, dst):
        return [push(src(d), dst(d), r[kind + "s"].at[d], r[kind + "r"].at[d], peer(d)) for d in dirs]

    def settle(copies):
        for c in copies:
            c.wait()

    send_bulk(0)
    send_bulk(1)

    own["pick"].wait()
    own["put"].wait()
    own_feat.wait()
    fv, held = r["fv"], r["held"]
    stacked = jnp.concatenate([fv[:, s * 1024:(s + 1) * 1024] for s in range(4)], axis=0)
    cols = nn(stacked, r["v_pick"][...]).astype(BF)
    both = nn(cols[0:32], r["v_put"][0])
    for s in range(1, 4):
        both = both + nn(cols[32 * s:32 * s + 32], r["v_put"][s])
    flip = flip_map()
    held[z * 4] = fv[:, 3968:4096]
    held[z * 4 + 1] = both[:, 0:128].astype(BF)
    held[z * 4 + 2] = nn(fv[:, 0:128], flip).astype(BF)
    held[z * 4 + 3] = both[:, 128:256].astype(BF)
    here = held.at[pl.ds(z * 4, 4)]
    c_z = spread("z1", ZD, z_peer, lambda d: here, lambda d: here)
    for n in range(2, 6):
        send_bulk(n)

    def entry(j, k):
        at = ((z * 8 + j) * 8 + k) * 2
        p = adj[at]
        s = lax.rem(adj[at + 1] + TURNS[k], 4)
        owned = jnp.logical_and(p >= 0, lax.rem(p, 8) == g)
        return owned, p // 8, s

    lane = lax.broadcasted_iota(jnp.int32, (1, 256), 1)
    depth = lax.broadcasted_iota(jnp.int32, (1024, 256), 0)
    for j in range(8):
        target = jnp.full((1, 256), -1, jnp.int32)
        for k in range(8):
            owned, zp, s = entry(j, k)
            base = jnp.where(owned, zp * 128 + s * 32, -4096)
            if k < 4:
                here_k = jnp.logical_and(lane >= 32 * k, lane < 32 * k + 32)
                target = jnp.where(here_k, base + lane - 32 * k, target)
            else:
                target = jnp.where(lane == 124 + k, base + (0, 31, 0, 31)[k - 4], target)
        r["maps"][j] = jnp.where(depth == target, 1.0, 0.0).astype(BF)

    own["perm"].wait()
    take_bulk(0)
    perm, cb, strip = r["v_perm"], r["cb"], r["strip"]
    perms = perm[...].reshape(384, 128)
    shift = jnp.where(q == 0, -1, jnp.where(q == 3, 1, 0))

    def strip_block(n):
        at = jnp.clip(n + shift, 0, 9)
        return strip[:, pl.ds(pl.multiple_of(at * 128, 128), 128)]

    for n in range(1, 9):
        turned = nt(perms, strip_block(n))
        for b in range(3):
            cb[b, n * 128:(n + 1) * 128, :] = turned[b * 128:(b + 1) * 128].astype(BF)

    own["cmap"].wait()
    settle(c_z)
    slots, landed = r["slots"], r["landed"]
    c_g = []
    for d in GD + (0,):
        j = lax.rem(g + d, 8)
        corner = jnp.zeros((32, 128), F32)
        for k in range(8):
            owned, zp, s = entry(j, k)
            block = held[jnp.where(owned, zp * 4 + s, 0)]
            block = jnp.where(owned, block, jnp.zeros_like(block))
            if k < 4:
                slots[d, :, k * 128:(k + 1) * 128] = block
            else:
                corner = corner + nn(block, r["v_cmap"][k - 4])
        slots[d, :, 512:640] = corner.astype(BF)
        if d:
            c_g += spread("g1", (d,), g_peer, lambda d: slots.at[d], lambda d: landed.at[d])
    settle(c_g)
    total = slots[0].astype(F32)
    for d in range(1, 8):
        total = total + landed[d].astype(F32)
    picked = r["picked"]
    picked[mine, :] = total.astype(BF)
    part = picked.at[mine, :]
    c_x = spread("x1", XD, x_peer, lambda d: part, lambda d: part)
    own["fsel"].wait()
    own["place"].wait()
    take_bulk(1)
    take_bulk(2)
    w1c = side_by_side(r["v_w1"], 9)
    settle(c_x)

    rim_rows = nt(r["v_fsel"][...], picked[...]).astype(BF)
    for n in (0, 9):
        block = strip_block(n)
        if n == 0:
            block = jnp.where(q == 0, picked[:, 0:128], block)
        else:
            block = jnp.where(q == 3, nn(picked[:, 256:384], flip).astype(BF), block)
        turned = nt(perms, block)
        for b in range(3):
            cb[b, n * 128:(n + 1) * 128, :] = turned[b * 128:(b + 1) * 128].astype(BF)
    for b in (0, 2):
        cb[b] = (cb[b].astype(F32) + nn(r["v_place"][b // 2], rim_rows)).astype(BF)
    z1, act1 = r["z1"], r["act1"]
    for n in range(4):
        taps = jnp.concatenate(
            [cb[b, a * 128 + n * 256:a * 128 + n * 256 + 256, :] for a in range(3) for b in range(3)], axis=1
        )
        pre = nt(taps, w1c)
        z1[n * 256:(n + 1) * 256, :] = pre
        act1[n * 256:(n + 1) * 256, :] = gelu(pre).astype(BF)
    pre = nt(quarters(act1[...]), side_by_side(r["v_wd"], 4))
    r["z2"][...] = pre
    act2 = gelu(pre).astype(BF)
    r["act2"][...] = act2
    own["rout"].wait()
    rq = r["rq"]
    rq[...] = tn(act2, r["v_rout"][...]).astype(BF)

    c_x = spread("x2", XD, x_peer, lambda d: rq.at[rows_of(lax.rem(x + d, 4)), :], lambda d: r["x2in"].at[d])
    c_h = [
        push(r["act2"].at[pl.ds(224, 32), :], r["h_top"], r["hs"].at[0], r["hr"].at[0], x_peer(1)),
        push(r["act2"].at[pl.ds(0, 32), :], r["h_bot"], r["hs"].at[1], r["hr"].at[1], x_peer(3)),
    ]
    total = rq[mine, :].astype(F32)
    settle(c_x)
    for d in XD:
        total = total + r["x2in"][d].astype(F32)
    held2 = r["held2"]
    held2[z] = total.astype(BF)
    c_z = spread("z2", ZD, z_peer, lambda d: held2.at[z], lambda d: held2.at[z])

    take_bulk(3)
    take_bulk(5)
    og, ogt, up = r["og"], r["ogt"], r["v_up"]
    flat = perm[1]
    for n in range(8):
        ogt[n * 128:(n + 1) * 128, :] = nt(flat, og[:, n * 128:(n + 1) * 128]).astype(BF)
    cells = ogt[...].astype(F32).reshape(8, 4, 32, 128)
    pooled = (cells[:, 0] + cells[:, 1] + cells[:, 2] + cells[:, 3]).reshape(256, 128).astype(BF)
    back_up = nn(pooled, up[...])

    settle(c_z)
    every = jnp.concatenate([held2[n] for n in range(8)], axis=1)
    slots2, landed2 = r["slots2"], r["landed2"]
    c_g = []
    for d in GD + (0,):
        slots2[d] = nn(every, r["maps"][lax.rem(g + d, 8)]).astype(BF)
        if d:
            c_g += spread("g2", (d,), g_peer, lambda d: slots2.at[d], lambda d: landed2.at[d])
    settle(c_g)
    total = slots2[0].astype(F32)
    for d in range(1, 8):
        total = total + landed2[d].astype(F32)
    picked2 = r["picked2"]
    picked2[mine, :] = total.astype(BF)
    part2 = picked2.at[mine, :]
    c_x = spread("x3", XD, x_peer, lambda d: part2, lambda d: part2)
    own["rin"].wait()
    take_bulk(4)
    settle(c_h)
    settle(c_x)

    sel = r["v_rin"][...]
    rim = nt(sel, picked2[...])
    upper = jnp.where(q == 0, 0.0, r["h_top"][...].astype(F32))
    lower = jnp.where(q == 3, 0.0, r["h_bot"][...].astype(F32))
    rows = jnp.concatenate([upper, act2.astype(F32), lower], axis=0) + rim[0:320]
    col = lax.rem(lax.broadcasted_iota(jnp.int32, (320, 128), 0), 32)
    west = jnp.where(col == 0, 0.0, pltpu.roll(rows, 1, 0)) + rim[320:640]
    east = jnp.where(col == 31, 0.0, pltpu.roll(rows, 319, 0)) + rim[640:960]
    blocks = [v.astype(BF) for v in (west, rows, east)]
    taps2 = jnp.concatenate([blocks[b][a * 32:a * 32 + 256] for a in range(3) for b in range(3)], axis=1)
    w2 = r["v_w2"]
    pre = nt(taps2, side_by_side(w2, 9))
    gz3 = (gelu_slope(pre) * back_up).astype(BF)
    none32, none64 = jnp.zeros((32, 128), F32), jnp.zeros((64, 128), F32)
    back = []
    for b in range(3):
        v0, v1, v2 = (nn(gz3, w2[3 * a + b]) for a in range(3))
        back.append(
            jnp.concatenate([v0, none64], axis=0)
            + jnp.concatenate([none32, v1, none32], axis=0)
            + jnp.concatenate([none64, v2], axis=0)
        )
    mid = (
        back[1]
        + jnp.where(col == 31, 0.0, pltpu.roll(back[0], 319, 0))
        + jnp.where(col == 0, 0.0, pltpu.roll(back[2], 1, 0))
    )
    cat = jnp.concatenate([mid.astype(BF), back[0].astype(BF), back[2].astype(BF)], axis=0)
    dq = r["dq"]
    dq[...] = tn(cat, sel).astype(BF)
    c_x = spread("x4", XD, x_peer, lambda d: dq.at[rows_of(lax.rem(x + d, 4)), :], lambda d: r["x4in"].at[d])
    r["first"][...] = mid[0:32]
    r["last"][...] = mid[288:320]
    c_h = [
        push(r["last"], r["b_top"], r["hs"].at[2], r["hr"].at[2], x_peer(1)),
        push(r["first"], r["b_bot"], r["hs"].at[3], r["hr"].at[3], x_peer(3)),
    ]

    other = 1 - core

    def halves(name, wide, parts):
        outs, ins = r[name + "c"], r[name + "ci"]
        for n in range(4):
            rows_n = pl.ds(pl.multiple_of(n * 32 + other * 16, 16), 16)
            at = 0
            for ref in parts:
                width = ref.shape[1]
                outs[n, :, at:at + width] = ref[rows_n, :].astype(BF)
                at += width
            outs[n, :, at:wide] = jnp.zeros((16, wide - at), BF)
        return [push(outs, ins, r[name + "cs"], r[name + "cr"], core_peer())]

    def shares(name, wide, parts):
        outs, ins = r[name + "o"], r[name + "i"]
        share = wide // 4
        for n in range(4):
            rows_n = pl.ds(pl.multiple_of(n * 32 + core * 16, 16), 16)
            own_n = jnp.concatenate(
                [ref[rows_n, :] for ref in parts]
                + [jnp.zeros((16, wide - sum(ref.shape[1] for ref in parts)), F32)],
                axis=1,
            )
            summed = (own_n + r[name + "ci"][n].astype(F32)).astype(BF)
            for m in range(4):
                outs[n, m] = summed[:, m * share:(m + 1) * share]
        sent = []
        for dx, dy in XYD:
            at = dx * 4 + dy
            sent.append(
                push(
                    outs.at[lax.rem(x + dx, 4), lax.rem(y + dy, 4)], ins.at[at],
                    r["gs_" + name].at[at], r["gr_" + name].at[at], xy_peer(dx, dy),
                )
            )
        return sent

    def along_z(name):
        total = r[name + "o"][x, y].astype(F32)
        for n in range(1, 16):
            total = total + r[name + "i"][n].astype(F32)
        zall = r[name + "z"]
        zall[z] = total.astype(BF)
        return spread(name + "z", ZD, z_peer, lambda d: zall.at[z], lambda d: zall.at[z])

    def whole(name):
        zall = r[name + "z"]
        total = zall[0].astype(F32)
        for n in range(1, 8):
            total = total + zall[n].astype(F32)
        return total.astype(BF)

    coarse = gelu(pre).astype(BF)
    r["gb_u"][...] = tn(pooled, coarse)
    r["gb_w"][...] = tn(gz3, taps2)
    parts_b = (r["gb_w"], r["gb_u"])
    c_bc = halves("b", BW, parts_b)
    settle(c_x)
    total = dq[mine, :].astype(F32)
    for d in XD:
        total = total + r["x4in"][d].astype(F32)
    held3 = r["held3"]
    held3[g] = total.astype(BF)
    c_g = spread("g3", GD, g_peer, lambda d: held3.at[g], lambda d: held3.at[g])

    settle(c_bc)
    c_b = shares("b", BW, parts_b)
    lifted = nt(coarse, up[...])
    out, ostrip = r["out"], r["ostrip"]
    for n in range(8):
        row = lifted[n * 32:(n + 1) * 32]
        summed = act1[n * 128:(n + 1) * 128, :].astype(F32) + jnp.concatenate([row] * 4, axis=0)
        ostrip[:, n * 128:(n + 1) * 128] = tn(summed.astype(BF), flat).astype(BF)

    settle(c_g)
    total = nt(held3[0], r["maps"][0])
    for j in range(1, 8):
        total = total + nt(held3[j], r["maps"][j])
    slots3, landed3 = r["slots3"], r["landed3"]
    for n in range(8):
        slots3[n] = total[:, n * 128:(n + 1) * 128].astype(BF)
    c_z = spread("z3", ZD, z_peer, lambda d: slots3.at[lax.rem(z + d, 8)], lambda d: landed3.at[d])
    lanes = pl.ds(pl.multiple_of(x * 1024, 1024), 1024)
    c_o = spread("o", XD, x_peer, lambda d: ostrip.at[rows_of(lax.rem(x + d, 4)), :], lambda d: out.at[:, lanes])
    c_o.append(local(15, ostrip.at[mine, :], out.at[:, lanes]))
    slope2 = gelu_slope(r["z2"][...])
    settle(c_z)
    total = slots3[z].astype(F32)
    for d in ZD:
        total = total + landed3[d].astype(F32)
    back_rim = r["back_rim"]
    back_rim[mine, :] = total.astype(BF)
    part3 = back_rim.at[mine, :]
    c_x = spread("x5", XD, x_peer, lambda d: part3, lambda d: part3)
    settle(c_b)
    c_bz = along_z("b")
    settle(c_h)
    upper = jnp.where(q == 0, 0.0, r["b_top"][...])
    lower = jnp.where(q == 3, 0.0, r["b_bot"][...])
    ga2 = mid[32:288] + jnp.concatenate([upper, jnp.zeros((192, 128), F32), lower], axis=0)
    settle(c_x)

    gz2 = (slope2 * (ga2 + nt(r["v_rout"][...], back_rim[...]))).astype(BF)
    wd = r["v_wd"]
    fine = [nn(gz2, wd[t]).reshape(8, 1, 32, 128) for t in range(4)]
    grown = jnp.concatenate(fine, axis=1).reshape(1024, 128)
    gz1 = (gelu_slope(z1[...]) * (ogt[...].astype(F32) + grown)).astype(BF)
    for a in range(3):
        for b in range(3):
            t = 3 * a + b
            r["ga_w"][:, t * 128:(t + 1) * 128] = tn(gz1, cb[b, a * 128:a * 128 + 1024, :])
    r["ga_d"][...] = tn(gz2, quarters(act1[...]))
    parts_a = (r["ga_w"], r["ga_d"])
    settle(halves("a", AW, parts_a))
    settle(shares("a", AW, parts_a))
    c_az = along_z("a")
    final, yall = r["final"], r["yall"]
    settle(c_bz)
    yall[y, :, 512:896] = whole("b")
    settle(c_o)
    settle(c_az)
    yall[y, :, 0:512] = whole("a")
    part4 = yall.at[y]
    settle(spread("y", XD, lambda d: xy_peer(0, d), lambda d: part4, lambda d: part4))
    final[core] = yall[...]
    settle([push(yall, final.at[core], r["fs"], r["fr"], core_peer())])


INPUTS = (
    "adj", "feat", "ograd", "w1", "wd", "w2", "up",
    "pick", "put", "perm", "cmap", "fsel", "place", "rout", "rin",
)


def buf(*shape, kind=BF):
    return pltpu.VMEM(shape, kind)


def sems(*shape):
    return pltpu.SemaphoreType.DMA(shape)


SCRATCH = [
    ("lsem", sems(16)), ("bs", sems(6, 4)), ("br", sems(6, 4)), ("hs", sems(4)), ("hr", sems(4)),
    ("fv", buf(32, 4096)), ("v_pick", buf(1024, 128)), ("v_put", buf(4, 128, 256)), ("v_perm", buf(3, 128, 128)),
    ("v_cmap", buf(4, 128, 128)), ("v_fsel", buf(128, 640)), ("v_place", buf(2, 1280, 128)),
    ("v_rout", buf(256, 128)), ("v_rin", buf(960, 256)),
    ("strip", buf(128, 1280)), ("og", buf(128, 1024)), ("v_w1", buf(9, 128, 128)), ("v_wd", buf(4, 128, 128)),
    ("v_w2", buf(9, 128, 128)), ("v_up", buf(128, 128)),
    ("held", buf(32, 32, 128)), ("slots", buf(8, 32, 640)), ("landed", buf(8, 32, 640)), ("picked", buf(128, 640)),
    ("maps", buf(8, 1024, 256)), ("cb", buf(3, 1280, 128)), ("z1", buf(1024, 128, kind=F32)), ("act1", buf(1024, 128)),
    ("z2", buf(256, 128, kind=F32)), ("act2", buf(256, 128)), ("rq", buf(128, 128)), ("x2in", buf(4, 32, 128)),
    ("h_top", buf(32, 128)), ("h_bot", buf(32, 128)), ("held2", buf(8, 32, 128)), ("ogt", buf(1024, 128)),
    ("slots2", buf(8, 32, 256)), ("landed2", buf(8, 32, 256)), ("picked2", buf(128, 256)),
    ("dq", buf(128, 256)), ("x4in", buf(4, 32, 256)),
    ("first", buf(32, 128, kind=F32)), ("last", buf(32, 128, kind=F32)),
    ("b_top", buf(32, 128, kind=F32)), ("b_bot", buf(32, 128, kind=F32)),
    ("held3", buf(8, 32, 256)), ("ostrip", buf(128, 1024)), ("slots3", buf(8, 32, 128)), ("landed3", buf(8, 32, 128)),
    ("back_rim", buf(128, 128)),
    ("gb_u", buf(128, 128, kind=F32)), ("gb_w", buf(128, 1152, kind=F32)),
    ("ga_d", buf(128, 512, kind=F32)), ("ga_w", buf(128, 1152, kind=F32)),
    ("bc", buf(4, 16, BW)), ("bci", buf(4, 16, BW)), ("bo", buf(4, 4, 16, BW // 4)), ("bi", buf(16, 16, BW // 4)),
    ("bz", buf(8, 16, BW // 4)), ("bcs", pltpu.SemaphoreType.DMA), ("bcr", pltpu.SemaphoreType.DMA),
    ("ac", buf(4, 16, AW)), ("aci", buf(4, 16, AW)), ("ao", buf(4, 4, 16, AW // 4)), ("ai", buf(16, 16, AW // 4)),
    ("az", buf(8, 16, AW // 4)), ("acs", pltpu.SemaphoreType.DMA), ("acr", pltpu.SemaphoreType.DMA),
    ("gs_b", sems(16)), ("gr_b", sems(16)), ("gs_a", sems(16)), ("gr_a", sems(16)),
    ("yall", buf(4, 16, 896)), ("fs", pltpu.SemaphoreType.DMA), ("fr", pltpu.SemaphoreType.DMA),
] + [
    (kind + way, sems(8))
    for kind in ("z1", "z2", "z3", "g1", "g2", "g3", "x1", "x2", "x3", "x4", "x5", "o", "y", "bz", "az")
    for way in ("s", "r")
]


def level_call(*args):
    return pl.pallas_call(
        level_kernel,
        out_shape=(jax.ShapeDtypeStruct((32, 4096), BF), jax.ShapeDtypeStruct((2, 4, 16, 896), BF)),
        in_specs=[SM] + [ANY] * 14,
        out_specs=[VM] * 2,
        scratch_shapes=[s for _, s in SCRATCH],
        compiler_params=pltpu.CompilerParams(collective_id=0, has_side_effects=True, vmem_limit_bytes=LIMIT),
    )(*args)


def result_kernel(out_in, final, out, g1, gd, g2, gu, *, scale):
    out[...] = out_in[...]
    for c in range(2):
        rows = pl.ds(c * 16, 16)
        for t in range(13):
            block = final[c, t // 4, :, (t % 4) * 128:(t % 4 + 1) * 128].astype(F32) * scale
            if t < 9:
                g1[t, rows, :] = block
            else:
                gd[t - 9, rows, :] = block
        for t in range(10):
            at = 512 + (t % 3) * 128
            block = final[c, t // 3, :, at:at + 128].astype(F32) * scale
            if t < 9:
                g2[t, rows, :] = block
            else:
                gu[rows, :] = block


def result_call(out_in, final, scale):
    return pl.pallas_call(
        functools.partial(result_kernel, scale=scale),
        out_shape=(
            jax.ShapeDtypeStruct((32, 4096), BF),
            jax.ShapeDtypeStruct((9, 32, 128), F32),
            jax.ShapeDtypeStruct((4, 32, 128), F32),
            jax.ShapeDtypeStruct((9, 32, 128), F32),
            jax.ShapeDtypeStruct((32, 128), F32),
        ),
        in_specs=[VM] * 2,
        out_specs=[VM] * 5,
        compiler_params=pltpu.CompilerParams(vmem_limit_bytes=16 * 1024 * 1024),
    )(out_in, final)


def per_device(features, conv1_weight, down_weight, conv2_weight, up_weight, out_grad, adjacency):
    pick, put = fine_rim_out()
    fine_sel, fine_place = fine_rim_maps()
    maps = [
        jnp.asarray(m, BF)
        for m in (pick, put, fine_perm(), corner_maps(), fine_sel, fine_place, coarse_rim_out(), coarse_rim_in())
    ]
    out, final = level_call(
        adjacency.reshape(1024), features, out_grad, conv1_weight, down_weight, conv2_weight, up_weight, *maps
    )
    return result_call(out, final, 262144 ** -0.5)


def solution(mesh):
    weights = P(None, "chan", None)
    return jax.shard_map(
        per_device,
        mesh=mesh,
        in_specs=(P("chan", "tile"), weights, weights, weights, P("chan", None), P("chan", "tile"), P()),
        out_specs=(P("chan", "tile"), weights, weights, weights, P("chan", None)),
        check_vma=False,
    )
```

time: 138 us -> 95.8 us (0.69)
  Pallas kernels: 121 us -> 91.4 us
  local copies, waits for them, and re-layouts: 12.4 us -> 3.5 us
  other arithmetic: 3.2 us -> 0 us
    pallas_call x7 -> x2, Pallas kernels: 121 us -> 91.4 us  [the longest x1 90.6 us: level_call(): pl.pallas_call(level_kernel, out_shape=(jax.ShapeDtypeStruct((32, 4096),...]
    unnamed x10 -> x5, local copies, waits for them, and re-layouts: 7.08 us -> 2.74 us
where the time goes in v2:
time: 95.8 us; the launch traced here: 95.6 us
  Pallas kernels  91.4 us (95%)
  local copies, waits for them, and re-layouts  3.5 us (4%)
    pallas_call x1, Pallas kernels, level_call(): pl.pallas_call(level_kernel, out_shape=(jax.ShapeDtypeStruct((32, 4096),...  90.6 us
    unnamed x5, local copies, waits for them, and re-layouts  2.74 us

profile of v2, /device:TPU:1, one launch (start us, length us, event | category | flops | bytes accessed | tf_op | source)
XLA Modules:
  0.0 95.6 jit_solution(15707322809165101682)
XLA Ops:
  0.6 0.9 copy.20
  1.5 0.8 reshape.13.refs_0_
  2.3 90.6 %shard_map.182 = (bf16[32,4096]{1,0:T(8,128)(2,1)}, bf16[2,4,16,896]{3,2,1,0:T(8,128)(2,1)}) custom-call(s32[1024]{0:T(1024)} %reshape.13.refs_0_, bf16[32,4096]{1,0:T(8,128)(2,1)} %refs_1_.1, bf16[32,4096]{1,0:T(8,128)(2,1)} %refs_2_.1, bf16[9,32,128]{2,1,0:T(8,128)(2,1)} %refs_3_.1, bf16[4,32,128]{2,1,0:T(8,128)(2,1)} %refs_4_.1, ...), custom_call_target="tpu_custom_call" | custom-call | tf_op jit(solution)/shard_map/pallas_call | solution.py:644
  92.8 0.0 copy-start
  92.8 0.9 copy-done
  93.8 0.0 copy-start.1
  93.8 0.9 copy-done.1
  94.7 0.8 shard_map.183
Async XLA Ops:
  92.8 1.0 copy-start
  93.8 0.9 copy-start.1

commit v3 on v2

--- a/solution.py
+++ b/solution.py
@@ -13,7 +13,6 @@
 MESH = pl.DeviceIdType.MESH
 TURNS = (0, 1, 2, 3, 0, 2, 2, 0)
 VM = pl.BlockSpec(memory_space=pltpu.VMEM)
-SM = pl.BlockSpec(memory_space=pltpu.SMEM)
 ANY = pl.BlockSpec(memory_space=pl.ANY)
 LIMIT = 56 * 1024 * 1024
 
@@ -97,9 +96,9 @@
         for r in range(10):
             row = 8 * q - 1 + r
             if row < 0:
-                west, east = 131, 128
+                west, east = 255, 128
             elif row >= 32:
-                west, east = 130, 129
+                west, east = 192, 191
             else:
                 west, east = 96 + 31 - row, 32 + row
             out[q, 320 + r * 32, west] = 1
@@ -161,26 +160,12 @@
     return (z * 8 + lax.rem(g + 2 * dy, 8), lax.rem(x + dx, 4))
 
 
-def greet(peers):
-    barrier = pltpu.get_barrier_semaphore()
-    for peer in peers:
-        pl.semaphore_signal(barrier, inc=1, device_id=peer, device_id_type=MESH)
-    pl.semaphore_wait(barrier, len(peers))
-
-
-def push(src, dst, ssem, rsem, peer):
-    copy = pltpu.make_async_remote_copy(
-        src_ref=src, dst_ref=dst, send_sem=ssem, recv_sem=rsem, device_id=peer, device_id_type=MESH
-    )
-    copy.start()
-    return copy
-
-
 AW, BW = 2048, 1536
 XD = (1, 3, 2)
 ZD = (4, 3, 5, 2, 6, 1, 7)
 GD = (4, 3, 5, 2, 6, 1, 7)
 XYD = [(dx, dy) for dx in range(4) for dy in range(4) if dx or dy]
+EDGE = (0, 31, 0, 31)
 
 
 def side_by_side(weights, count):
@@ -206,8 +191,8 @@
     tile, z, g, x = place_of()
     y, core = g // 2, lax.rem(g, 2)
     q = x
-    adj = r["adj"]
     mine = pl.ds(pl.multiple_of(x * 32, 32), 32)
+    rounds = []
 
     def rows_of(n):
         return pl.ds(pl.multiple_of(n * 32, 32), 32)
@@ -217,21 +202,71 @@
         copy.start()
         return copy
 
+    def begin(whole):
+        rounds.append(whole)
+        return len(rounds) - 1
+
+    def push(n, src, dst, peer):
+        pltpu.make_async_remote_copy(
+            src_ref=src, dst_ref=dst, send_sem=r["ss"].at[n], recv_sem=r["rs"].at[n],
+            device_id=peer, device_id_type=MESH,
+        ).start()
+
+    def spread(whole, dirs, peer, src, dst):
+        n = begin(whole)
+        for d in dirs:
+            push(n, src(d), dst(d), peer(d))
+        return n
+
+    def settle(n):
+        pltpu.make_async_copy(rounds[n], rounds[n], r["rs"].at[n]).wait()
+
+    barrier = pltpu.get_barrier_semaphore()
+    peers = [x_peer(d) for d in XD] + [z_peer(d) for d in ZD] + [g_peer(d) for d in GD]
+    peers += [xy_peer(dx, dy) for dx, dy in XYD if dx and dy]
+    for peer in peers:
+        pl.semaphore_signal(barrier, inc=1, device_id=peer, device_id_type=MESH)
+
     own_feat = local(0, r["feat"], r["fv"])
     own = {
         "pick": local(1, r["pick"], r["v_pick"]),
         "put": local(2, r["put"], r["v_put"]),
-        "perm": local(3, r["perm"], r["v_perm"]),
+        "adj": local(3, r["adj"], r["s_adj"]),
         "cmap": local(4, r["cmap"], r["v_cmap"]),
-        "fsel": local(5, r["fsel"].at[q], r["v_fsel"]),
-        "place": local(6, r["place"], r["v_place"]),
-        "rout": local(7, r["rout"].at[q], r["v_rout"]),
-        "rin": local(8, r["rin"].at[q], r["v_rin"]),
+        "perm": local(5, r["perm"], r["v_perm"]),
+        "fsel": local(6, r["fsel"], r["v_fsel"]),
+        "place": local(7, r["place"], r["v_place"]),
+        "rout": local(8, r["rout"].at[q], r["v_rout"]),
+        "rin": local(9, r["rin"].at[q], r["v_rin"]),
     }
-    greet(
-        [x_peer(d) for d in XD] + [z_peer(d) for d in ZD] + [g_peer(d) for d in GD]
-        + [xy_peer(dx, dy) for dx, dy in XYD if dx and dy]
-    )
+    adj = r["s_adj"]
+
+    own["pick"].wait()
+    own["put"].wait()
+    own_feat.wait()
+    fv, held = r["fv"], (r["held0"], r["held1"])
+    stacked = jnp.concatenate([fv[:, s * 1024:(s + 1) * 1024] for s in range(4)], axis=0)
+    cols = nn(stacked, r["v_pick"][...]).astype(BF)
+    both = nn(cols[0:32], r["v_put"][0])
+    for s in range(1, 4):
+        both = both + nn(cols[32 * s:32 * s + 32], r["v_put"][s])
+    flip = flip_map()
+    rims = (
+        fv[:, 3968:4096],
+        both[:, 0:128].astype(BF),
+        nn(fv[:, 0:128], flip).astype(BF),
+        both[:, 128:256].astype(BF),
+    )
+    for s in range(4):
+        held[0][z * 4 + s] = rims[s][0:16]
+        held[1][g * 4 + s] = rims[s][16:32]
+    pl.semaphore_wait(barrier, len(peers))
+    ways = ((z, ZD, z_peer), (g, GD, g_peer))
+    first = []
+    for h in range(2):
+        at, dirs, peer = ways[h]
+        part = held[h].at[pl.ds(at * 4, 4)]
+        first.append(spread(held[h].at[pl.ds(0, 28)], dirs, peer, lambda d: part, lambda d: part))
 
     def piece(n, j):
         if n == 0:
@@ -244,68 +279,35 @@
         name = {1: "w1", 2: "wd", 4: "w2"}[n]
         return r[name], r["v_" + name].at[:, mine, :]
 
-    bulk = [[] for _ in range(6)]
+    bulk = {}
 
     def send_bulk(n):
+        three = pl.ds(0, 96)
+        into = r[("strip", "v_w1", "v_wd", "og", "v_w2", "v_up")[n]]
+        whole = into.at[:, three, :] if n in (1, 2, 4) else into.at[three, :]
+        m = begin(whole)
         for d in XD:
             src, dst = piece(n, lax.rem(x + d, 4))
-            bulk[n].append(push(src, dst, r["bs"].at[n, d], r["br"].at[n, d], x_peer(d)))
+            push(m, src, dst, x_peer(d))
         src, dst = piece(n, x)
-        bulk[n].append(local(9 + n, src, dst))
+        bulk[n] = (m, local(10 + n, src, dst))
 
     def take_bulk(n):
-        for c in bulk[n]:
-            c.wait()
-
-    def spread(kind, dirs, peer, src, dst):
-        return [push(src(d), dst(d), r[kind + "s"].at[d], r[kind + "r"].at[d], peer(d)) for d in dirs]
-
-    def settle(copies):
-        for c in copies:
-            c.wait()
-
-    send_bulk(0)
-    send_bulk(1)
-
-    own["pick"].wait()
-    own["put"].wait()
-    own_feat.wait()
-    fv, held = r["fv"], r["held"]
-    stacked = jnp.concatenate([fv[:, s * 1024:(s + 1) * 1024] for s in range(4)], axis=0)
-    cols = nn(stacked, r["v_pick"][...]).astype(BF)
-    both = nn(cols[0:32], r["v_put"][0])
-    for s in range(1, 4):
-        both = both + nn(cols[32 * s:32 * s + 32], r["v_put"][s])
-    flip = flip_map()
-    held[z * 4] = fv[:, 3968:4096]
-    held[z * 4 + 1] = both[:, 0:128].astype(BF)
-    held[z * 4 + 2] = nn(fv[:, 0:128], flip).astype(BF)
-    held[z * 4 + 3] = both[:, 128:256].astype(BF)
-    here = held.at[pl.ds(z * 4, 4)]
-    c_z = spread("z1", ZD, z_peer, lambda d: here, lambda d: here)
-    for n in range(2, 6):
+        m, copy = bulk[n]
+        copy.wait()
+        settle(m)
+
+    for n in range(3):
         send_bulk(n)
 
-    def entry(j, k):
-        at = ((z * 8 + j) * 8 + k) * 2
-        p = adj[at]
-        s = lax.rem(adj[at + 1] + TURNS[k], 4)
-        owned = jnp.logical_and(p >= 0, lax.rem(p, 8) == g)
-        return owned, p // 8, s
-
-    lane = lax.broadcasted_iota(jnp.int32, (1, 256), 1)
-    depth = lax.broadcasted_iota(jnp.int32, (1024, 256), 0)
-    for j in range(8):
-        target = jnp.full((1, 256), -1, jnp.int32)
-        for k in range(8):
-            owned, zp, s = entry(j, k)
-            base = jnp.where(owned, zp * 128 + s * 32, -4096)
-            if k < 4:
-                here_k = jnp.logical_and(lane >= 32 * k, lane < 32 * k + 32)
-                target = jnp.where(here_k, base + lane - 32 * k, target)
-            else:
-                target = jnp.where(lane == 124 + k, base + (0, 31, 0, 31)[k - 4], target)
-        r["maps"][j] = jnp.where(depth == target, 1.0, 0.0).astype(BF)
+    own["adj"].wait()
+
+    def entry(t, k, h=0):
+        p = adj[2 * k, t]
+        s = lax.rem(adj[2 * k + 1, t] + TURNS[k], 4)
+        if h:
+            return jnp.logical_and(p >= 0, p // 8 == z), lax.rem(p, 8), s
+        return jnp.logical_and(p >= 0, lax.rem(p, 8) == g), p // 8, s
 
     own["perm"].wait()
     take_bulk(0)
@@ -323,50 +325,67 @@
             cb[b, n * 128:(n + 1) * 128, :] = turned[b * 128:(b + 1) * 128].astype(BF)
 
     own["cmap"].wait()
-    settle(c_z)
     slots, landed = r["slots"], r["landed"]
-    c_g = []
-    for d in GD + (0,):
-        j = lax.rem(g + d, 8)
-        corner = jnp.zeros((32, 128), F32)
-        for k in range(8):
-            owned, zp, s = entry(j, k)
-            block = held[jnp.where(owned, zp * 4 + s, 0)]
-            block = jnp.where(owned, block, jnp.zeros_like(block))
-            if k < 4:
-                slots[d, :, k * 128:(k + 1) * 128] = block
-            else:
-                corner = corner + nn(block, r["v_cmap"][k - 4])
-        slots[d, :, 512:640] = corner.astype(BF)
-        if d:
-            c_g += spread("g1", (d,), g_peer, lambda d: slots.at[d], lambda d: landed.at[d])
-    settle(c_g)
-    total = slots[0].astype(F32)
-    for d in range(1, 8):
-        total = total + landed[d].astype(F32)
-    picked = r["picked"]
-    picked[mine, :] = total.astype(BF)
-    part = picked.at[mine, :]
-    c_x = spread("x1", XD, x_peer, lambda d: part, lambda d: part)
+    second = []
+    for h in (1, 0):
+        settle(first[h])
+        _, dirs, peer = ways[1 - h]
+        order = dirs + (0,)
+        m = begin(landed.at[h, pl.ds(1, 7)])
+        second.append(m)
+        corners = [[] for _ in range(4)]
+        for d in order:
+            t = z * 8 + lax.rem(g + d, 8) if h == 0 else lax.rem(z + d, 8) * 8 + g
+            for k in range(8):
+                owned, n, s = entry(t, k, h)
+                block = held[h][jnp.where(owned, n * 4 + s, 0)]
+                block = jnp.where(owned, block, jnp.zeros_like(block))
+                if k < 4:
+                    slots[h, d, :, k * 128:(k + 1) * 128] = block
+                else:
+                    corners[k - 4].append(block)
+        corner = nn(jnp.concatenate(corners[0], axis=0), r["v_cmap"][0])
+        for k in range(1, 4):
+            corner = corner + nn(jnp.concatenate(corners[k], axis=0), r["v_cmap"][k])
+        for n, d in enumerate(order):
+            slots[h, d, :, 512:640] = corner[16 * n:16 * n + 16].astype(BF)
+            if d:
+                push(m, slots.at[h, d], landed.at[h, d], peer(d))
+    halves_of = []
+    for m, h in zip(second, (1, 0)):
+        settle(m)
+        total = slots[h, 0].astype(F32)
+        for d in range(1, 8):
+            total = total + landed[h, d].astype(F32)
+        halves_of.append(total)
+    total = jnp.concatenate([halves_of[1], halves_of[0]], axis=0).astype(BF)
+
     own["fsel"].wait()
+    picked, pout = r["picked"], r["pout"]
+    ends = (total[:, 0:128], None, None, nn(total[:, 256:384], flip).astype(BF))
+    for j in range(4):
+        pout[j, :, 0:128] = nt(total, r["v_fsel"][j]).astype(BF)
+        pout[j, :, 128:256] = jnp.zeros((32, 128), BF) if ends[j] is None else ends[j]
+    c_x = spread(
+        picked.at[pl.ds(0, 96), :], XD, x_peer, lambda d: pout.at[lax.rem(x + d, 4)], lambda d: picked.at[mine, :]
+    )
+    picked[mine, :] = pout[x]
+    for n in range(3, 6):
+        send_bulk(n)
     own["place"].wait()
     take_bulk(1)
     take_bulk(2)
     w1c = side_by_side(r["v_w1"], 9)
     settle(c_x)
 
-    rim_rows = nt(r["v_fsel"][...], picked[...]).astype(BF)
     for n in (0, 9):
-        block = strip_block(n)
-        if n == 0:
-            block = jnp.where(q == 0, picked[:, 0:128], block)
-        else:
-            block = jnp.where(q == 3, nn(picked[:, 256:384], flip).astype(BF), block)
+        block = jnp.where(q == n // 3, picked[:, 128:256], strip_block(n))
         turned = nt(perms, block)
         for b in range(3):
             cb[b, n * 128:(n + 1) * 128, :] = turned[b * 128:(b + 1) * 128].astype(BF)
+    sides = picked[:, 0:128]
     for b in (0, 2):
-        cb[b] = (cb[b].astype(F32) + nn(r["v_place"][b // 2], rim_rows)).astype(BF)
+        cb[b] = (cb[b].astype(F32) + nt(r["v_place"][b // 2], sides)).astype(BF)
     z1, act1 = r["z1"], r["act1"]
     for n in range(4):
         taps = jnp.concatenate(
@@ -383,18 +402,20 @@
     rq = r["rq"]
     rq[...] = tn(act2, r["v_rout"][...]).astype(BF)
 
-    c_x = spread("x2", XD, x_peer, lambda d: rq.at[rows_of(lax.rem(x + d, 4)), :], lambda d: r["x2in"].at[d])
-    c_h = [
-        push(r["act2"].at[pl.ds(224, 32), :], r["h_top"], r["hs"].at[0], r["hr"].at[0], x_peer(1)),
-        push(r["act2"].at[pl.ds(0, 32), :], r["h_bot"], r["hs"].at[1], r["hr"].at[1], x_peer(3)),
-    ]
+    x2in, halo = r["x2in"], r["halo"]
+    c_x = spread(
+        x2in.at[pl.ds(1, 3)], XD, x_peer, lambda d: rq.at[rows_of(lax.rem(x + d, 4)), :], lambda d: x2in.at[d]
+    )
+    c_h = begin(halo)
+    push(c_h, r["act2"].at[pl.ds(224, 32), :], halo.at[0], x_peer(1))
+    push(c_h, r["act2"].at[pl.ds(0, 32), :], halo.at[1], x_peer(3))
     total = rq[mine, :].astype(F32)
     settle(c_x)
     for d in XD:
-        total = total + r["x2in"][d].astype(F32)
+        total = total + x2in[d].astype(F32)
     held2 = r["held2"]
     held2[z] = total.astype(BF)
-    c_z = spread("z2", ZD, z_peer, lambda d: held2.at[z], lambda d: held2.at[z])
+    c_z = spread(held2.at[pl.ds(0, 7)], ZD, z_peer, lambda d: held2.at[z], lambda d: held2.at[z])
 
     take_bulk(3)
     take_bulk(5)
@@ -407,13 +428,30 @@
     back_up = nn(pooled, up[...])
 
     settle(c_z)
-    every = jnp.concatenate([held2[n] for n in range(8)], axis=1)
+    rolled = r["rolled"]
+    for n in range(8):
+        block = held2[n].astype(F32)
+        rolled[n * 4] = held2[n]
+        for m in range(1, 4):
+            rolled[n * 4 + m] = pltpu.roll(block, 32 * m, 1).astype(BF)
+    lane = lax.broadcasted_iota(jnp.int32, (32, 128), 1)
     slots2, landed2 = r["slots2"], r["landed2"]
-    c_g = []
+    c_g = begin(landed2.at[pl.ds(1, 7)])
     for d in GD + (0,):
-        slots2[d] = nn(every, r["maps"][lax.rem(g + d, 8)]).astype(BF)
+        t = z * 8 + lax.rem(g + d, 8)
+        both = [jnp.zeros((32, 128), F32), jnp.zeros((32, 128), F32)]
+        for k in range(8):
+            owned, n, s = entry(t, k)
+            block = rolled[jnp.where(owned, n * 4 + lax.rem(k + 4 - s, 4), 0)].astype(F32)
+            block = jnp.where(owned, block, 0.0)
+            if k < 4:
+                both[0] = jnp.where(lane // 32 == k, block, both[0])
+            else:
+                both[1] = jnp.where(lane == 32 * (k - 4) + EDGE[k - 4], block, both[1])
+        slots2[d, :, 0:128] = both[0].astype(BF)
+        slots2[d, :, 128:256] = both[1].astype(BF)
         if d:
-            c_g += spread("g2", (d,), g_peer, lambda d: slots2.at[d], lambda d: landed2.at[d])
+            push(c_g, slots2.at[d], landed2.at[d], g_peer(d))
     settle(c_g)
     total = slots2[0].astype(F32)
     for d in range(1, 8):
@@ -421,7 +459,7 @@
     picked2 = r["picked2"]
     picked2[mine, :] = total.astype(BF)
     part2 = picked2.at[mine, :]
-    c_x = spread("x3", XD, x_peer, lambda d: part2, lambda d: part2)
+    c_x = spread(picked2.at[pl.ds(0, 96), :], XD, x_peer, lambda d: part2, lambda d: part2)
     own["rin"].wait()
     take_bulk(4)
     settle(c_h)
@@ -429,8 +467,8 @@
 
     sel = r["v_rin"][...]
     rim = nt(sel, picked2[...])
-    upper = jnp.where(q == 0, 0.0, r["h_top"][...].astype(F32))
-    lower = jnp.where(q == 3, 0.0, r["h_bot"][...].astype(F32))
+    upper = jnp.where(q == 0, 0.0, halo[0].astype(F32))
+    lower = jnp.where(q == 3, 0.0, halo[1].astype(F32))
     rows = jnp.concatenate([upper, act2.astype(F32), lower], axis=0) + rim[0:320]
     col = lax.rem(lax.broadcasted_iota(jnp.int32, (320, 128), 0), 32)
     west = jnp.where(col == 0, 0.0, pltpu.roll(rows, 1, 0)) + rim[320:640]
@@ -457,13 +495,15 @@
     cat = jnp.concatenate([mid.astype(BF), back[0].astype(BF), back[2].astype(BF)], axis=0)
     dq = r["dq"]
     dq[...] = tn(cat, sel).astype(BF)
-    c_x = spread("x4", XD, x_peer, lambda d: dq.at[rows_of(lax.rem(x + d, 4)), :], lambda d: r["x4in"].at[d])
-    r["first"][...] = mid[0:32]
-    r["last"][...] = mid[288:320]
-    c_h = [
-        push(r["last"], r["b_top"], r["hs"].at[2], r["hr"].at[2], x_peer(1)),
-        push(r["first"], r["b_bot"], r["hs"].at[3], r["hr"].at[3], x_peer(3)),
-    ]
+    x4in, hout, hin = r["x4in"], r["hout"], r["hin"]
+    c_x = spread(
+        x4in.at[pl.ds(1, 3)], XD, x_peer, lambda d: dq.at[rows_of(lax.rem(x + d, 4)), :], lambda d: x4in.at[d]
+    )
+    hout[0] = mid[288:320]
+    hout[1] = mid[0:32]
+    c_h = begin(hin)
+    push(c_h, hout.at[0], hin.at[0], x_peer(1))
+    push(c_h, hout.at[1], hin.at[1], x_peer(3))
 
     other = 1 - core
 
@@ -477,7 +517,9 @@
                 outs[n, :, at:at + width] = ref[rows_n, :].astype(BF)
                 at += width
             outs[n, :, at:wide] = jnp.zeros((16, wide - at), BF)
-        return [push(outs, ins, r[name + "cs"], r[name + "cr"], core_peer())]
+        n = begin(ins)
+        push(n, outs, ins, core_peer())
+        return n
 
     def shares(name, wide, parts):
         outs, ins = r[name + "o"], r[name + "i"]
@@ -492,16 +534,10 @@
             summed = (own_n + r[name + "ci"][n].astype(F32)).astype(BF)
             for m in range(4):
                 outs[n, m] = summed[:, m * share:(m + 1) * share]
-        sent = []
+        m = begin(ins.at[pl.ds(1, 15)])
         for dx, dy in XYD:
-            at = dx * 4 + dy
-            sent.append(
-                push(
-                    outs.at[lax.rem(x + dx, 4), lax.rem(y + dy, 4)], ins.at[at],
-                    r["gs_" + name].at[at], r["gr_" + name].at[at], xy_peer(dx, dy),
-                )
-            )
-        return sent
+            push(m, outs.at[lax.rem(x + dx, 4), lax.rem(y + dy, 4)], ins.at[dx * 4 + dy], xy_peer(dx, dy))
+        return m
 
     def along_z(name):
         total = r[name + "o"][x, y].astype(F32)
@@ -509,7 +545,7 @@
             total = total + r[name + "i"][n].astype(F32)
         zall = r[name + "z"]
         zall[z] = total.astype(BF)
-        return spread(name + "z", ZD, z_peer, lambda d: zall.at[z], lambda d: zall.at[z])
+        return spread(zall.at[pl.ds(0, 7)], ZD, z_peer, lambda d: zall.at[z], lambda d: zall.at[z])
 
     def whole(name):
         zall = r[name + "z"]
@@ -526,10 +562,10 @@
     settle(c_x)
     total = dq[mine, :].astype(F32)
     for d in XD:
-        total = total + r["x4in"][d].astype(F32)
+        total = total + x4in[d].astype(F32)
     held3 = r["held3"]
     held3[g] = total.astype(BF)
-    c_g = spread("g3", GD, g_peer, lambda d: held3.at[g], lambda d: held3.at[g])
+    c_g = spread(held3.at[pl.ds(0, 7)], GD, g_peer, lambda d: held3.at[g], lambda d: held3.at[g])
 
     settle(c_bc)
     c_b = shares("b", BW, parts_b)
@@ -541,16 +577,31 @@
         ostrip[:, n * 128:(n + 1) * 128] = tn(summed.astype(BF), flat).astype(BF)
 
     settle(c_g)
-    total = nt(held3[0], r["maps"][0])
-    for j in range(1, 8):
-        total = total + nt(held3[j], r["maps"][j])
+    rolled3 = r["rolled3"]
+    for j in range(8):
+        for h in range(2):
+            block = held3[j, :, 128 * h:128 * h + 128]
+            rolled3[j * 8 + h * 4] = block
+            for m in range(1, 4):
+                rolled3[j * 8 + h * 4 + m] = pltpu.roll(block.astype(F32), 32 * m, 1).astype(BF)
+    sums = [jnp.zeros((32, 128), F32) for _ in range(8)]
+    for j in range(8):
+        for k in range(8):
+            owned, n, s = entry(z * 8 + j, k)
+            block = rolled3[j * 8 + (k // 4) * 4 + lax.rem(s + 4 - k % 4, 4)].astype(F32)
+            if k < 4:
+                block = jnp.where(lane // 32 == s, block, 0.0)
+            else:
+                block = jnp.where(lane == 32 * s + EDGE[k - 4], block, 0.0)
+            n = jnp.where(owned, n, -1)
+            for m in range(8):
+                sums[m] = sums[m] + jnp.where(n == m, block, 0.0)
     slots3, landed3 = r["slots3"], r["landed3"]
     for n in range(8):
-        slots3[n] = total[:, n * 128:(n + 1) * 128].astype(BF)
-    c_z = spread("z3", ZD, z_peer, lambda d: slots3.at[lax.rem(z + d, 8)], lambda d: landed3.at[d])
-    lanes = pl.ds(pl.multiple_of(x * 1024, 1024), 1024)
-    c_o = spread("o", XD, x_peer, lambda d: ostrip.at[rows_of(lax.rem(x + d, 4)), :], lambda d: out.at[:, lanes])
-    c_o.append(local(15, ostrip.at[mine, :], out.at[:, lanes]))
+        slots3[n] = sums[n].astype(BF)
+    c_z = spread(
+        landed3.at[pl.ds(1, 7)], ZD, z_peer, lambda d: slots3.at[lax.rem(z + d, 8)], lambda d: landed3.at[d]
+    )
     slope2 = gelu_slope(r["z2"][...])
     settle(c_z)
     total = slots3[z].astype(F32)
@@ -559,12 +610,18 @@
     back_rim = r["back_rim"]
     back_rim[mine, :] = total.astype(BF)
     part3 = back_rim.at[mine, :]
-    c_x = spread("x5", XD, x_peer, lambda d: part3, lambda d: part3)
+    c_x = spread(back_rim.at[pl.ds(0, 96), :], XD, x_peer, lambda d: part3, lambda d: part3)
+    lanes = pl.ds(pl.multiple_of(x * 1024, 1024), 1024)
+    c_o = spread(
+        out.at[:, pl.ds(0, 3072)], XD, x_peer,
+        lambda d: ostrip.at[rows_of(lax.rem(x + d, 4)), :], lambda d: out.at[:, lanes],
+    )
+    own_out = local(16, ostrip.at[mine, :], out.at[:, lanes])
     settle(c_b)
     c_bz = along_z("b")
     settle(c_h)
-    upper = jnp.where(q == 0, 0.0, r["b_top"][...])
-    lower = jnp.where(q == 3, 0.0, r["b_bot"][...])
+    upper = jnp.where(q == 0, 0.0, hin[0])
+    lower = jnp.where(q == 3, 0.0, hin[1])
     ga2 = mid[32:288] + jnp.concatenate([upper, jnp.zeros((192, 128), F32), lower], axis=0)
     settle(c_x)
 
@@ -589,9 +646,14 @@
     settle(c_az)
     yall[y, :, 0:512] = whole("a")
     part4 = yall.at[y]
-    settle(spread("y", XD, lambda d: xy_peer(0, d), lambda d: part4, lambda d: part4))
+    settle(spread(yall.at[pl.ds(0, 3)], XD, lambda d: xy_peer(0, d), lambda d: part4, lambda d: part4))
     final[core] = yall[...]
-    settle([push(yall, final.at[core], r["fs"], r["fr"], core_peer())])
+    n = begin(yall)
+    push(n, yall, final.at[core], core_peer())
+    settle(n)
+    own_out.wait()
+    for n, whole in enumerate(rounds):
+        pltpu.make_async_copy(whole, whole, r["ss"].at[n]).wait()
 
 
 INPUTS = (
@@ -609,34 +671,29 @@
 
 
 SCRATCH = [
-    ("lsem", sems(16)), ("bs", sems(6, 4)), ("br", sems(6, 4)), ("hs", sems(4)), ("hr", sems(4)),
+    ("lsem", sems(17)), ("ss", sems(30)), ("rs", sems(30)), ("s_adj", pltpu.SMEM((16, 64), jnp.int32)),
     ("fv", buf(32, 4096)), ("v_pick", buf(1024, 128)), ("v_put", buf(4, 128, 256)), ("v_perm", buf(3, 128, 128)),
-    ("v_cmap", buf(4, 128, 128)), ("v_fsel", buf(128, 640)), ("v_place", buf(2, 1280, 128)),
+    ("v_cmap", buf(4, 128, 128)), ("v_fsel", buf(4, 128, 640)), ("v_place", buf(2, 1280, 128)),
     ("v_rout", buf(256, 128)), ("v_rin", buf(960, 256)),
     ("strip", buf(128, 1280)), ("og", buf(128, 1024)), ("v_w1", buf(9, 128, 128)), ("v_wd", buf(4, 128, 128)),
     ("v_w2", buf(9, 128, 128)), ("v_up", buf(128, 128)),
-    ("held", buf(32, 32, 128)), ("slots", buf(8, 32, 640)), ("landed", buf(8, 32, 640)), ("picked", buf(128, 640)),
-    ("maps", buf(8, 1024, 256)), ("cb", buf(3, 1280, 128)), ("z1", buf(1024, 128, kind=F32)), ("act1", buf(1024, 128)),
+    ("held0", buf(32, 16, 128)), ("held1", buf(32, 16, 128)), ("slots", buf(2, 8, 16, 640)), ("landed", buf(2, 8, 16, 640)),
+    ("pout", buf(4, 32, 256)), ("picked", buf(128, 256)),
+    ("cb", buf(3, 1280, 128)), ("z1", buf(1024, 128, kind=F32)), ("act1", buf(1024, 128)),
     ("z2", buf(256, 128, kind=F32)), ("act2", buf(256, 128)), ("rq", buf(128, 128)), ("x2in", buf(4, 32, 128)),
-    ("h_top", buf(32, 128)), ("h_bot", buf(32, 128)), ("held2", buf(8, 32, 128)), ("ogt", buf(1024, 128)),
+    ("halo", buf(2, 32, 128)), ("held2", buf(8, 32, 128)), ("rolled", buf(32, 32, 128)), ("ogt", buf(1024, 128)),
     ("slots2", buf(8, 32, 256)), ("landed2", buf(8, 32, 256)), ("picked2", buf(128, 256)),
     ("dq", buf(128, 256)), ("x4in", buf(4, 32, 256)),
-    ("first", buf(32, 128, kind=F32)), ("last", buf(32, 128, kind=F32)),
-    ("b_top", buf(32, 128, kind=F32)), ("b_bot", buf(32, 128, kind=F32)),
-    ("held3", buf(8, 32, 256)), ("ostrip", buf(128, 1024)), ("slots3", buf(8, 32, 128)), ("landed3", buf(8, 32, 128)),
-    ("back_rim", buf(128, 128)),
+    ("hout", buf(2, 32, 128, kind=F32)), ("hin", buf(2, 32, 128, kind=F32)),
+    ("held3", buf(8, 32, 256)), ("rolled3", buf(64, 32, 128)), ("ostrip", buf(128, 1024)),
+    ("slots3", buf(8, 32, 128)), ("landed3", buf(8, 32, 128)), ("back_rim", buf(128, 128)),
     ("gb_u", buf(128, 128, kind=F32)), ("gb_w", buf(128, 1152, kind=F32)),
     ("ga_d", buf(128, 512, kind=F32)), ("ga_w", buf(128, 1152, kind=F32)),
     ("bc", buf(4, 16, BW)), ("bci", buf(4, 16, BW)), ("bo", buf(4, 4, 16, BW // 4)), ("bi", buf(16, 16, BW // 4)),
-    ("bz", buf(8, 16, BW // 4)), ("bcs", pltpu.SemaphoreType.DMA), ("bcr", pltpu.SemaphoreType.DMA),
+    ("bz", buf(8, 16, BW // 4)),
     ("ac", buf(4, 16, AW)), ("aci", buf(4, 16, AW)), ("ao", buf(4, 4, 16, AW // 4)), ("ai", buf(16, 16, AW // 4)),
-    ("az", buf(8, 16, AW // 4)), ("acs", pltpu.SemaphoreType.DMA), ("acr", pltpu.SemaphoreType.DMA),
-    ("gs_b", sems(16)), ("gr_b", sems(16)), ("gs_a", sems(16)), ("gr_a", sems(16)),
-    ("yall", buf(4, 16, 896)), ("fs", pltpu.SemaphoreType.DMA), ("fr", pltpu.SemaphoreType.DMA),
-] + [
-    (kind + way, sems(8))
-    for kind in ("z1", "z2", "z3", "g1", "g2", "g3", "x1", "x2", "x3", "x4", "x5", "o", "y", "bz", "az")
-    for way in ("s", "r")
+    ("az", buf(8, 16, AW // 4)),
+    ("yall", buf(4, 16, 896)),
 ]
 
 
@@ -644,7 +701,7 @@
     return pl.pallas_call(
         level_kernel,
         out_shape=(jax.ShapeDtypeStruct((32, 4096), BF), jax.ShapeDtypeStruct((2, 4, 16, 896), BF)),
-        in_specs=[SM] + [ANY] * 14,
+        in_specs=[ANY] * 15,
         out_specs=[VM] * 2,
         scratch_shapes=[s for _, s in SCRATCH],
         compiler_params=pltpu.CompilerParams(collective_id=0, has_side_effects=True, vmem_limit_bytes=LIMIT),
@@ -694,7 +751,7 @@
         for m in (pick, put, fine_perm(), corner_maps(), fine_sel, fine_place, coarse_rim_out(), coarse_rim_in())
     ]
     out, final = level_call(
-        adjacency.reshape(1024), features, out_grad, conv1_weight, down_weight, conv2_weight, up_weight, *maps
+        adjacency.transpose(1, 2, 0).reshape(16, 64), features, out_grad, conv1_weight, down_weight, conv2_weight, up_weight, *maps
     )
     return result_call(out, final, 262144 ** -0.5)
 

time: 95.8 us -> 89.4 us (0.933)
  Pallas kernels: 91.4 us -> 86.6 us
  local copies, waits for them, and re-layouts: 3.5 us -> 1.88 us
    pallas_call x1, Pallas kernels: 90.6 us -> 85.8 us  [level_call(): pl.pallas_call(level_kernel, out_shape=(jax.ShapeDtypeStruct((32, 4096),...]
    unnamed x5 -> x4, local copies, waits for them, and re-layouts: 2.74 us -> 1.88 us
where the time goes in v3:
time: 89.4 us; the launch traced here: 89.2 us
  Pallas kernels  86.6 us (97%)
  local copies, waits for them, and re-layouts  1.88 us (2%)
    pallas_call x1, Pallas kernels, level_call(): pl.pallas_call(level_kernel, out_shape=(jax.ShapeDtypeStruct((32, 4096),...  85.8 us
    unnamed x4, local copies, waits for them, and re-layouts  1.88 us

profile of v3, /device:TPU:1, one launch (start us, length us, event | category | flops | bytes accessed | tf_op | source)
XLA Modules:
  0.0 89.2 jit_solution(2393432357898677978)
XLA Ops:
  0.6 85.8 %shard_map.182 = (bf16[32,4096]{1,0:T(8,128)(2,1)}, bf16[2,4,16,896]{3,2,1,0:T(8,128)(2,1)}) custom-call(s32[16,64]{1,0:T(8,128)} %bitcast.3, bf16[32,4096]{1,0:T(8,128)(2,1)} %refs_1_.1, bf16[32,4096]{1,0:T(8,128)(2,1)} %refs_2_.1, bf16[9,32,128]{2,1,0:T(8,128)(2,1)} %refs_3_.1, bf16[4,32,128]{2,1,0:T(8,128)(2,1)} %refs_4_.1, bf16[9,32,128]{2,1,0:T(8,128)(2,1)} %refs_5_.1, ...), custom_call_target="tpu_custom_call" | custom-call | tf_op jit(solution)/shard_map/pallas_call | solution.py:701
  86.4 0.0 copy-start
  86.4 0.9 %copy-done = bf16[32,4096]{1,0:T(8,128)(2,1)S(1)} copy-done((bf16[32,4096]{1,0:T(8,128)(2,1)S(1)}, bf16[32,4096]{1,0:T(8,128)(2,1)}, u32[]{:S(2)}) %copy-start) | copy-done | bytes 262168
  87.4 0.0 copy-start.1
  87.4 0.9 %copy-done.1 = bf16[2,4,16,896]{3,2,1,0:T(8,128)(2,1)S(1)} copy-done((bf16[2,4,16,896]{3,2,1,0:T(8,128)(2,1)S(1)}, bf16[2,4,16,896]{3,2,1,0:T(8,128)(2,1)}, u32[]{:S(2)}) %copy-start.1) | copy-done | bytes 229400
  88.3 0.8 shard_map.183
Async XLA Ops:
  86.4 1.0 %copy-start = (bf16[32,4096]{1,0:T(8,128)(2,1)S(1)}, bf16[32,4096]{1,0:T(8,128)(2,1)}, u32[]{:S(2)}) copy-start(bf16[32,4096]{1,0:T(8,128)(2,1)} %get-tuple-element.7.out_in) | copy-start | bytes 786436
  87.4 0.9 %copy-start.1 = (bf16[2,4,16,896]{3,2,1,0:T(8,128)(2,1)S(1)}, bf16[2,4,16,896]{3,2,1,0:T(8,128)(2,1)}, u32[]{:S(2)}) copy-start(bf16[2,4,16,896]{3,2,1,0:T(8,128)(2,1)} %get-tuple-element.8.final) | copy-start | bytes 688132

commit v4 on v3

--- a/solution.py
+++ b/solution.py
@@ -186,7 +186,7 @@
 
 
 def level_kernel(*refs):
-    names = INPUTS + ("out", "final") + tuple(n for n, _ in SCRATCH)
+    names = INPUTS + ("out", "final_a", "final_b") + tuple(n for n, _ in SCRATCH)
     r = dict(zip(names, refs))
     tile, z, g, x = place_of()
     y, core = g // 2, lax.rem(g, 2)
@@ -297,7 +297,7 @@
         copy.wait()
         settle(m)
 
-    for n in range(3):
+    for n in range(4):
         send_bulk(n)
 
     own["adj"].wait()
@@ -308,21 +308,6 @@
         if h:
             return jnp.logical_and(p >= 0, p // 8 == z), lax.rem(p, 8), s
         return jnp.logical_and(p >= 0, lax.rem(p, 8) == g), p // 8, s
-
-    own["perm"].wait()
-    take_bulk(0)
-    perm, cb, strip = r["v_perm"], r["cb"], r["strip"]
-    perms = perm[...].reshape(384, 128)
-    shift = jnp.where(q == 0, -1, jnp.where(q == 3, 1, 0))
-
-    def strip_block(n):
-        at = jnp.clip(n + shift, 0, 9)
-        return strip[:, pl.ds(pl.multiple_of(at * 128, 128), 128)]
-
-    for n in range(1, 9):
-        turned = nt(perms, strip_block(n))
-        for b in range(3):
-            cb[b, n * 128:(n + 1) * 128, :] = turned[b * 128:(b + 1) * 128].astype(BF)
 
     own["cmap"].wait()
     slots, landed = r["slots"], r["landed"]
@@ -351,6 +336,21 @@
             slots[h, d, :, 512:640] = corner[16 * n:16 * n + 16].astype(BF)
             if d:
                 push(m, slots.at[h, d], landed.at[h, d], peer(d))
+    own["perm"].wait()
+    take_bulk(0)
+    perm, cb, strip = r["v_perm"], r["cb"], r["strip"]
+    perms = perm[...].reshape(384, 128)
+    shift = jnp.where(q == 0, -1, jnp.where(q == 3, 1, 0))
+
+    def strip_block(n):
+        at = jnp.clip(n + shift, 0, 9)
+        return strip[:, pl.ds(pl.multiple_of(at * 128, 128), 128)]
+
+    for n in range(1, 9):
+        turned = nt(perms, strip_block(n))
+        for b in range(3):
+            cb[b, n * 128:(n + 1) * 128, :] = turned[b * 128:(b + 1) * 128].astype(BF)
+
     halves_of = []
     for m, h in zip(second, (1, 0)):
         settle(m)
@@ -370,7 +370,7 @@
         picked.at[pl.ds(0, 96), :], XD, x_peer, lambda d: pout.at[lax.rem(x + d, 4)], lambda d: picked.at[mine, :]
     )
     picked[mine, :] = pout[x]
-    for n in range(3, 6):
+    for n in (5, 4):
         send_bulk(n)
     own["place"].wait()
     take_bulk(1)
@@ -555,10 +555,13 @@
         return total.astype(BF)
 
     coarse = gelu(pre).astype(BF)
-    r["gb_u"][...] = tn(pooled, coarse)
-    r["gb_w"][...] = tn(gz3, taps2)
-    parts_b = (r["gb_w"], r["gb_u"])
-    c_bc = halves("b", BW, parts_b)
+    lifted = nt(coarse, up[...])
+    out, ostrip = r["out"], r["ostrip"]
+    for n in range(8):
+        row = lifted[n * 32:(n + 1) * 32]
+        summed = act1[n * 128:(n + 1) * 128, :].astype(F32) + jnp.concatenate([row] * 4, axis=0)
+        ostrip[:, n * 128:(n + 1) * 128] = tn(summed.astype(BF), flat).astype(BF)
+
     settle(c_x)
     total = dq[mine, :].astype(F32)
     for d in XD:
@@ -566,16 +569,17 @@
     held3 = r["held3"]
     held3[g] = total.astype(BF)
     c_g = spread(held3.at[pl.ds(0, 7)], GD, g_peer, lambda d: held3.at[g], lambda d: held3.at[g])
-
-    settle(c_bc)
-    c_b = shares("b", BW, parts_b)
-    lifted = nt(coarse, up[...])
-    out, ostrip = r["out"], r["ostrip"]
-    for n in range(8):
-        row = lifted[n * 32:(n + 1) * 32]
-        summed = act1[n * 128:(n + 1) * 128, :].astype(F32) + jnp.concatenate([row] * 4, axis=0)
-        ostrip[:, n * 128:(n + 1) * 128] = tn(summed.astype(BF), flat).astype(BF)
-
+    lanes = pl.ds(pl.multiple_of(x * 1024, 1024), 1024)
+    c_o = spread(
+        out.at[:, pl.ds(0, 3072)], XD, x_peer,
+        lambda d: ostrip.at[rows_of(lax.rem(x + d, 4)), :], lambda d: out.at[:, lanes],
+    )
+    own_out = local(16, ostrip.at[mine, :], out.at[:, lanes])
+
+    r["gb_u"][...] = tn(pooled, coarse)
+    r["gb_w"][...] = tn(gz3, taps2)
+    parts_b = (r["gb_w"], r["gb_u"])
+    c_bc = halves("b", BW, parts_b)
     settle(c_g)
     rolled3 = r["rolled3"]
     for j in range(8):
@@ -602,6 +606,8 @@
     c_z = spread(
         landed3.at[pl.ds(1, 7)], ZD, z_peer, lambda d: slots3.at[lax.rem(z + d, 8)], lambda d: landed3.at[d]
     )
+    settle(c_bc)
+    c_b = shares("b", BW, parts_b)
     slope2 = gelu_slope(r["z2"][...])
     settle(c_z)
     total = slots3[z].astype(F32)
@@ -611,12 +617,6 @@
     back_rim[mine, :] = total.astype(BF)
     part3 = back_rim.at[mine, :]
     c_x = spread(back_rim.at[pl.ds(0, 96), :], XD, x_peer, lambda d: part3, lambda d: part3)
-    lanes = pl.ds(pl.multiple_of(x * 1024, 1024), 1024)
-    c_o = spread(
-        out.at[:, pl.ds(0, 3072)], XD, x_peer,
-        lambda d: ostrip.at[rows_of(lax.rem(x + d, 4)), :], lambda d: out.at[:, lanes],
-    )
-    own_out = local(16, ostrip.at[mine, :], out.at[:, lanes])
     settle(c_b)
     c_bz = along_z("b")
     settle(c_h)
@@ -636,21 +636,31 @@
             r["ga_w"][:, t * 128:(t + 1) * 128] = tn(gz1, cb[b, a * 128:a * 128 + 1024, :])
     r["ga_d"][...] = tn(gz2, quarters(act1[...]))
     parts_a = (r["ga_w"], r["ga_d"])
-    settle(halves("a", AW, parts_a))
-    settle(shares("a", AW, parts_a))
+    c_ac = halves("a", AW, parts_a)
+
+    def along_y(name, n):
+        settle(n)
+        yall = r[name + "y"]
+        yall[y] = whole(name)
+        return spread(yall.at[pl.ds(0, 3)], XD, lambda d: xy_peer(0, d), lambda d: yall.at[y], lambda d: yall.at[y])
+
+    def to_core(name, n):
+        settle(n)
+        yall, final = r[name + "y"], r["final_" + name]
+        m = begin(yall)
+        push(m, yall, final.at[core], core_peer())
+        final[core] = yall[...]
+        return m
+
+    c_by = along_y("b", c_bz)
+    settle(c_ac)
+    c_a = shares("a", AW, parts_a)
+    c_bf = to_core("b", c_by)
+    settle(c_a)
     c_az = along_z("a")
-    final, yall = r["final"], r["yall"]
-    settle(c_bz)
-    yall[y, :, 512:896] = whole("b")
+    settle(c_bf)
     settle(c_o)
-    settle(c_az)
-    yall[y, :, 0:512] = whole("a")
-    part4 = yall.at[y]
-    settle(spread(yall.at[pl.ds(0, 3)], XD, lambda d: xy_peer(0, d), lambda d: part4, lambda d: part4))
-    final[core] = yall[...]
-    n = begin(yall)
-    push(n, yall, final.at[core], core_peer())
-    settle(n)
+    settle(to_core("a", along_y("a", c_az)))
     own_out.wait()
     for n, whole in enumerate(rounds):
         pltpu.make_async_copy(whole, whole, r["ss"].at[n]).wait()
@@ -671,7 +681,7 @@
 
 
 SCRATCH = [
-    ("lsem", sems(17)), ("ss", sems(30)), ("rs", sems(30)), ("s_adj", pltpu.SMEM((16, 64), jnp.int32)),
+    ("lsem", sems(17)), ("ss", sems(32)), ("rs", sems(32)), ("s_adj", pltpu.SMEM((16, 64), jnp.int32)),
     ("fv", buf(32, 4096)), ("v_pick", buf(1024, 128)), ("v_put", buf(4, 128, 256)), ("v_perm", buf(3, 128, 128)),
     ("v_cmap", buf(4, 128, 128)), ("v_fsel", buf(4, 128, 640)), ("v_place", buf(2, 1280, 128)),
     ("v_rout", buf(256, 128)), ("v_rin", buf(960, 256)),
@@ -693,41 +703,41 @@
     ("bz", buf(8, 16, BW // 4)),
     ("ac", buf(4, 16, AW)), ("aci", buf(4, 16, AW)), ("ao", buf(4, 4, 16, AW // 4)), ("ai", buf(16, 16, AW // 4)),
     ("az", buf(8, 16, AW // 4)),
-    ("yall", buf(4, 16, 896)),
+    ("ay", buf(4, 16, AW // 4)), ("by", buf(4, 16, BW // 4)),
 ]
 
 
 def level_call(*args):
     return pl.pallas_call(
         level_kernel,
-        out_shape=(jax.ShapeDtypeStruct((32, 4096), BF), jax.ShapeDtypeStruct((2, 4, 16, 896), BF)),
+        out_shape=(pltpu.VMEM((32, 4096), BF), pltpu.VMEM((2, 4, 16, AW // 4), BF), pltpu.VMEM((2, 4, 16, BW // 4), BF)),
         in_specs=[ANY] * 15,
-        out_specs=[VM] * 2,
+        out_specs=[VM] * 3,
         scratch_shapes=[s for _, s in SCRATCH],
         compiler_params=pltpu.CompilerParams(collective_id=0, has_side_effects=True, vmem_limit_bytes=LIMIT),
     )(*args)
 
 
-def result_kernel(out_in, final, out, g1, gd, g2, gu, *, scale):
+def result_kernel(out_in, final_a, final_b, out, g1, gd, g2, gu, *, scale):
     out[...] = out_in[...]
     for c in range(2):
         rows = pl.ds(c * 16, 16)
         for t in range(13):
-            block = final[c, t // 4, :, (t % 4) * 128:(t % 4 + 1) * 128].astype(F32) * scale
+            block = final_a[c, t // 4, :, (t % 4) * 128:(t % 4 + 1) * 128].astype(F32) * scale
             if t < 9:
                 g1[t, rows, :] = block
             else:
                 gd[t - 9, rows, :] = block
         for t in range(10):
-            at = 512 + (t % 3) * 128
-            block = final[c, t // 3, :, at:at + 128].astype(F32) * scale
+            at = (t % 3) * 128
+            block = final_b[c, t // 3, :, at:at + 128].astype(F32) * scale
             if t < 9:
                 g2[t, rows, :] = block
             else:
                 gu[rows, :] = block
 
 
-def result_call(out_in, final, scale):
+def result_call(out_in, final_a, final_b, scale):
     return pl.pallas_call(
         functools.partial(result_kernel, scale=scale),
         out_shape=(
@@ -737,10 +747,10 @@
             jax.ShapeDtypeStruct((9, 32, 128), F32),
             jax.ShapeDtypeStruct((32, 128), F32),
         ),
-        in_specs=[VM] * 2,
+        in_specs=[VM] * 3,
         out_specs=[VM] * 5,
         compiler_params=pltpu.CompilerParams(vmem_limit_bytes=16 * 1024 * 1024),
-    )(out_in, final)
+    )(out_in, final_a, final_b)
 
 
 def per_device(features, conv1_weight, down_weight, conv2_weight, up_weight, out_grad, adjacency):
@@ -750,10 +760,10 @@
         jnp.asarray(m, BF)
         for m in (pick, put, fine_perm(), corner_maps(), fine_sel, fine_place, coarse_rim_out(), coarse_rim_in())
     ]
-    out, final = level_call(
+    out, final_a, final_b = level_call(
         adjacency.transpose(1, 2, 0).reshape(16, 64), features, out_grad, conv1_weight, down_weight, conv2_weight, up_weight, *maps
     )
-    return result_call(out, final, 262144 ** -0.5)
+    return result_call(out, final_a, final_b, 262144 ** -0.5)
 
 
 def solution(mesh):

time: 89.4 us -> 83.1 us (0.930)
  Pallas kernels: 86.6 us -> 82.3 us
  local copies, waits for them, and re-layouts: 1.88 us -> 0 us
    pallas_call x1, Pallas kernels: 85.8 us -> 81.5 us  [level_call(): pl.pallas_call(level_kernel, out_shape=(pltpu.VMEM((32, 4096), BF), pltpu...]
    unnamed x4 -> x0, local copies, waits for them, and re-layouts: 1.88 us -> none
where the time goes in v4:
time: 83.1 us; the launch traced here: 83 us
  Pallas kernels  82.3 us (99%)
    pallas_call x1, Pallas kernels, level_call(): pl.pallas_call(level_kernel, out_shape=(pltpu.VMEM((32, 4096), BF), pltpu...  81.5 us

profile of v4, /device:TPU:1, one launch (start us, length us, event | category | flops | bytes accessed | tf_op | source)
XLA Modules:
  0.0 83.0 jit_solution(11856211227431890638)
XLA Ops:
  0.6 81.5 %shard_map.182 = (bf16[32,4096]{1,0:T(8,128)(2,1)S(1)}, bf16[2,4,16,512]{3,2,1,0:T(8,128)(2,1)S(1)}, bf16[2,4,16,384]{3,2,1,0:T(8,128)(2,1)S(1)}) custom-call(s32[16,64]{1,0:T(8,128)} %bitcast.3, bf16[32,4096]{1,0:T(8,128)(2,1)} %refs_1_.1, bf16[32,4096]{1,0:T(8,128)(2,1)} %refs_2_.1, bf16[9,32,128]{2,1,0:T(8,128)(2,1)} %refs_3_.1, ...), custom_call_target="tpu_custom_call" | custom-call | tf_op jit(solution)/shard_map/pallas_call | solution.py:711
  82.1 0.9 %shard_map.183 = (bf16[32,4096]{1,0:T(8,128)(2,1)}, f32[9,32,128]{2,1,0:T(8,128)}, f32[4,32,128]{2,1,0:T(8,128)}, f32[9,32,128]{2,1,0:T(8,128)}, f32[32,128]{1,0:T(8,128)}) custom-call(bf16[32,4096]{1,0:T(8,128)(2,1)S(1)} %get-tuple-element.8.out_in, bf16[2,4,16,512]{3,2,1,0:T(8,128)(2,1)S(1)} %get-tuple-element.9.final_a, ...), custom_call_target="tpu_custom_call" | custom-call | tf_op jit(solution)/shard_map/pallas_call | solution.py:741

commit v5 on v4

--- a/solution.py
+++ b/solution.py
@@ -161,10 +161,11 @@
 
 
 AW, BW = 2048, 1536
-XD = (1, 3, 2)
+XD = (2, 1, 3)
 ZD = (4, 3, 5, 2, 6, 1, 7)
 GD = (4, 3, 5, 2, 6, 1, 7)
-XYD = [(dx, dy) for dx in range(4) for dy in range(4) if dx or dy]
+FAR = (2, 1, 3, 0)
+XYD = [(dx, dy) for dx in FAR for dy in FAR if dx or dy]
 EDGE = (0, 31, 0, 31)
 
 
@@ -232,12 +233,6 @@
         "pick": local(1, r["pick"], r["v_pick"]),
         "put": local(2, r["put"], r["v_put"]),
         "adj": local(3, r["adj"], r["s_adj"]),
-        "cmap": local(4, r["cmap"], r["v_cmap"]),
-        "perm": local(5, r["perm"], r["v_perm"]),
-        "fsel": local(6, r["fsel"], r["v_fsel"]),
-        "place": local(7, r["place"], r["v_place"]),
-        "rout": local(8, r["rout"].at[q], r["v_rout"]),
-        "rin": local(9, r["rin"].at[q], r["v_rin"]),
     }
     adj = r["s_adj"]
 
@@ -267,6 +262,15 @@
         at, dirs, peer = ways[h]
         part = held[h].at[pl.ds(at * 4, 4)]
         first.append(spread(held[h].at[pl.ds(0, 28)], dirs, peer, lambda d: part, lambda d: part))
+
+    own.update({
+        "cmap": local(4, r["cmap"], r["v_cmap"]),
+        "perm": local(5, r["perm"], r["v_perm"]),
+        "fsel": local(6, r["fsel"], r["v_fsel"]),
+        "place": local(7, r["place"], r["v_place"]),
+        "rout": local(8, r["rout"].at[q], r["v_rout"]),
+        "rin": local(9, r["rin"].at[q], r["v_rin"]),
+    })
 
     def piece(n, j):
         if n == 0:
@@ -376,24 +380,49 @@
     take_bulk(1)
     take_bulk(2)
     w1c = side_by_side(r["v_w1"], 9)
-    settle(c_x)
-
     for n in (0, 9):
-        block = jnp.where(q == n // 3, picked[:, 128:256], strip_block(n))
-        turned = nt(perms, block)
+        block = strip_block(n)
+        turned = nt(perms, jnp.where(q == n // 3, jnp.zeros_like(block), block))
         for b in range(3):
             cb[b, n * 128:(n + 1) * 128, :] = turned[b * 128:(b + 1) * 128].astype(BF)
-    sides = picked[:, 0:128]
-    for b in (0, 2):
-        cb[b] = (cb[b].astype(F32) + nt(r["v_place"][b // 2], sides)).astype(BF)
     z1, act1 = r["z1"], r["act1"]
-    for n in range(4):
-        taps = jnp.concatenate(
+    w1 = r["v_w1"]
+
+    def fine_taps(n):
+        return jnp.concatenate(
             [cb[b, a * 128 + n * 256:a * 128 + n * 256 + 256, :] for a in range(3) for b in range(3)], axis=1
         )
-        pre = nt(taps, w1c)
-        z1[n * 256:(n + 1) * 256, :] = pre
-        act1[n * 256:(n + 1) * 256, :] = gelu(pre).astype(BF)
+
+    for n in range(4):
+        z1[n * 256:(n + 1) * 256, :] = nt(fine_taps(n), w1c)
+    w1_west = jnp.concatenate([w1[3 * a] for a in range(3)], axis=1)
+    w1_east = jnp.concatenate([w1[3 * a + 2] for a in range(3)], axis=1)
+    w1_end = jnp.where(q == 0, side_by_side(w1, 3), side_by_side(w1[6:9], 3))
+    unit = jnp.where(
+        lax.broadcasted_iota(jnp.int32, (128, 128), 0) == lax.broadcasted_iota(jnp.int32, (128, 128), 1), 1.0, 0.0
+    ).astype(BF)
+    settle(c_x)
+
+    sides = picked[:, 0:128]
+    side_rows = nt(unit, sides)
+    end_rows = nt(perms, picked[:, 128:256])
+    west = jnp.concatenate([side_rows[4 * a:4 * a + 32] for a in range(3)], axis=1).astype(BF)
+    east = jnp.concatenate([side_rows[64 + 4 * a:96 + 4 * a] for a in range(3)], axis=1).astype(BF)
+    ends = jnp.concatenate([end_rows[128 * b:128 * b + 128] for b in range(3)], axis=1).astype(BF)
+    west, east, ends = nt(west, w1_west), nt(east, w1_east), nt(ends, w1_end)
+    for n in range(8):
+        rows = slice(n * 128, (n + 1) * 128)
+        add = []
+        cell = lax.broadcasted_iota(jnp.int32, (32, 128), 0)
+        for m in range(4 * n, 4 * n + 4):
+            add.append(
+                jnp.where(cell == 0, west[m:m + 1], 0.0) + jnp.where(cell == 31, east[m:m + 1], 0.0)
+            )
+        pre = z1[rows, :] + jnp.concatenate(add, axis=0)
+        if n in (0, 7):
+            pre = pre + jnp.where(q == (0 if n == 0 else 3), ends, 0.0)
+        z1[rows, :] = pre
+        act1[rows, :] = gelu(pre).astype(BF)
     pre = nt(quarters(act1[...]), side_by_side(r["v_wd"], 4))
     r["z2"][...] = pre
     act2 = gelu(pre).astype(BF)
@@ -426,6 +455,16 @@
     cells = ogt[...].astype(F32).reshape(8, 4, 32, 128)
     pooled = (cells[:, 0] + cells[:, 1] + cells[:, 2] + cells[:, 3]).reshape(256, 128).astype(BF)
     back_up = nn(pooled, up[...])
+    for n in (0, 9):
+        for b in range(3):
+            rows = slice(n * 128, (n + 1) * 128)
+            new = jnp.where(q == n // 3, end_rows[b * 128:(b + 1) * 128], cb[b, rows, :].astype(F32))
+            cb[b, rows, :] = new.astype(BF)
+    for b in (0, 2):
+        cb[b] = (cb[b].astype(F32) + nt(r["v_place"][b // 2], sides)).astype(BF)
+    slope = gelu_slope(z1[...])
+    r["slope"][...] = slope
+    r["direct"][...] = slope * ogt[...].astype(F32)
 
     settle(c_z)
     rolled = r["rolled"]
@@ -629,38 +668,28 @@
     wd = r["v_wd"]
     fine = [nn(gz2, wd[t]).reshape(8, 1, 32, 128) for t in range(4)]
     grown = jnp.concatenate(fine, axis=1).reshape(1024, 128)
-    gz1 = (gelu_slope(z1[...]) * (ogt[...].astype(F32) + grown)).astype(BF)
-    for a in range(3):
-        for b in range(3):
-            t = 3 * a + b
-            r["ga_w"][:, t * 128:(t + 1) * 128] = tn(gz1, cb[b, a * 128:a * 128 + 1024, :])
+    gz1 = (r["direct"][...] + r["slope"][...] * grown).astype(BF)
+    r["ga_w"][...] = tn(
+        gz1, jnp.concatenate([cb[b, a * 128:a * 128 + 1024, :] for a in range(3) for b in range(3)], axis=1)
+    )
     r["ga_d"][...] = tn(gz2, quarters(act1[...]))
     parts_a = (r["ga_w"], r["ga_d"])
     c_ac = halves("a", AW, parts_a)
 
-    def along_y(name, n):
+    def to_row(name, n):
         settle(n)
-        yall = r[name + "y"]
-        yall[y] = whole(name)
-        return spread(yall.at[pl.ds(0, 3)], XD, lambda d: xy_peer(0, d), lambda d: yall.at[y], lambda d: yall.at[y])
-
-    def to_core(name, n):
-        settle(n)
-        yall, final = r[name + "y"], r["final_" + name]
-        m = begin(yall)
-        push(m, yall, final.at[core], core_peer())
-        final[core] = yall[...]
-        return m
-
-    c_by = along_y("b", c_bz)
+        final = r["final_" + name]
+        final[g] = whole(name)
+        return spread(final.at[pl.ds(0, 7)], GD, g_peer, lambda d: final.at[g], lambda d: final.at[g])
+
+    c_bg = to_row("b", c_bz)
     settle(c_ac)
     c_a = shares("a", AW, parts_a)
-    c_bf = to_core("b", c_by)
     settle(c_a)
     c_az = along_z("a")
-    settle(c_bf)
+    settle(c_bg)
     settle(c_o)
-    settle(to_core("a", along_y("a", c_az)))
+    settle(to_row("a", c_az))
     own_out.wait()
     for n, whole in enumerate(rounds):
         pltpu.make_async_copy(whole, whole, r["ss"].at[n]).wait()
@@ -691,6 +720,7 @@
     ("pout", buf(4, 32, 256)), ("picked", buf(128, 256)),
     ("cb", buf(3, 1280, 128)), ("z1", buf(1024, 128, kind=F32)), ("act1", buf(1024, 128)),
     ("z2", buf(256, 128, kind=F32)), ("act2", buf(256, 128)), ("rq", buf(128, 128)), ("x2in", buf(4, 32, 128)),
+    ("slope", buf(1024, 128, kind=F32)), ("direct", buf(1024, 128, kind=F32)),
     ("halo", buf(2, 32, 128)), ("held2", buf(8, 32, 128)), ("rolled", buf(32, 32, 128)), ("ogt", buf(1024, 128)),
     ("slots2", buf(8, 32, 256)), ("landed2", buf(8, 32, 256)), ("picked2", buf(128, 256)),
     ("dq", buf(128, 256)), ("x4in", buf(4, 32, 256)),
@@ -703,14 +733,13 @@
     ("bz", buf(8, 16, BW // 4)),
     ("ac", buf(4, 16, AW)), ("aci", buf(4, 16, AW)), ("ao", buf(4, 4, 16, AW // 4)), ("ai", buf(16, 16, AW // 4)),
     ("az", buf(8, 16, AW // 4)),
-    ("ay", buf(4, 16, AW // 4)), ("by", buf(4, 16, BW // 4)),
 ]
 
 
 def level_call(*args):
     return pl.pallas_call(
         level_kernel,
-        out_shape=(pltpu.VMEM((32, 4096), BF), pltpu.VMEM((2, 4, 16, AW // 4), BF), pltpu.VMEM((2, 4, 16, BW // 4), BF)),
+        out_shape=(pltpu.VMEM((32, 4096), BF), pltpu.VMEM((8, 16, AW // 4), BF), pltpu.VMEM((8, 16, BW // 4), BF)),
         in_specs=[ANY] * 15,
         out_specs=[VM] * 3,
         scratch_shapes=[s for _, s in SCRATCH],
@@ -723,14 +752,14 @@
     for c in range(2):
         rows = pl.ds(c * 16, 16)
         for t in range(13):
-            block = final_a[c, t // 4, :, (t % 4) * 128:(t % 4 + 1) * 128].astype(F32) * scale
+            block = final_a[2 * (t // 4) + c, :, (t % 4) * 128:(t % 4 + 1) * 128].astype(F32) * scale
             if t < 9:
                 g1[t, rows, :] = block
             else:
                 gd[t - 9, rows, :] = block
         for t in range(10):
             at = (t % 3) * 128
-            block = final_b[c, t // 3, :, at:at + 128].astype(F32) * scale
+            block = final_b[2 * (t // 3) + c, :, at:at + 128].astype(F32) * scale
             if t < 9:
                 g2[t, rows, :] = block
             else:

time: 83.1 us -> 80.6 us (0.970)
  Pallas kernels: 82.3 us -> 79.8 us
    pallas_call x1, Pallas kernels: 81.5 us -> 79 us  [level_call(): pl.pallas_call(level_kernel, out_shape=(pltpu.VMEM((32, 4096), BF), pltpu...]
where the time goes in v5:
time: 80.6 us; the launch traced here: 80.5 us
  Pallas kernels  79.8 us (99%)
    pallas_call x1, Pallas kernels, level_call(): pl.pallas_call(level_kernel, out_shape=(pltpu.VMEM((32, 4096), BF), pltpu...  79 us

profile of v5, /device:TPU:1, one launch (start us, length us, event | category | flops | bytes accessed | tf_op | source)
XLA Modules:
  0.0 80.5 jit_solution(13294163043950724719)
XLA Ops:
  0.6 79.0 %shard_map.182 = (bf16[32,4096]{1,0:T(8,128)(2,1)S(1)}, bf16[8,16,512]{2,1,0:T(8,128)(2,1)S(1)}, bf16[8,16,384]{2,1,0:T(8,128)(2,1)S(1)}) custom-call(s32[16,64]{1,0:T(8,128)} %bitcast.3, bf16[32,4096]{1,0:T(8,128)(2,1)} %refs_1_.1, bf16[32,4096]{1,0:T(8,128)(2,1)} %refs_2_.1, bf16[9,32,128]{2,1,0:T(8,128)(2,1)} %refs_3_.1, bf16[4,32,128]{2,1,0:T(8,128)(2,1)} %refs_4_.1, ...), custom_call_target="tpu_custom_call" | custom-call | tf_op jit(solution)/shard_map/pallas_call | solution.py:740
  79.6 0.9 %shard_map.183 = (bf16[32,4096]{1,0:T(8,128)(2,1)}, f32[9,32,128]{2,1,0:T(8,128)}, f32[4,32,128]{2,1,0:T(8,128)}, f32[9,32,128]{2,1,0:T(8,128)}, f32[32,128]{1,0:T(8,128)}) custom-call(bf16[32,4096]{1,0:T(8,128)(2,1)S(1)} %get-tuple-element.8.out_in, bf16[8,16,512]{2,1,0:T(8,128)(2,1)S(1)} %get-tuple-element.9.final_a, ...), custom_call_target="tpu_custom_call" | custom-call | tf_op jit(solution)/shard_map/pallas_call | solution.py:770

commit v6 on v5

--- a/solution.py
+++ b/solution.py
@@ -130,36 +130,6 @@
     return 0.5 * (1.0 + t) + 0.5 * v * (1.0 - t * t) * (ROOT * (1.0 + 3 * 0.044715 * (v * v)))
 
 
-def place_of():
-    tile = lax.axis_index("tile")
-    return tile, tile // 8, lax.rem(tile, 8), lax.axis_index("chan")
-
-
-def x_peer(d):
-    tile, _, _, x = place_of()
-    return (tile, lax.rem(x + d, 4))
-
-
-def z_peer(d):
-    _, z, g, x = place_of()
-    return (lax.rem(z + d, 8) * 8 + g, x)
-
-
-def g_peer(d):
-    _, z, g, x = place_of()
-    return (z * 8 + lax.rem(g + d, 8), x)
-
-
-def core_peer():
-    tile, _, g, x = place_of()
-    return (tile + 1 - 2 * lax.rem(g, 2), x)
-
-
-def xy_peer(dx, dy):
-    _, z, g, x = place_of()
-    return (z * 8 + lax.rem(g + 2 * dy, 8), lax.rem(x + dx, 4))
-
-
 AW, BW = 2048, 1536
 XD = (2, 1, 3)
 ZD = (4, 3, 5, 2, 6, 1, 7)
@@ -189,9 +159,22 @@
 def level_kernel(*refs):
     names = INPUTS + ("out", "final_a", "final_b") + tuple(n for n, _ in SCRATCH)
     r = dict(zip(names, refs))
-    tile, z, g, x = place_of()
+    tile, x = lax.axis_index("tile"), lax.axis_index("chan")
+    z, g = tile // 8, lax.rem(tile, 8)
     y, core = g // 2, lax.rem(g, 2)
     q = x
+    xs = [x] + [lax.rem(x + d, 4) for d in range(1, 4)]
+    ys = [y] + [lax.rem(y + d, 4) for d in range(1, 4)]
+    zs = [z] + [lax.rem(z + d, 8) for d in range(1, 8)]
+    gs = [g] + [lax.rem(g + d, 8) for d in range(1, 8)]
+    x_at = [(tile, xs[d]) for d in range(4)]
+    z_at = [(zs[d] * 8 + g, x) for d in range(8)]
+    g_at = [(z * 8 + gs[d], x) for d in range(8)]
+    x_peer, z_peer, g_peer = x_at.__getitem__, z_at.__getitem__, g_at.__getitem__
+
+    def xy_peer(dx, dy):
+        return (g_at[2 * dy][0], xs[dx])
+
     mine = pl.ds(pl.multiple_of(x * 32, 32), 32)
     rounds = []
 
@@ -291,7 +274,7 @@
         whole = into.at[:, three, :] if n in (1, 2, 4) else into.at[three, :]
         m = begin(whole)
         for d in XD:
-            src, dst = piece(n, lax.rem(x + d, 4))
+            src, dst = piece(n, xs[d])
             push(m, src, dst, x_peer(d))
         src, dst = piece(n, x)
         bulk[n] = (m, local(10 + n, src, dst))
@@ -306,12 +289,22 @@
 
     own["adj"].wait()
 
-    def entry(t, k, h=0):
-        p = adj[2 * k, t]
-        s = lax.rem(adj[2 * k + 1, t] + TURNS[k], 4)
-        if h:
-            return jnp.logical_and(p >= 0, p // 8 == z), lax.rem(p, 8), s
-        return jnp.logical_and(p >= 0, lax.rem(p, 8) == g), p // 8, s
+    table = r["table"]
+    for n in range(8):
+        for k in range(8):
+            at = n * 8 + k
+            for h in range(2):
+                t = z * 8 + n if h == 0 else n * 8 + g
+                p = adj[2 * k, t]
+                s = lax.rem(adj[2 * k + 1, t] + TURNS[k], 4)
+                owned = jnp.logical_and(p >= 0, (p // 8 == z) if h else (lax.rem(p, 8) == g))
+                m = lax.rem(p, 8) if h else p // 8
+                table[h, at] = jnp.where(owned, m * 4 + s, -1)
+                if h == 0:
+                    table[2, at] = jnp.where(owned, m * 4 + lax.rem(k + 4 - s, 4), -1)
+                    table[3, at] = jnp.where(owned, m, -1)
+                    table[4, at] = s
+                    table[5, at] = n * 8 + (k // 4) * 4 + lax.rem(s + 4 - k % 4, 4)
 
     own["cmap"].wait()
     slots, landed = r["slots"], r["landed"]
@@ -324,11 +317,11 @@
         second.append(m)
         corners = [[] for _ in range(4)]
         for d in order:
-            t = z * 8 + lax.rem(g + d, 8) if h == 0 else lax.rem(z + d, 8) * 8 + g
+            t = (gs[d] if h == 0 else zs[d]) * 8
             for k in range(8):
-                owned, n, s = entry(t, k, h)
-                block = held[h][jnp.where(owned, n * 4 + s, 0)]
-                block = jnp.where(owned, block, jnp.zeros_like(block))
+                n = table[h, t + k]
+                block = held[h][jnp.maximum(n, 0)]
+                block = jnp.where(n >= 0, block, jnp.zeros_like(block))
                 if k < 4:
                     slots[h, d, :, k * 128:(k + 1) * 128] = block
                 else:
@@ -371,7 +364,7 @@
         pout[j, :, 0:128] = nt(total, r["v_fsel"][j]).astype(BF)
         pout[j, :, 128:256] = jnp.zeros((32, 128), BF) if ends[j] is None else ends[j]
     c_x = spread(
-        picked.at[pl.ds(0, 96), :], XD, x_peer, lambda d: pout.at[lax.rem(x + d, 4)], lambda d: picked.at[mine, :]
+        picked.at[pl.ds(0, 96), :], XD, x_peer, lambda d: pout.at[xs[d]], lambda d: picked.at[mine, :]
     )
     picked[mine, :] = pout[x]
     for n in (5, 4):
@@ -433,7 +426,7 @@
 
     x2in, halo = r["x2in"], r["halo"]
     c_x = spread(
-        x2in.at[pl.ds(1, 3)], XD, x_peer, lambda d: rq.at[rows_of(lax.rem(x + d, 4)), :], lambda d: x2in.at[d]
+        x2in.at[pl.ds(1, 3)], XD, x_peer, lambda d: rq.at[rows_of(xs[d]), :], lambda d: x2in.at[d]
     )
     c_h = begin(halo)
     push(c_h, r["act2"].at[pl.ds(224, 32), :], halo.at[0], x_peer(1))
@@ -477,12 +470,12 @@
     slots2, landed2 = r["slots2"], r["landed2"]
     c_g = begin(landed2.at[pl.ds(1, 7)])
     for d in GD + (0,):
-        t = z * 8 + lax.rem(g + d, 8)
+        t = gs[d] * 8
         both = [jnp.zeros((32, 128), F32), jnp.zeros((32, 128), F32)]
         for k in range(8):
-            owned, n, s = entry(t, k)
-            block = rolled[jnp.where(owned, n * 4 + lax.rem(k + 4 - s, 4), 0)].astype(F32)
-            block = jnp.where(owned, block, 0.0)
+            n = table[2, t + k]
+            block = rolled[jnp.maximum(n, 0)].astype(F32)
+            block = jnp.where(n >= 0, block, 0.0)
             if k < 4:
                 both[0] = jnp.where(lane // 32 == k, block, both[0])
             else:
@@ -536,7 +529,7 @@
     dq[...] = tn(cat, sel).astype(BF)
     x4in, hout, hin = r["x4in"], r["hout"], r["hin"]
     c_x = spread(
-        x4in.at[pl.ds(1, 3)], XD, x_peer, lambda d: dq.at[rows_of(lax.rem(x + d, 4)), :], lambda d: x4in.at[d]
+        x4in.at[pl.ds(1, 3)], XD, x_peer, lambda d: dq.at[rows_of(xs[d]), :], lambda d: x4in.at[d]
     )
     hout[0] = mid[288:320]
     hout[1] = mid[0:32]
@@ -557,7 +550,7 @@
                 at += width
             outs[n, :, at:wide] = jnp.zeros((16, wide - at), BF)
         n = begin(ins)
-        push(n, outs, ins, core_peer())
+        push(n, outs, ins, (tile + 1 - 2 * core, x))
         return n
 
     def shares(name, wide, parts):
@@ -575,7 +568,7 @@
                 outs[n, m] = summed[:, m * share:(m + 1) * share]
         m = begin(ins.at[pl.ds(1, 15)])
         for dx, dy in XYD:
-            push(m, outs.at[lax.rem(x + dx, 4), lax.rem(y + dy, 4)], ins.at[dx * 4 + dy], xy_peer(dx, dy))
+            push(m, outs.at[xs[dx], ys[dy]], ins.at[dx * 4 + dy], xy_peer(dx, dy))
         return m
 
     def along_z(name):
@@ -611,7 +604,7 @@
     lanes = pl.ds(pl.multiple_of(x * 1024, 1024), 1024)
     c_o = spread(
         out.at[:, pl.ds(0, 3072)], XD, x_peer,
-        lambda d: ostrip.at[rows_of(lax.rem(x + d, 4)), :], lambda d: out.at[:, lanes],
+        lambda d: ostrip.at[rows_of(xs[d]), :], lambda d: out.at[:, lanes],
     )
     own_out = local(16, ostrip.at[mine, :], out.at[:, lanes])
 
@@ -630,20 +623,20 @@
     sums = [jnp.zeros((32, 128), F32) for _ in range(8)]
     for j in range(8):
         for k in range(8):
-            owned, n, s = entry(z * 8 + j, k)
-            block = rolled3[j * 8 + (k // 4) * 4 + lax.rem(s + 4 - k % 4, 4)].astype(F32)
+            at = j * 8 + k
+            n, s = table[3, at], table[4, at]
+            block = rolled3[table[5, at]].astype(F32)
             if k < 4:
                 block = jnp.where(lane // 32 == s, block, 0.0)
             else:
                 block = jnp.where(lane == 32 * s + EDGE[k - 4], block, 0.0)
-            n = jnp.where(owned, n, -1)
             for m in range(8):
                 sums[m] = sums[m] + jnp.where(n == m, block, 0.0)
     slots3, landed3 = r["slots3"], r["landed3"]
     for n in range(8):
         slots3[n] = sums[n].astype(BF)
     c_z = spread(
-        landed3.at[pl.ds(1, 7)], ZD, z_peer, lambda d: slots3.at[lax.rem(z + d, 8)], lambda d: landed3.at[d]
+        landed3.at[pl.ds(1, 7)], ZD, z_peer, lambda d: slots3.at[zs[d]], lambda d: landed3.at[d]
     )
     settle(c_bc)
     c_b = shares("b", BW, parts_b)
@@ -711,6 +704,7 @@
 
 SCRATCH = [
     ("lsem", sems(17)), ("ss", sems(32)), ("rs", sems(32)), ("s_adj", pltpu.SMEM((16, 64), jnp.int32)),
+    ("table", pltpu.SMEM((6, 64), jnp.int32)),
     ("fv", buf(32, 4096)), ("v_pick", buf(1024, 128)), ("v_put", buf(4, 128, 256)), ("v_perm", buf(3, 128, 128)),
     ("v_cmap", buf(4, 128, 128)), ("v_fsel", buf(4, 128, 640)), ("v_place", buf(2, 1280, 128)),
     ("v_rout", buf(256, 128)), ("v_rin", buf(960, 256)),

time: 80.6 us -> 80.6 us (level)
  no operation moved by 1% of the time
where the time goes in v6:
time: 80.6 us; the launch traced here: 80.5 us
  Pallas kernels  79.9 us (99%)
    pallas_call x1, Pallas kernels, level_call(): pl.pallas_call(level_kernel, out_shape=(pltpu.VMEM((32, 4096), BF), pltpu...  79 us

profile of v6, /device:TPU:1, one launch (start us, length us, event | category | flops | bytes accessed | tf_op | source)
XLA Modules:
  0.0 80.5 jit_solution(12886281828695292255)
XLA Ops:
  0.6 79.0 %shard_map.182 = (bf16[32,4096]{1,0:T(8,128)(2,1)S(1)}, bf16[8,16,512]{2,1,0:T(8,128)(2,1)S(1)}, bf16[8,16,384]{2,1,0:T(8,128)(2,1)S(1)}) custom-call(s32[16,64]{1,0:T(8,128)} %bitcast.3, bf16[32,4096]{1,0:T(8,128)(2,1)} %refs_1_.1, bf16[32,4096]{1,0:T(8,128)(2,1)} %refs_2_.1, bf16[9,32,128]{2,1,0:T(8,128)(2,1)} %refs_3_.1, bf16[4,32,128]{2,1,0:T(8,128)(2,1)} %refs_4_.1, ...), custom_call_target="tpu_custom_call" | custom-call | tf_op jit(solution)/shard_map/pallas_call | solution.py:734
  79.7 0.9 %shard_map.183 = (bf16[32,4096]{1,0:T(8,128)(2,1)}, f32[9,32,128]{2,1,0:T(8,128)}, f32[4,32,128]{2,1,0:T(8,128)}, f32[9,32,128]{2,1,0:T(8,128)}, f32[32,128]{1,0:T(8,128)}) custom-call(bf16[32,4096]{1,0:T(8,128)(2,1)S(1)} %get-tuple-element.8.out_in, bf16[8,16,512]{2,1,0:T(8,128)(2,1)S(1)} %get-tuple-element.9.final_a, ...), custom_call_target="tpu_custom_call" | custom-call | tf_op jit(solution)/shard_map/pallas_call | solution.py:764

commit v7 on v6

--- a/solution.py
+++ b/solution.py
@@ -1,4 +1,5 @@
 import functools
+import math
 
 import jax
 import jax.numpy as jnp
@@ -176,15 +177,16 @@
         return (g_at[2 * dy][0], xs[dx])
 
     mine = pl.ds(pl.multiple_of(x * 32, 32), 32)
-    rounds = []
+    rounds, sent = [], []
 
     def rows_of(n):
         return pl.ds(pl.multiple_of(n * 32, 32), 32)
 
-    def local(n, src, dst):
-        copy = pltpu.make_async_copy(src, dst, r["lsem"].at[n])
-        copy.start()
-        return copy
+    def local(sem, src, dst):
+        pltpu.make_async_copy(src, dst, sem).start()
+
+    def wait(whole, sem):
+        pltpu.make_async_copy(whole, whole, sem).wait()
 
     def begin(whole):
         rounds.append(whole)
@@ -192,9 +194,10 @@
 
     def push(n, src, dst, peer):
         pltpu.make_async_remote_copy(
-            src_ref=src, dst_ref=dst, send_sem=r["ss"].at[n], recv_sem=r["rs"].at[n],
+            src_ref=src, dst_ref=dst, send_sem=r["ss"], recv_sem=r["rs"].at[n],
             device_id=peer, device_id_type=MESH,
         ).start()
+        sent.append(math.prod(src.shape) * src.dtype.itemsize)
 
     def spread(whole, dirs, peer, src, dst):
         n = begin(whole)
@@ -203,25 +206,21 @@
         return n
 
     def settle(n):
-        pltpu.make_async_copy(rounds[n], rounds[n], r["rs"].at[n]).wait()
-
+        wait(rounds[n], r["rs"].at[n])
+
+    early = (("feat", "fv"), ("pick", "v_pick"), ("put", "v_put"))
+    for src, dst in early:
+        local(r["lsem"].at[0], r[src], r[dst])
+    local(r["lsem"].at[1], r["adj"], r["s_adj"])
     barrier = pltpu.get_barrier_semaphore()
     peers = [x_peer(d) for d in XD] + [z_peer(d) for d in ZD] + [g_peer(d) for d in GD]
     peers += [xy_peer(dx, dy) for dx, dy in XYD if dx and dy]
     for peer in peers:
         pl.semaphore_signal(barrier, inc=1, device_id=peer, device_id_type=MESH)
 
-    own_feat = local(0, r["feat"], r["fv"])
-    own = {
-        "pick": local(1, r["pick"], r["v_pick"]),
-        "put": local(2, r["put"], r["v_put"]),
-        "adj": local(3, r["adj"], r["s_adj"]),
-    }
     adj = r["s_adj"]
 
-    own["pick"].wait()
-    own["put"].wait()
-    own_feat.wait()
+    wait(r["early"], r["lsem"].at[0])
     fv, held = r["fv"], (r["held0"], r["held1"])
     stacked = jnp.concatenate([fv[:, s * 1024:(s + 1) * 1024] for s in range(4)], axis=0)
     cols = nn(stacked, r["v_pick"][...]).astype(BF)
@@ -246,14 +245,10 @@
         part = held[h].at[pl.ds(at * 4, 4)]
         first.append(spread(held[h].at[pl.ds(0, 28)], dirs, peer, lambda d: part, lambda d: part))
 
-    own.update({
-        "cmap": local(4, r["cmap"], r["v_cmap"]),
-        "perm": local(5, r["perm"], r["v_perm"]),
-        "fsel": local(6, r["fsel"], r["v_fsel"]),
-        "place": local(7, r["place"], r["v_place"]),
-        "rout": local(8, r["rout"].at[q], r["v_rout"]),
-        "rin": local(9, r["rin"].at[q], r["v_rin"]),
-    })
+    for name in ("cmap", "perm", "fsel", "place"):
+        local(r["lsem"].at[2], r[name], r["v_" + name])
+    for name in ("rout", "rin"):
+        local(r["lsem"].at[2], r[name].at[q], r["v_" + name])
 
     def piece(n, j):
         if n == 0:
@@ -269,25 +264,21 @@
     bulk = {}
 
     def send_bulk(n):
-        three = pl.ds(0, 96)
-        into = r[("strip", "v_w1", "v_wd", "og", "v_w2", "v_up")[n]]
-        whole = into.at[:, three, :] if n in (1, 2, 4) else into.at[three, :]
-        m = begin(whole)
+        m = begin(r[("strip", "v_w1", "v_wd", "og", "v_w2", "v_up")[n]])
         for d in XD:
             src, dst = piece(n, xs[d])
             push(m, src, dst, x_peer(d))
         src, dst = piece(n, x)
-        bulk[n] = (m, local(10 + n, src, dst))
+        local(r["rs"].at[m], src, dst)
+        bulk[n] = m
 
     def take_bulk(n):
-        m, copy = bulk[n]
-        copy.wait()
-        settle(m)
+        settle(bulk[n])
 
     for n in range(4):
         send_bulk(n)
 
-    own["adj"].wait()
+    wait(r["s_adj"], r["lsem"].at[1])
 
     table = r["table"]
     for n in range(8):
@@ -306,7 +297,7 @@
                     table[4, at] = s
                     table[5, at] = n * 8 + (k // 4) * 4 + lax.rem(s + 4 - k % 4, 4)
 
-    own["cmap"].wait()
+    wait(r["late"], r["lsem"].at[2])
     slots, landed = r["slots"], r["landed"]
     second = []
     for h in (1, 0):
@@ -333,7 +324,6 @@
             slots[h, d, :, 512:640] = corner[16 * n:16 * n + 16].astype(BF)
             if d:
                 push(m, slots.at[h, d], landed.at[h, d], peer(d))
-    own["perm"].wait()
     take_bulk(0)
     perm, cb, strip = r["v_perm"], r["cb"], r["strip"]
     perms = perm[...].reshape(384, 128)
@@ -357,7 +347,6 @@
         halves_of.append(total)
     total = jnp.concatenate([halves_of[1], halves_of[0]], axis=0).astype(BF)
 
-    own["fsel"].wait()
     picked, pout = r["picked"], r["pout"]
     ends = (total[:, 0:128], None, None, nn(total[:, 256:384], flip).astype(BF))
     for j in range(4):
@@ -369,7 +358,6 @@
     picked[mine, :] = pout[x]
     for n in (5, 4):
         send_bulk(n)
-    own["place"].wait()
     take_bulk(1)
     take_bulk(2)
     w1c = side_by_side(r["v_w1"], 9)
@@ -420,7 +408,6 @@
     r["z2"][...] = pre
     act2 = gelu(pre).astype(BF)
     r["act2"][...] = act2
-    own["rout"].wait()
     rq = r["rq"]
     rq[...] = tn(act2, r["v_rout"][...]).astype(BF)
 
@@ -492,7 +479,6 @@
     picked2[mine, :] = total.astype(BF)
     part2 = picked2.at[mine, :]
     c_x = spread(picked2.at[pl.ds(0, 96), :], XD, x_peer, lambda d: part2, lambda d: part2)
-    own["rin"].wait()
     take_bulk(4)
     settle(c_h)
     settle(c_x)
@@ -603,10 +589,10 @@
     c_g = spread(held3.at[pl.ds(0, 7)], GD, g_peer, lambda d: held3.at[g], lambda d: held3.at[g])
     lanes = pl.ds(pl.multiple_of(x * 1024, 1024), 1024)
     c_o = spread(
-        out.at[:, pl.ds(0, 3072)], XD, x_peer,
+        out, XD, x_peer,
         lambda d: ostrip.at[rows_of(xs[d]), :], lambda d: out.at[:, lanes],
     )
-    own_out = local(16, ostrip.at[mine, :], out.at[:, lanes])
+    local(r["rs"].at[c_o], ostrip.at[mine, :], out.at[:, lanes])
 
     r["gb_u"][...] = tn(pooled, coarse)
     r["gb_w"][...] = tn(gz3, taps2)
@@ -683,9 +669,8 @@
     settle(c_bg)
     settle(c_o)
     settle(to_row("a", c_az))
-    own_out.wait()
-    for n, whole in enumerate(rounds):
-        pltpu.make_async_copy(whole, whole, r["ss"].at[n]).wait()
+    assert sum(sent) == 256 * SENT, sum(sent) // 256
+    wait(r["drain"], r["ss"])
 
 
 INPUTS = (
@@ -702,8 +687,10 @@
     return pltpu.SemaphoreType.DMA(shape)
 
 
+SENT = 14064
 SCRATCH = [
-    ("lsem", sems(17)), ("ss", sems(32)), ("rs", sems(32)), ("s_adj", pltpu.SMEM((16, 64), jnp.int32)),
+    ("early", buf(3072, 128)), ("late", buf(8192, 128)), ("drain", buf(SENT, 128)),
+    ("lsem", sems(3)), ("ss", pltpu.SemaphoreType.DMA), ("rs", sems(30)), ("s_adj", pltpu.SMEM((16, 64), jnp.int32)),
     ("table", pltpu.SMEM((6, 64), jnp.int32)),
     ("fv", buf(32, 4096)), ("v_pick", buf(1024, 128)), ("v_put", buf(4, 128, 256)), ("v_perm", buf(3, 128, 128)),
     ("v_cmap", buf(4, 128, 128)), ("v_fsel", buf(4, 128, 640)), ("v_place", buf(2, 1280, 128)),

time: 80.6 us -> 80.3 us (level)
  no operation moved by 1% of the time
where the time goes in v7:
time: 80.3 us; the launch traced here: 80.2 us
  Pallas kernels  79.5 us (99%)
    pallas_call x1, Pallas kernels, level_call(): pl.pallas_call(level_kernel, out_shape=(pltpu.VMEM((32, 4096), BF), pltpu...  78.7 us

profile of v7, /device:TPU:1, one launch (start us, length us, event | category | flops | bytes accessed | tf_op | source)
XLA Modules:
  0.0 80.2 jit_solution(6944873037312254609)
XLA Ops:
  0.6 78.7 %shard_map.182 = (bf16[32,4096]{1,0:T(8,128)(2,1)S(1)}, bf16[8,16,512]{2,1,0:T(8,128)(2,1)S(1)}, bf16[8,16,384]{2,1,0:T(8,128)(2,1)S(1)}) custom-call(s32[16,64]{1,0:T(8,128)} %bitcast.3, bf16[32,4096]{1,0:T(8,128)(2,1)} %refs_1_.1, bf16[32,4096]{1,0:T(8,128)(2,1)} %refs_2_.1, bf16[9,32,128]{2,1,0:T(8,128)(2,1)} %refs_3_.1, bf16[4,32,128]{2,1,0:T(8,128)(2,1)} %refs_4_.1, ...), custom_call_target="tpu_custom_call" | custom-call | tf_op jit(solution)/shard_map/pallas_call | solution.py:721
  79.3 0.9 %shard_map.183 = (bf16[32,4096]{1,0:T(8,128)(2,1)}, f32[9,32,128]{2,1,0:T(8,128)}, f32[4,32,128]{2,1,0:T(8,128)}, f32[9,32,128]{2,1,0:T(8,128)}, f32[32,128]{1,0:T(8,128)}) custom-call(bf16[32,4096]{1,0:T(8,128)(2,1)S(1)} %get-tuple-element.8.out_in, bf16[8,16,512]{2,1,0:T(8,128)(2,1)S(1)} %get-tuple-element.9.final_a, ...), custom_call_target="tpu_custom_call" | custom-call | tf_op jit(solution)/shard_map/pallas_call | solution.py:751

commit v8 on v7

--- a/solution.py
+++ b/solution.py
@@ -259,12 +259,13 @@
         if n == 5:
             return r["up"], r["v_up"].at[mine, :]
         name = {1: "w1", 2: "wd", 4: "w2"}[n]
-        return r[name], r["v_" + name].at[:, mine, :]
+        return r[name].at[:, core], r["v_" + name].at[:, x, core]
 
     bulk = {}
 
     def send_bulk(n):
-        m = begin(r[("strip", "v_w1", "v_wd", "og", "v_w2", "v_up")[n]])
+        into = r[("strip", "v_w1", "v_wd", "og", "v_w2", "v_up")[n]]
+        m = begin(into.at[:, :, 0] if n in (1, 2, 4) else into)
         for d in XD:
             src, dst = piece(n, xs[d])
             push(m, src, dst, x_peer(d))
@@ -272,10 +273,16 @@
         local(r["rs"].at[m], src, dst)
         bulk[n] = m
 
+    def share_bulk(n):
+        settle(bulk[n])
+        into = r[{1: "v_w1", 2: "v_wd", 4: "v_w2"}[n]]
+        bulk[n] = begin(into.at[:, :, 0])
+        push(bulk[n], into.at[:, :, core], into.at[:, :, core], (tile + 1 - 2 * core, x))
+
     def take_bulk(n):
         settle(bulk[n])
 
-    for n in range(4):
+    for n in range(6):
         send_bulk(n)
 
     wait(r["s_adj"], r["lsem"].at[1])
@@ -338,6 +345,8 @@
         for b in range(3):
             cb[b, n * 128:(n + 1) * 128, :] = turned[b * 128:(b + 1) * 128].astype(BF)
 
+    share_bulk(1)
+    share_bulk(2)
     halves_of = []
     for m, h in zip(second, (1, 0)):
         settle(m)
@@ -356,18 +365,16 @@
         picked.at[pl.ds(0, 96), :], XD, x_peer, lambda d: pout.at[xs[d]], lambda d: picked.at[mine, :]
     )
     picked[mine, :] = pout[x]
-    for n in (5, 4):
-        send_bulk(n)
     take_bulk(1)
     take_bulk(2)
-    w1c = side_by_side(r["v_w1"], 9)
+    w1 = r["v_w1"][...].reshape(9, 128, 128)
+    w1c = side_by_side(w1, 9)
     for n in (0, 9):
         block = strip_block(n)
         turned = nt(perms, jnp.where(q == n // 3, jnp.zeros_like(block), block))
         for b in range(3):
             cb[b, n * 128:(n + 1) * 128, :] = turned[b * 128:(b + 1) * 128].astype(BF)
     z1, act1 = r["z1"], r["act1"]
-    w1 = r["v_w1"]
 
     def fine_taps(n):
         return jnp.concatenate(
@@ -404,7 +411,7 @@
             pre = pre + jnp.where(q == (0 if n == 0 else 3), ends, 0.0)
         z1[rows, :] = pre
         act1[rows, :] = gelu(pre).astype(BF)
-    pre = nt(quarters(act1[...]), side_by_side(r["v_wd"], 4))
+    pre = nt(quarters(act1[...]), side_by_side(r["v_wd"][...].reshape(4, 128, 128), 4))
     r["z2"][...] = pre
     act2 = gelu(pre).astype(BF)
     r["act2"][...] = act2
@@ -428,6 +435,7 @@
 
     take_bulk(3)
     take_bulk(5)
+    share_bulk(4)
     og, ogt, up = r["og"], r["ogt"], r["v_up"]
     flat = perm[1]
     for n in range(8):
@@ -493,7 +501,7 @@
     east = jnp.where(col == 31, 0.0, pltpu.roll(rows, 319, 0)) + rim[640:960]
     blocks = [v.astype(BF) for v in (west, rows, east)]
     taps2 = jnp.concatenate([blocks[b][a * 32:a * 32 + 256] for a in range(3) for b in range(3)], axis=1)
-    w2 = r["v_w2"]
+    w2 = r["v_w2"][...].reshape(9, 128, 128)
     pre = nt(taps2, side_by_side(w2, 9))
     gz3 = (gelu_slope(pre) * back_up).astype(BF)
     none32, none64 = jnp.zeros((32, 128), F32), jnp.zeros((64, 128), F32)
@@ -644,7 +652,7 @@
     settle(c_x)
 
     gz2 = (slope2 * (ga2 + nt(r["v_rout"][...], back_rim[...]))).astype(BF)
-    wd = r["v_wd"]
+    wd = r["v_wd"][...].reshape(4, 128, 128)
     fine = [nn(gz2, wd[t]).reshape(8, 1, 32, 128) for t in range(4)]
     grown = jnp.concatenate(fine, axis=1).reshape(1024, 128)
     gz1 = (r["direct"][...] + r["slope"][...] * grown).astype(BF)
@@ -661,14 +669,15 @@
         final[g] = whole(name)
         return spread(final.at[pl.ds(0, 7)], GD, g_peer, lambda d: final.at[g], lambda d: final.at[g])
 
-    c_bg = to_row("b", c_bz)
     settle(c_ac)
     c_a = shares("a", AW, parts_a)
     settle(c_a)
     c_az = along_z("a")
+    c_bg = to_row("b", c_bz)
+    settle(c_o)
+    c_ag = to_row("a", c_az)
     settle(c_bg)
-    settle(c_o)
-    settle(to_row("a", c_az))
+    settle(c_ag)
     assert sum(sent) == 256 * SENT, sum(sent) // 256
     wait(r["drain"], r["ss"])
 
@@ -687,16 +696,16 @@
     return pltpu.SemaphoreType.DMA(shape)
 
 
-SENT = 14064
+SENT = 14416
 SCRATCH = [
     ("early", buf(3072, 128)), ("late", buf(8192, 128)), ("drain", buf(SENT, 128)),
-    ("lsem", sems(3)), ("ss", pltpu.SemaphoreType.DMA), ("rs", sems(30)), ("s_adj", pltpu.SMEM((16, 64), jnp.int32)),
+    ("lsem", sems(3)), ("ss", pltpu.SemaphoreType.DMA), ("rs", sems(33)), ("s_adj", pltpu.SMEM((16, 64), jnp.int32)),
     ("table", pltpu.SMEM((6, 64), jnp.int32)),
     ("fv", buf(32, 4096)), ("v_pick", buf(1024, 128)), ("v_put", buf(4, 128, 256)), ("v_perm", buf(3, 128, 128)),
     ("v_cmap", buf(4, 128, 128)), ("v_fsel", buf(4, 128, 640)), ("v_place", buf(2, 1280, 128)),
     ("v_rout", buf(256, 128)), ("v_rin", buf(960, 256)),
-    ("strip", buf(128, 1280)), ("og", buf(128, 1024)), ("v_w1", buf(9, 128, 128)), ("v_wd", buf(4, 128, 128)),
-    ("v_w2", buf(9, 128, 128)), ("v_up", buf(128, 128)),
+    ("strip", buf(128, 1280)), ("og", buf(128, 1024)), ("v_w1", buf(9, 4, 2, 16, 128)), ("v_wd", buf(4, 4, 2, 16, 128)),
+    ("v_w2", buf(9, 4, 2, 16, 128)), ("v_up", buf(128, 128)),
     ("held0", buf(32, 16, 128)), ("held1", buf(32, 16, 128)), ("slots", buf(2, 8, 16, 640)), ("landed", buf(2, 8, 16, 640)),
     ("pout", buf(4, 32, 256)), ("picked", buf(128, 256)),
     ("cb", buf(3, 1280, 128)), ("z1", buf(1024, 128, kind=F32)), ("act1", buf(1024, 128)),
@@ -771,7 +780,9 @@
         for m in (pick, put, fine_perm(), corner_maps(), fine_sel, fine_place, coarse_rim_out(), coarse_rim_in())
     ]
     out, final_a, final_b = level_call(
-        adjacency.transpose(1, 2, 0).reshape(16, 64), features, out_grad, conv1_weight, down_weight, conv2_weight, up_weight, *maps
+        adjacency.transpose(1, 2, 0).reshape(16, 64), features, out_grad,
+        conv1_weight.reshape(9, 2, 16, 128), down_weight.reshape(4, 2, 16, 128), conv2_weight.reshape(9, 2, 16, 128),
+        up_weight, *maps
     )
     return result_call(out, final_a, final_b, 262144 ** -0.5)
 

time: 80.3 us -> 78.1 us (0.973)
  Pallas kernels: 79.5 us -> 77.4 us
    pallas_call x1, Pallas kernels: 78.7 us -> 76.5 us  [level_call(): pl.pallas_call(level_kernel, out_shape=(pltpu.VMEM((32, 4096), BF), pltpu...]
where the time goes in v8:
time: 78.1 us; the launch traced here: 78 us
  Pallas kernels  77.4 us (99%)
    pallas_call x1, Pallas kernels, level_call(): pl.pallas_call(level_kernel, out_shape=(pltpu.VMEM((32, 4096), BF), pltpu...  76.5 us

profile of v8, /device:TPU:1, one launch (start us, length us, event | category | flops | bytes accessed | tf_op | source)
XLA Modules:
  0.0 78.0 jit_solution(15235860363374188526)
XLA Ops:
  0.6 76.5 %shard_map.182 = (bf16[32,4096]{1,0:T(8,128)(2,1)S(1)}, bf16[8,16,512]{2,1,0:T(8,128)(2,1)S(1)}, bf16[8,16,384]{2,1,0:T(8,128)(2,1)S(1)}) custom-call(s32[16,64]{1,0:T(8,128)} %bitcast.9, bf16[32,4096]{1,0:T(8,128)(2,1)} %refs_1_.1, bf16[32,4096]{1,0:T(8,128)(2,1)} %refs_2_.1, bf16[9,2,16,128]{3,2,1,0:T(8,128)(2,1)} %bitcast.6, ...), custom_call_target="tpu_custom_call" | custom-call | tf_op jit(solution)/shard_map/pallas_call | solution.py:730
  77.2 0.9 %shard_map.183 = (bf16[32,4096]{1,0:T(8,128)(2,1)}, f32[9,32,128]{2,1,0:T(8,128)}, f32[4,32,128]{2,1,0:T(8,128)}, f32[9,32,128]{2,1,0:T(8,128)}, f32[32,128]{1,0:T(8,128)}) custom-call(bf16[32,4096]{1,0:T(8,128)(2,1)S(1)} %get-tuple-element.8.out_in, bf16[8,16,512]{2,1,0:T(8,128)(2,1)S(1)} %get-tuple-element.9.final_a, ...), custom_call_target="tpu_custom_call" | custom-call | tf_op jit(solution)/shard_map/pallas_call | solution.py:760

commit v9 on v8

--- a/solution.py
+++ b/solution.py
@@ -88,6 +88,18 @@
     return out
 
 
+def strip_rims():
+    out = np.zeros((4, 48, 256), np.float32)
+    for q in range(4):
+        for r in range(8):
+            out[q, r, r * 32] = 1
+            out[q, 8 + r, r * 32 + 31] = 1
+    for k in range(32):
+        out[0, 16 + k, k] = 1
+        out[3, 16 + k, 7 * 32 + k] = 1
+    return out
+
+
 def coarse_rim_in():
     out = np.zeros((4, 960, 256), np.float32)
     for k in range(32):
@@ -136,6 +148,10 @@
 ZD = (4, 3, 5, 2, 6, 1, 7)
 GD = (4, 3, 5, 2, 6, 1, 7)
 FAR = (2, 1, 3, 0)
+GXD = sorted(
+    ((dg, dx) for dg in range(8) for dx in range(4) if dg or dx),
+    key=lambda d: -(min(d[0], 8 - d[0]) / 2 + min(d[1], 4 - d[1])),
+)
 XYD = [(dx, dy) for dx in FAR for dy in FAR if dx or dy]
 EDGE = (0, 31, 0, 31)
 
@@ -177,6 +193,9 @@
         return (g_at[2 * dy][0], xs[dx])
 
     mine = pl.ds(pl.multiple_of(x * 32, 32), 32)
+    def gx_peer(dg, dx):
+        return (g_at[dg][0], xs[dx])
+
     rounds, sent = [], []
 
     def rows_of(n):
@@ -214,7 +233,7 @@
     local(r["lsem"].at[1], r["adj"], r["s_adj"])
     barrier = pltpu.get_barrier_semaphore()
     peers = [x_peer(d) for d in XD] + [z_peer(d) for d in ZD] + [g_peer(d) for d in GD]
-    peers += [xy_peer(dx, dy) for dx, dy in XYD if dx and dy]
+    peers += [gx_peer(dg, dx) for dg, dx in GXD if dg and dx]
     for peer in peers:
         pl.semaphore_signal(barrier, inc=1, device_id=peer, device_id_type=MESH)
 
@@ -247,7 +266,7 @@
 
     for name in ("cmap", "perm", "fsel", "place"):
         local(r["lsem"].at[2], r[name], r["v_" + name])
-    for name in ("rout", "rin"):
+    for name in ("rout", "rin", "src"):
         local(r["lsem"].at[2], r[name].at[q], r["v_" + name])
 
     def piece(n, j):
@@ -299,7 +318,6 @@
                 m = lax.rem(p, 8) if h else p // 8
                 table[h, at] = jnp.where(owned, m * 4 + s, -1)
                 if h == 0:
-                    table[2, at] = jnp.where(owned, m * 4 + lax.rem(k + 4 - s, 4), -1)
                     table[3, at] = jnp.where(owned, m, -1)
                     table[4, at] = s
                     table[5, at] = n * 8 + (k // 4) * 4 + lax.rem(s + 4 - k % 4, 4)
@@ -347,6 +365,36 @@
 
     share_bulk(1)
     share_bulk(2)
+
+    spot = lax.broadcasted_iota(jnp.int32, (64, 128), 0)
+    lane = lax.broadcasted_iota(jnp.int32, (64, 128), 1)
+    in_west, in_side = spot < 16, spot < 32
+    step = jnp.where(in_west, spot, spot - 16)
+    for dg, dx in GXD + [(0, 0)]:
+        at, xd = gs[dg] * 8, xs[dx]
+        row = step + (8 * xd - 1)
+        above, below = jnp.logical_and(in_side, row < 0), jnp.logical_and(in_side, row > 31)
+
+        def by_spot(kind):
+            v = [table[kind, at + k] for k in range(8)]
+            end = jnp.where(xd == 0, v[0], v[2])
+            side = jnp.where(in_west, v[3], jnp.where(in_side, v[1], end))
+            side = jnp.where(above, jnp.where(in_west, v[7], v[4]), side)
+            return jnp.where(below, jnp.where(in_west, v[6], v[5]), side)
+
+        of, turn = by_spot(3), by_spot(4)
+        cell = jnp.where(in_west, 31 - row, jnp.where(in_side, row, jnp.where(xd == 0, spot - 32, 63 - spot)))
+        cell = jnp.where(above, jnp.where(in_west, 31, 0), cell)
+        cell = jnp.where(below, jnp.where(in_west, 0, 31), cell)
+        cell = jnp.where(turn <= 1, cell, 31 - cell)
+        odd = jnp.logical_or(turn == 1, turn == 3)
+        here = jnp.where(odd, jnp.logical_and(cell >= 8 * q, cell < 8 * q + 8).astype(jnp.int32),
+                         jnp.where(turn == 0, jnp.where(q == 3, 1, 0), jnp.where(q == 0, 1, 0)))
+        source = jnp.where(odd, cell - 8 * q + jnp.where(turn == 3, 8, 0), cell + 16)
+        source = jnp.where(jnp.logical_and(of >= 0, here == 1), of * 48 + source, -1)
+        for c in range(3):
+            r["picks"][dg * 4 + dx, :, c * 128:(c + 1) * 128] = jnp.where(source == lane + 128 * c, 1.0, 0.0).astype(BF)
+
     halves_of = []
     for m, h in zip(second, (1, 0)):
         settle(m)
@@ -415,23 +463,14 @@
     r["z2"][...] = pre
     act2 = gelu(pre).astype(BF)
     r["act2"][...] = act2
-    rq = r["rq"]
-    rq[...] = tn(act2, r["v_rout"][...]).astype(BF)
-
-    x2in, halo = r["x2in"], r["halo"]
-    c_x = spread(
-        x2in.at[pl.ds(1, 3)], XD, x_peer, lambda d: rq.at[rows_of(xs[d]), :], lambda d: x2in.at[d]
-    )
+    held2 = r["held2"]
+    held2[z] = nn(r["v_src"][...], act2).astype(BF)
+
+    c_z = spread(held2.at[pl.ds(0, 7)], ZD, z_peer, lambda d: held2.at[z], lambda d: held2.at[z])
+    halo = r["halo"]
     c_h = begin(halo)
     push(c_h, r["act2"].at[pl.ds(224, 32), :], halo.at[0], x_peer(1))
     push(c_h, r["act2"].at[pl.ds(0, 32), :], halo.at[1], x_peer(3))
-    total = rq[mine, :].astype(F32)
-    settle(c_x)
-    for d in XD:
-        total = total + x2in[d].astype(F32)
-    held2 = r["held2"]
-    held2[z] = total.astype(BF)
-    c_z = spread(held2.at[pl.ds(0, 7)], ZD, z_peer, lambda d: held2.at[z], lambda d: held2.at[z])
 
     take_bulk(3)
     take_bulk(5)
@@ -455,50 +494,64 @@
     r["direct"][...] = slope * ogt[...].astype(F32)
 
     settle(c_z)
-    rolled = r["rolled"]
-    for n in range(8):
-        block = held2[n].astype(F32)
-        rolled[n * 4] = held2[n]
-        for m in range(1, 4):
-            rolled[n * 4 + m] = pltpu.roll(block, 32 * m, 1).astype(BF)
     lane = lax.broadcasted_iota(jnp.int32, (32, 128), 1)
-    slots2, landed2 = r["slots2"], r["landed2"]
-    c_g = begin(landed2.at[pl.ds(1, 7)])
-    for d in GD + (0,):
-        t = gs[d] * 8
-        both = [jnp.zeros((32, 128), F32), jnp.zeros((32, 128), F32)]
-        for k in range(8):
-            n = table[2, t + k]
-            block = rolled[jnp.maximum(n, 0)].astype(F32)
-            block = jnp.where(n >= 0, block, 0.0)
-            if k < 4:
-                both[0] = jnp.where(lane // 32 == k, block, both[0])
-            else:
-                both[1] = jnp.where(lane == 32 * (k - 4) + EDGE[k - 4], block, both[1])
-        slots2[d, :, 0:128] = both[0].astype(BF)
-        slots2[d, :, 128:256] = both[1].astype(BF)
+    slots2, landed2, picks = r["slots2"], r["landed2"], r["picks"]
+    every = jnp.concatenate([held2[n] for n in range(8)], axis=0)
+    c_g = begin(landed2)
+
+    def at_end(n):
+        return jnp.logical_or(n == 0, n == 3)
+
+    for dg, dx in GXD + [(0, 0)]:
+        d = dg * 4 + dx
+        slots2[d] = nn(picks[d], every).astype(BF)
         if d:
-            push(c_g, slots2.at[d], landed2.at[d], g_peer(d))
-    settle(c_g)
-    total = slots2[0].astype(F32)
-    for d in range(1, 8):
-        total = total + landed2[d].astype(F32)
-    picked2 = r["picked2"]
-    picked2[mine, :] = total.astype(BF)
-    part2 = picked2.at[mine, :]
-    c_x = spread(picked2.at[pl.ds(0, 96), :], XD, x_peer, lambda d: part2, lambda d: part2)
+            for size, ok in ((64, at_end(xs[dx])), (32, jnp.logical_not(at_end(xs[dx])))):
+
+                @pl.when(ok)
+                def _():
+                    some = pl.ds(0, size)
+                    pltpu.make_async_remote_copy(
+                        src_ref=slots2.at[d, some], dst_ref=landed2.at[d, some],
+                        send_sem=r["ss2"], recv_sem=r["rs"].at[c_g],
+                        device_id=gx_peer(dg, dx), device_id_type=MESH,
+                    ).start()
+
+    @pl.when(at_end(x))
+    def _():
+        wait(landed2.at[pl.ds(1, 31)], r["rs"].at[c_g])
+
+    @pl.when(jnp.logical_not(at_end(x)))
+    def _():
+        wait(landed2.at[pl.ds(1, 31), pl.ds(0, 32)], r["rs"].at[c_g])
+
+    total = slots2[0, 0:32, :].astype(F32)
+    for d in range(1, 32):
+        total = total + landed2[d, 0:32, :].astype(F32)
+    beyond = r["beyond"]
+    beyond[...] = jnp.zeros((32, 128), F32)
+
+    @pl.when(at_end(x))
+    def _():
+        row = slots2[0, 32:64, :].astype(F32)
+        for d in range(1, 32):
+            row = row + landed2[d, 32:64, :].astype(F32)
+        beyond[...] = row
+
     take_bulk(4)
     settle(c_h)
-    settle(c_x)
 
     sel = r["v_rin"][...]
-    rim = nt(sel, picked2[...])
-    upper = jnp.where(q == 0, 0.0, halo[0].astype(F32))
-    lower = jnp.where(q == 3, 0.0, halo[1].astype(F32))
-    rows = jnp.concatenate([upper, act2.astype(F32), lower], axis=0) + rim[0:320]
+    upper = jnp.where(q == 0, beyond[...], halo[0].astype(F32))
+    lower = jnp.where(q == 3, beyond[...], halo[1].astype(F32))
+    rows = jnp.concatenate([upper, act2.astype(F32), lower], axis=0)
     col = lax.rem(lax.broadcasted_iota(jnp.int32, (320, 128), 0), 32)
-    west = jnp.where(col == 0, 0.0, pltpu.roll(rows, 1, 0)) + rim[320:640]
-    east = jnp.where(col == 31, 0.0, pltpu.roll(rows, 319, 0)) + rim[640:960]
+
+    def along(first):
+        return jnp.concatenate([jnp.broadcast_to(total[n:n + 1], (32, 128)) for n in range(first, first + 10)], axis=0)
+
+    west = jnp.where(col == 0, along(0), pltpu.roll(rows, 1, 0))
+    east = jnp.where(col == 31, along(16), pltpu.roll(rows, 319, 0))
     blocks = [v.astype(BF) for v in (west, rows, east)]
     taps2 = jnp.concatenate([blocks[b][a * 32:a * 32 + 256] for a in range(3) for b in range(3)], axis=1)
     w2 = r["v_w2"][...].reshape(9, 128, 128)
@@ -681,10 +734,18 @@
     assert sum(sent) == 256 * SENT, sum(sent) // 256
     wait(r["drain"], r["ss"])
 
+    @pl.when(at_end(x))
+    def _():
+        wait(r["drain"].at[pl.ds(0, 15 * 64 + 16 * 32)], r["ss2"])
+
+    @pl.when(jnp.logical_not(at_end(x)))
+    def _():
+        wait(r["drain"].at[pl.ds(0, 16 * 64 + 15 * 32)], r["ss2"])
+
 
 INPUTS = (
     "adj", "feat", "ograd", "w1", "wd", "w2", "up",
-    "pick", "put", "perm", "cmap", "fsel", "place", "rout", "rin",
+    "pick", "put", "perm", "cmap", "fsel", "place", "rout", "rin", "src",
 )
 
 
@@ -696,23 +757,23 @@
     return pltpu.SemaphoreType.DMA(shape)
 
 
-SENT = 14416
+SENT = 13792
 SCRATCH = [
-    ("early", buf(3072, 128)), ("late", buf(8192, 128)), ("drain", buf(SENT, 128)),
-    ("lsem", sems(3)), ("ss", pltpu.SemaphoreType.DMA), ("rs", sems(33)), ("s_adj", pltpu.SMEM((16, 64), jnp.int32)),
+    ("early", buf(3072, 128)), ("late", buf(8288, 128)), ("drain", buf(SENT, 128)),
+    ("lsem", sems(3)), ("ss", pltpu.SemaphoreType.DMA), ("ss2", pltpu.SemaphoreType.DMA), ("rs", sems(33)), ("s_adj", pltpu.SMEM((16, 64), jnp.int32)),
     ("table", pltpu.SMEM((6, 64), jnp.int32)),
     ("fv", buf(32, 4096)), ("v_pick", buf(1024, 128)), ("v_put", buf(4, 128, 256)), ("v_perm", buf(3, 128, 128)),
     ("v_cmap", buf(4, 128, 128)), ("v_fsel", buf(4, 128, 640)), ("v_place", buf(2, 1280, 128)),
-    ("v_rout", buf(256, 128)), ("v_rin", buf(960, 256)),
+    ("v_rout", buf(256, 128)), ("v_rin", buf(960, 256)), ("v_src", buf(48, 256)),
     ("strip", buf(128, 1280)), ("og", buf(128, 1024)), ("v_w1", buf(9, 4, 2, 16, 128)), ("v_wd", buf(4, 4, 2, 16, 128)),
     ("v_w2", buf(9, 4, 2, 16, 128)), ("v_up", buf(128, 128)),
     ("held0", buf(32, 16, 128)), ("held1", buf(32, 16, 128)), ("slots", buf(2, 8, 16, 640)), ("landed", buf(2, 8, 16, 640)),
     ("pout", buf(4, 32, 256)), ("picked", buf(128, 256)),
     ("cb", buf(3, 1280, 128)), ("z1", buf(1024, 128, kind=F32)), ("act1", buf(1024, 128)),
-    ("z2", buf(256, 128, kind=F32)), ("act2", buf(256, 128)), ("rq", buf(128, 128)), ("x2in", buf(4, 32, 128)),
+    ("z2", buf(256, 128, kind=F32)), ("act2", buf(256, 128)),
     ("slope", buf(1024, 128, kind=F32)), ("direct", buf(1024, 128, kind=F32)),
-    ("halo", buf(2, 32, 128)), ("held2", buf(8, 32, 128)), ("rolled", buf(32, 32, 128)), ("ogt", buf(1024, 128)),
-    ("slots2", buf(8, 32, 256)), ("landed2", buf(8, 32, 256)), ("picked2", buf(128, 256)),
+    ("halo", buf(2, 32, 128)), ("held2", buf(8, 48, 128)), ("picks", buf(32, 64, 384)), ("beyond", buf(32, 128, kind=F32)), ("ogt", buf(1024, 128)),
+    ("slots2", buf(32, 64, 128)), ("landed2", buf(32, 64, 128)),
     ("dq", buf(128, 256)), ("x4in", buf(4, 32, 256)),
     ("hout", buf(2, 32, 128, kind=F32)), ("hin", buf(2, 32, 128, kind=F32)),
     ("held3", buf(8, 32, 256)), ("rolled3", buf(64, 32, 128)), ("ostrip", buf(128, 1024)),
@@ -730,7 +791,7 @@
     return pl.pallas_call(
         level_kernel,
         out_shape=(pltpu.VMEM((32, 4096), BF), pltpu.VMEM((8, 16, AW // 4), BF), pltpu.VMEM((8, 16, BW // 4), BF)),
-        in_specs=[ANY] * 15,
+        in_specs=[ANY] * 16,
         out_specs=[VM] * 3,
         scratch_shapes=[s for _, s in SCRATCH],
         compiler_params=pltpu.CompilerParams(collective_id=0, has_side_effects=True, vmem_limit_bytes=LIMIT),
@@ -777,7 +838,7 @@
     fine_sel, fine_place = fine_rim_maps()
     maps = [
         jnp.asarray(m, BF)
-        for m in (pick, put, fine_perm(), corner_maps(), fine_sel, fine_place, coarse_rim_out(), coarse_rim_in())
+        for m in (pick, put, fine_perm(), corner_maps(), fine_sel, fine_place, coarse_rim_out(), coarse_rim_in(), strip_rims())
     ]
     out, final_a, final_b = level_call(
         adjacency.transpose(1, 2, 0).reshape(16, 64), features, out_grad,

time: 78.1 us -> 76.1 us (0.974)
  Pallas kernels: 77.4 us -> 75.3 us
    pallas_call x1, Pallas kernels: 76.5 us -> 74.5 us  [level_call(): pl.pallas_call(level_kernel, out_shape=(pltpu.VMEM((32, 4096), BF), pltpu...]
where the time goes in v9:
time: 76.1 us; the launch traced here: 76 us
  Pallas kernels  75.3 us (99%)
    pallas_call x1, Pallas kernels, level_call(): pl.pallas_call(level_kernel, out_shape=(pltpu.VMEM((32, 4096), BF), pltpu...  74.5 us

profile of v9, /device:TPU:1, one launch (start us, length us, event | category | flops | bytes accessed | tf_op | source)
XLA Modules:
  0.0 76.0 jit_solution(12757903856444587783)
XLA Ops:
  0.6 74.5 %shard_map.191 = (bf16[32,4096]{1,0:T(8,128)(2,1)S(1)}, bf16[8,16,512]{2,1,0:T(8,128)(2,1)S(1)}, bf16[8,16,384]{2,1,0:T(8,128)(2,1)S(1)}) custom-call(s32[16,64]{1,0:T(8,128)} %bitcast.9, bf16[32,4096]{1,0:T(8,128)(2,1)} %refs_1_.1, bf16[32,4096]{1,0:T(8,128)(2,1)} %refs_2_.1, bf16[9,2,16,128]{3,2,1,0:T(8,128)(2,1)} %bitcast.6, ...), custom_call_target="tpu_custom_call" | custom-call | tf_op jit(solution)/shard_map/pallas_call | solution.py:791
  75.1 0.9 %shard_map.192 = (bf16[32,4096]{1,0:T(8,128)(2,1)}, f32[9,32,128]{2,1,0:T(8,128)}, f32[4,32,128]{2,1,0:T(8,128)}, f32[9,32,128]{2,1,0:T(8,128)}, f32[32,128]{1,0:T(8,128)}) custom-call(bf16[32,4096]{1,0:T(8,128)(2,1)S(1)} %get-tuple-element.8.out_in, bf16[8,16,512]{2,1,0:T(8,128)(2,1)S(1)} %get-tuple-element.9.final_a, ...), custom_call_target="tpu_custom_call" | custom-call | tf_op jit(solution)/shard_map/pallas_call | solution.py:821

commit v10 on v9

--- a/solution.py
+++ b/solution.py
@@ -80,14 +80,6 @@
     return pick, put
 
 
-def coarse_rim_out():
-    out = np.zeros((4, 256, 128), np.float32)
-    for i in range(32):
-        for s, (r, k) in enumerate(((31, i), (i, 0), (0, 31 - i), (31 - i, 31))):
-            out[r // 8, (r % 8) * 32 + k, s * 32 + i] = 1
-    return out
-
-
 def strip_rims():
     out = np.zeros((4, 48, 256), np.float32)
     for q in range(4):
@@ -100,22 +92,15 @@
     return out
 
 
-def coarse_rim_in():
-    out = np.zeros((4, 960, 256), np.float32)
-    for k in range(32):
-        out[0, k, k] = 1
-        out[3, 9 * 32 + k, 64 + 31 - k] = 1
+def side_cells():
+    out = np.zeros((4, 64, 1024), np.float32)
     for q in range(4):
         for r in range(10):
-            row = 8 * q - 1 + r
-            if row < 0:
-                west, east = 255, 128
-            elif row >= 32:
-                west, east = 192, 191
-            else:
-                west, east = 96 + 31 - row, 32 + row
-            out[q, 320 + r * 32, west] = 1
-            out[q, 640 + r * 32 + 31, east] = 1
+            out[q, r, 320 + r * 32] = 1
+            out[q, 16 + r, 640 + r * 32 + 31] = 1
+    for k in range(32):
+        out[0, 32 + k, k] = 1
+        out[3, 32 + k, 288 + k] = 1
     return out
 
 
@@ -153,7 +138,6 @@
     key=lambda d: -(min(d[0], 8 - d[0]) / 2 + min(d[1], 4 - d[1])),
 )
 XYD = [(dx, dy) for dx in FAR for dy in FAR if dx or dy]
-EDGE = (0, 31, 0, 31)
 
 
 def side_by_side(weights, count):
@@ -231,6 +215,7 @@
     for src, dst in early:
         local(r["lsem"].at[0], r[src], r[dst])
     local(r["lsem"].at[1], r["adj"], r["s_adj"])
+    r["landed3"][...] = jnp.zeros((32, 64, 128), BF)
     barrier = pltpu.get_barrier_semaphore()
     peers = [x_peer(d) for d in XD] + [z_peer(d) for d in ZD] + [g_peer(d) for d in GD]
     peers += [gx_peer(dg, dx) for dg, dx in GXD if dg and dx]
@@ -266,7 +251,7 @@
 
     for name in ("cmap", "perm", "fsel", "place"):
         local(r["lsem"].at[2], r[name], r["v_" + name])
-    for name in ("rout", "rin", "src"):
+    for name in ("rin", "src"):
         local(r["lsem"].at[2], r[name].at[q], r["v_" + name])
 
     def piece(n, j):
@@ -320,7 +305,6 @@
                 if h == 0:
                     table[3, at] = jnp.where(owned, m, -1)
                     table[4, at] = s
-                    table[5, at] = n * 8 + (k // 4) * 4 + lax.rem(s + 4 - k % 4, 4)
 
     wait(r["late"], r["lsem"].at[2])
     slots, landed = r["slots"], r["landed"]
@@ -366,13 +350,9 @@
     share_bulk(1)
     share_bulk(2)
 
-    spot = lax.broadcasted_iota(jnp.int32, (64, 128), 0)
-    lane = lax.broadcasted_iota(jnp.int32, (64, 128), 1)
-    in_west, in_side = spot < 16, spot < 32
-    step = jnp.where(in_west, spot, spot - 16)
-    for dg, dx in GXD + [(0, 0)]:
-        at, xd = gs[dg] * 8, xs[dx]
-        row = step + (8 * xd - 1)
+    def sources(spot, at, xd):
+        in_west, in_side = spot < 16, spot < 32
+        row = jnp.where(in_west, spot, spot - 16) + (8 * xd - 1)
         above, below = jnp.logical_and(in_side, row < 0), jnp.logical_and(in_side, row > 31)
 
         def by_spot(kind):
@@ -391,7 +371,12 @@
         here = jnp.where(odd, jnp.logical_and(cell >= 8 * q, cell < 8 * q + 8).astype(jnp.int32),
                          jnp.where(turn == 0, jnp.where(q == 3, 1, 0), jnp.where(q == 0, 1, 0)))
         source = jnp.where(odd, cell - 8 * q + jnp.where(turn == 3, 8, 0), cell + 16)
-        source = jnp.where(jnp.logical_and(of >= 0, here == 1), of * 48 + source, -1)
+        return jnp.where(jnp.logical_and(of >= 0, here == 1), of * 48 + source, -1)
+
+    spot = lax.broadcasted_iota(jnp.int32, (64, 128), 0)
+    lane = lax.broadcasted_iota(jnp.int32, (64, 128), 1)
+    for dg, dx in GXD + [(0, 0)]:
+        source = sources(spot, gs[dg] * 8, xs[dx])
         for c in range(3):
             r["picks"][dg * 4 + dx, :, c * 128:(c + 1) * 128] = jnp.where(source == lane + 128 * c, 1.0, 0.0).astype(BF)
 
@@ -493,8 +478,16 @@
     r["slope"][...] = slope
     r["direct"][...] = slope * ogt[...].astype(F32)
 
+    lane = lax.broadcasted_iota(jnp.int32, (8, 128), 1)
+    depth = lax.broadcasted_iota(jnp.int32, (384, 128), 0)
+    for n in range(16):
+        dg, dx = n // 2, 2 * (n % 2)
+        left = lane < 64
+        source = sources(jnp.where(left, lane, lane - 64), gs[dg] * 8, jnp.where(left, xs[dx], xs[dx + 1]))
+        source = jnp.broadcast_to(source[0:1], (384, 128))
+        r["adds"][:, n * 128:(n + 1) * 128] = jnp.where(source == depth, 1.0, 0.0).astype(BF)
+
     settle(c_z)
-    lane = lax.broadcasted_iota(jnp.int32, (32, 128), 1)
     slots2, landed2, picks = r["slots2"], r["landed2"], r["picks"]
     every = jnp.concatenate([held2[n] for n in range(8)], axis=0)
     c_g = begin(landed2)
@@ -541,7 +534,6 @@
     take_bulk(4)
     settle(c_h)
 
-    sel = r["v_rin"][...]
     upper = jnp.where(q == 0, beyond[...], halo[0].astype(F32))
     lower = jnp.where(q == 3, beyond[...], halo[1].astype(F32))
     rows = jnp.concatenate([upper, act2.astype(F32), lower], axis=0)
@@ -571,13 +563,24 @@
         + jnp.where(col == 31, 0.0, pltpu.roll(back[0], 319, 0))
         + jnp.where(col == 0, 0.0, pltpu.roll(back[2], 1, 0))
     )
-    cat = jnp.concatenate([mid.astype(BF), back[0].astype(BF), back[2].astype(BF)], axis=0)
-    dq = r["dq"]
-    dq[...] = tn(cat, sel).astype(BF)
-    x4in, hout, hin = r["x4in"], r["hout"], r["hin"]
-    c_x = spread(
-        x4in.at[pl.ds(1, 3)], XD, x_peer, lambda d: dq.at[rows_of(xs[d]), :], lambda d: x4in.at[d]
-    )
+    cat = jnp.concatenate([mid, back[0], back[2], none64], axis=0).astype(BF)
+    landed3 = r["landed3"]
+    landed3[0] = nn(r["v_rin"][...], cat).astype(BF)
+    hout, hin = r["hout"], r["hin"]
+    c_g = begin(landed3)
+    for size, ok in ((64, at_end(x)), (32, jnp.logical_not(at_end(x)))):
+
+        @pl.when(ok)
+        def _():
+            some = pl.ds(0, size)
+            for dg, dx in GXD:
+                back_at = ((8 - dg) % 8) * 4 + (4 - dx) % 4
+                pltpu.make_async_remote_copy(
+                    src_ref=landed3.at[0, some], dst_ref=landed3.at[back_at, some],
+                    send_sem=r["ss3"], recv_sem=r["rs"].at[c_g],
+                    device_id=gx_peer(dg, dx), device_id_type=MESH,
+                ).start()
+
     hout[0] = mid[288:320]
     hout[1] = mid[0:32]
     c_h = begin(hin)
@@ -641,13 +644,6 @@
         summed = act1[n * 128:(n + 1) * 128, :].astype(F32) + jnp.concatenate([row] * 4, axis=0)
         ostrip[:, n * 128:(n + 1) * 128] = tn(summed.astype(BF), flat).astype(BF)
 
-    settle(c_x)
-    total = dq[mine, :].astype(F32)
-    for d in XD:
-        total = total + x4in[d].astype(F32)
-    held3 = r["held3"]
-    held3[g] = total.astype(BF)
-    c_g = spread(held3.at[pl.ds(0, 7)], GD, g_peer, lambda d: held3.at[g], lambda d: held3.at[g])
     lanes = pl.ds(pl.multiple_of(x * 1024, 1024), 1024)
     c_o = spread(
         out, XD, x_peer,
@@ -659,52 +655,36 @@
     r["gb_w"][...] = tn(gz3, taps2)
     parts_b = (r["gb_w"], r["gb_u"])
     c_bc = halves("b", BW, parts_b)
-    settle(c_g)
-    rolled3 = r["rolled3"]
-    for j in range(8):
-        for h in range(2):
-            block = held3[j, :, 128 * h:128 * h + 128]
-            rolled3[j * 8 + h * 4] = block
-            for m in range(1, 4):
-                rolled3[j * 8 + h * 4 + m] = pltpu.roll(block.astype(F32), 32 * m, 1).astype(BF)
-    sums = [jnp.zeros((32, 128), F32) for _ in range(8)]
-    for j in range(8):
-        for k in range(8):
-            at = j * 8 + k
-            n, s = table[3, at], table[4, at]
-            block = rolled3[table[5, at]].astype(F32)
-            if k < 4:
-                block = jnp.where(lane // 32 == s, block, 0.0)
-            else:
-                block = jnp.where(lane == 32 * s + EDGE[k - 4], block, 0.0)
-            for m in range(8):
-                sums[m] = sums[m] + jnp.where(n == m, block, 0.0)
-    slots3, landed3 = r["slots3"], r["landed3"]
+    some_rows, more_rows = pl.ds(0, 15 * 64 + 16 * 32), pl.ds(0, 16 * 64 + 15 * 32)
+
+    @pl.when(at_end(x))
+    def _():
+        wait(r["drain"].at[some_rows], r["rs"].at[c_g])
+
+    @pl.when(jnp.logical_not(at_end(x)))
+    def _():
+        wait(r["drain"].at[more_rows], r["rs"].at[c_g])
+
+    total = nn(r["adds"][...], landed3[...].reshape(2048, 128))
+    slots3, landed4 = r["slots3"], r["landed4"]
     for n in range(8):
-        slots3[n] = sums[n].astype(BF)
+        slots3[n] = total[n * 48:(n + 1) * 48].astype(BF)
     c_z = spread(
-        landed3.at[pl.ds(1, 7)], ZD, z_peer, lambda d: slots3.at[zs[d]], lambda d: landed3.at[d]
+        landed4.at[pl.ds(1, 7)], ZD, z_peer, lambda d: slots3.at[zs[d]], lambda d: landed4.at[d]
     )
     settle(c_bc)
     c_b = shares("b", BW, parts_b)
     slope2 = gelu_slope(r["z2"][...])
-    settle(c_z)
-    total = slots3[z].astype(F32)
-    for d in ZD:
-        total = total + landed3[d].astype(F32)
-    back_rim = r["back_rim"]
-    back_rim[mine, :] = total.astype(BF)
-    part3 = back_rim.at[mine, :]
-    c_x = spread(back_rim.at[pl.ds(0, 96), :], XD, x_peer, lambda d: part3, lambda d: part3)
-    settle(c_b)
-    c_bz = along_z("b")
     settle(c_h)
     upper = jnp.where(q == 0, 0.0, hin[0])
     lower = jnp.where(q == 3, 0.0, hin[1])
     ga2 = mid[32:288] + jnp.concatenate([upper, jnp.zeros((192, 128), F32), lower], axis=0)
-    settle(c_x)
-
-    gz2 = (slope2 * (ga2 + nt(r["v_rout"][...], back_rim[...]))).astype(BF)
+    settle(c_z)
+    total = slots3[z].astype(F32)
+    for d in ZD:
+        total = total + landed4[d].astype(F32)
+
+    gz2 = (slope2 * (ga2 + tn(r["v_src"][...], total.astype(BF)))).astype(BF)
     wd = r["v_wd"][...].reshape(4, 128, 128)
     fine = [nn(gz2, wd[t]).reshape(8, 1, 32, 128) for t in range(4)]
     grown = jnp.concatenate(fine, axis=1).reshape(1024, 128)
@@ -715,6 +695,8 @@
     r["ga_d"][...] = tn(gz2, quarters(act1[...]))
     parts_a = (r["ga_w"], r["ga_d"])
     c_ac = halves("a", AW, parts_a)
+    settle(c_b)
+    c_bz = along_z("b")
 
     def to_row(name, n):
         settle(n)
@@ -736,16 +718,18 @@
 
     @pl.when(at_end(x))
     def _():
-        wait(r["drain"].at[pl.ds(0, 15 * 64 + 16 * 32)], r["ss2"])
+        wait(r["drain"].at[some_rows], r["ss2"])
+        wait(r["drain"].at[pl.ds(0, 31 * 64)], r["ss3"])
 
     @pl.when(jnp.logical_not(at_end(x)))
     def _():
-        wait(r["drain"].at[pl.ds(0, 16 * 64 + 15 * 32)], r["ss2"])
+        wait(r["drain"].at[more_rows], r["ss2"])
+        wait(r["drain"].at[pl.ds(0, 31 * 32)], r["ss3"])
 
 
 INPUTS = (
     "adj", "feat", "ograd", "w1", "wd", "w2", "up",
-    "pick", "put", "perm", "cmap", "fsel", "place", "rout", "rin", "src",
+    "pick", "put", "perm", "cmap", "fsel", "place", "rin", "src",
 )
 
 
@@ -757,14 +741,14 @@
     return pltpu.SemaphoreType.DMA(shape)
 
 
-SENT = 13792
+SENT = 13168
 SCRATCH = [
-    ("early", buf(3072, 128)), ("late", buf(8288, 128)), ("drain", buf(SENT, 128)),
-    ("lsem", sems(3)), ("ss", pltpu.SemaphoreType.DMA), ("ss2", pltpu.SemaphoreType.DMA), ("rs", sems(33)), ("s_adj", pltpu.SMEM((16, 64), jnp.int32)),
+    ("early", buf(3072, 128)), ("late", buf(6624, 128)), ("drain", buf(SENT, 128)),
+    ("lsem", sems(3)), ("ss", pltpu.SemaphoreType.DMA), ("ss2", pltpu.SemaphoreType.DMA), ("ss3", pltpu.SemaphoreType.DMA), ("rs", sems(33)), ("s_adj", pltpu.SMEM((16, 64), jnp.int32)),
     ("table", pltpu.SMEM((6, 64), jnp.int32)),
     ("fv", buf(32, 4096)), ("v_pick", buf(1024, 128)), ("v_put", buf(4, 128, 256)), ("v_perm", buf(3, 128, 128)),
     ("v_cmap", buf(4, 128, 128)), ("v_fsel", buf(4, 128, 640)), ("v_place", buf(2, 1280, 128)),
-    ("v_rout", buf(256, 128)), ("v_rin", buf(960, 256)), ("v_src", buf(48, 256)),
+    ("v_rin", buf(64, 1024)), ("v_src", buf(48, 256)),
     ("strip", buf(128, 1280)), ("og", buf(128, 1024)), ("v_w1", buf(9, 4, 2, 16, 128)), ("v_wd", buf(4, 4, 2, 16, 128)),
     ("v_w2", buf(9, 4, 2, 16, 128)), ("v_up", buf(128, 128)),
     ("held0", buf(32, 16, 128)), ("held1", buf(32, 16, 128)), ("slots", buf(2, 8, 16, 640)), ("landed", buf(2, 8, 16, 640)),
@@ -774,10 +758,8 @@
     ("slope", buf(1024, 128, kind=F32)), ("direct", buf(1024, 128, kind=F32)),
     ("halo", buf(2, 32, 128)), ("held2", buf(8, 48, 128)), ("picks", buf(32, 64, 384)), ("beyond", buf(32, 128, kind=F32)), ("ogt", buf(1024, 128)),
     ("slots2", buf(32, 64, 128)), ("landed2", buf(32, 64, 128)),
-    ("dq", buf(128, 256)), ("x4in", buf(4, 32, 256)),
-    ("hout", buf(2, 32, 128, kind=F32)), ("hin", buf(2, 32, 128, kind=F32)),
-    ("held3", buf(8, 32, 256)), ("rolled3", buf(64, 32, 128)), ("ostrip", buf(128, 1024)),
-    ("slots3", buf(8, 32, 128)), ("landed3", buf(8, 32, 128)), ("back_rim", buf(128, 128)),
+    ("adds", buf(384, 2048)), ("landed3", buf(32, 64, 128)), ("slots3", buf(8, 48, 128)), ("landed4", buf(8, 48, 128)),
+    ("hout", buf(2, 32, 128, kind=F32)), ("hin", buf(2, 32, 128, kind=F32)), ("ostrip", buf(128, 1024)),
     ("gb_u", buf(128, 128, kind=F32)), ("gb_w", buf(128, 1152, kind=F32)),
     ("ga_d", buf(128, 512, kind=F32)), ("ga_w", buf(128, 1152, kind=F32)),
     ("bc", buf(4, 16, BW)), ("bci", buf(4, 16, BW)), ("bo", buf(4, 4, 16, BW // 4)), ("bi", buf(16, 16, BW // 4)),
@@ -791,7 +773,7 @@
     return pl.pallas_call(
         level_kernel,
         out_shape=(pltpu.VMEM((32, 4096), BF), pltpu.VMEM((8, 16, AW // 4), BF), pltpu.VMEM((8, 16, BW // 4), BF)),
-        in_specs=[ANY] * 16,
+        in_specs=[ANY] * 15,
         out_specs=[VM] * 3,
         scratch_shapes=[s for _, s in SCRATCH],
         compiler_params=pltpu.CompilerParams(collective_id=0, has_side_effects=True, vmem_limit_bytes=LIMIT),
@@ -838,7 +820,7 @@
     fine_sel, fine_place = fine_rim_maps()
     maps = [
         jnp.asarray(m, BF)
-        for m in (pick, put, fine_perm(), corner_maps(), fine_sel, fine_place, coarse_rim_out(), coarse_rim_in(), strip_rims())
+        for m in (pick, put, fine_perm(), corner_maps(), fine_sel, fine_place, side_cells(), strip_rims())
     ]
     out, final_a, final_b = level_call(
         adjacency.transpose(1, 2, 0).reshape(16, 64), features, out_grad,

time: 76.1 us -> 73.3 us (0.963)
  Pallas kernels: 75.3 us -> 72.5 us
    pallas_call x1, Pallas kernels: 74.5 us -> 71.7 us  [level_call(): pl.pallas_call(level_kernel, out_shape=(pltpu.VMEM((32, 4096), BF), pltpu...]
where the time goes in v10:
time: 73.3 us; the launch traced here: 73.2 us
  Pallas kernels  72.5 us (99%)
    pallas_call x1, Pallas kernels, level_call(): pl.pallas_call(level_kernel, out_shape=(pltpu.VMEM((32, 4096), BF), pltpu...  71.7 us

profile of v10, /device:TPU:1, one launch (start us, length us, event | category | flops | bytes accessed | tf_op | source)
XLA Modules:
  0.0 73.2 jit_solution(17084285470799048017)
XLA Ops:
  0.6 71.7 %shard_map.182 = (bf16[32,4096]{1,0:T(8,128)(2,1)S(1)}, bf16[8,16,512]{2,1,0:T(8,128)(2,1)S(1)}, bf16[8,16,384]{2,1,0:T(8,128)(2,1)S(1)}) custom-call(s32[16,64]{1,0:T(8,128)} %bitcast.9, bf16[32,4096]{1,0:T(8,128)(2,1)} %refs_1_.1, bf16[32,4096]{1,0:T(8,128)(2,1)} %refs_2_.1, bf16[9,2,16,128]{3,2,1,0:T(8,128)(2,1)} %bitcast.6, ...), custom_call_target="tpu_custom_call" | custom-call | tf_op jit(solution)/shard_map/pallas_call | solution.py:773
  72.3 0.9 %shard_map.183 = (bf16[32,4096]{1,0:T(8,128)(2,1)}, f32[9,32,128]{2,1,0:T(8,128)}, f32[4,32,128]{2,1,0:T(8,128)}, f32[9,32,128]{2,1,0:T(8,128)}, f32[32,128]{1,0:T(8,128)}) custom-call(bf16[32,4096]{1,0:T(8,128)(2,1)S(1)} %get-tuple-element.8.out_in, bf16[8,16,512]{2,1,0:T(8,128)(2,1)S(1)} %get-tuple-element.9.final_a, ...), custom_call_target="tpu_custom_call" | custom-call | tf_op jit(solution)/shard_map/pallas_call | solution.py:803

commit v11 on v10

--- a/solution.py
+++ b/solution.py
@@ -495,20 +495,21 @@
     def at_end(n):
         return jnp.logical_or(n == 0, n == 3)
 
-    for dg, dx in GXD + [(0, 0)]:
-        d = dg * 4 + dx
-        slots2[d] = nn(picks[d], every).astype(BF)
-        if d:
-            for size, ok in ((64, at_end(xs[dx])), (32, jnp.logical_not(at_end(xs[dx])))):
-
-                @pl.when(ok)
-                def _():
-                    some = pl.ds(0, size)
-                    pltpu.make_async_remote_copy(
-                        src_ref=slots2.at[d, some], dst_ref=landed2.at[d, some],
-                        send_sem=r["ss2"], recv_sem=r["rs"].at[c_g],
-                        device_id=gx_peer(dg, dx), device_id_type=MESH,
-                    ).start()
+    for dx in FAR:
+        for dg in GD + (0,):
+            slots2[dg * 4 + dx] = nn(picks[dg * 4 + dx], every).astype(BF)
+        for size, ok in ((64, at_end(xs[dx])), (32, jnp.logical_not(at_end(xs[dx])))):
+
+            @pl.when(ok)
+            def _():
+                some = pl.ds(0, size)
+                for dg in GD + (0,):
+                    if dg or dx:
+                        pltpu.make_async_remote_copy(
+                            src_ref=slots2.at[dg * 4 + dx, some], dst_ref=landed2.at[dg * 4 + dx, some],
+                            send_sem=r["ss2"], recv_sem=r["rs"].at[c_g],
+                            device_id=gx_peer(dg, dx), device_id_type=MESH,
+                        ).start()
 
     @pl.when(at_end(x))
     def _():

time: 73.3 us -> 72.8 us (level)
  no operation moved by 1% of the time
where the time goes in v11:
time: 72.8 us; the launch traced here: 72.7 us
  Pallas kernels  72.1 us (99%)
    pallas_call x1, Pallas kernels, level_call(): pl.pallas_call(level_kernel, out_shape=(pltpu.VMEM((32, 4096), BF), pltpu...  71.2 us

profile of v11, /device:TPU:1, one launch (start us, length us, event | category | flops | bytes accessed | tf_op | source)
XLA Modules:
  0.0 72.7 jit_solution(10848034462317387324)
XLA Ops:
  0.6 71.2 %shard_map.182 = (bf16[32,4096]{1,0:T(8,128)(2,1)S(1)}, bf16[8,16,512]{2,1,0:T(8,128)(2,1)S(1)}, bf16[8,16,384]{2,1,0:T(8,128)(2,1)S(1)}) custom-call(s32[16,64]{1,0:T(8,128)} %bitcast.9, bf16[32,4096]{1,0:T(8,128)(2,1)} %refs_1_.1, bf16[32,4096]{1,0:T(8,128)(2,1)} %refs_2_.1, bf16[9,2,16,128]{3,2,1,0:T(8,128)(2,1)} %bitcast.6, ...), custom_call_target="tpu_custom_call" | custom-call | tf_op jit(solution)/shard_map/pallas_call | solution.py:774
  71.9 0.9 %shard_map.183 = (bf16[32,4096]{1,0:T(8,128)(2,1)}, f32[9,32,128]{2,1,0:T(8,128)}, f32[4,32,128]{2,1,0:T(8,128)}, f32[9,32,128]{2,1,0:T(8,128)}, f32[32,128]{1,0:T(8,128)}) custom-call(bf16[32,4096]{1,0:T(8,128)(2,1)S(1)} %get-tuple-element.8.out_in, bf16[8,16,512]{2,1,0:T(8,128)(2,1)S(1)} %get-tuple-element.9.final_a, ...), custom_call_target="tpu_custom_call" | custom-call | tf_op jit(solution)/shard_map/pallas_call | solution.py:804
